TPU v7x, 256 devices: a whole 4x4x8 slice. The times are simulated.
256 devices in a mesh: row: 4 (over z_hi), col: 64 (over x, y, z_lo, core).
Axes of the slice: x: 4, y: 4, z: 8 (z_hi: 4, z_lo: 2; z = z_hi * 2 + z_lo), core: 2. Of those that a mesh axis runs over, the one named last changes fastest.
Arguments:
- object_field: float32 [2, 2048, 32768], P(None, 'row', 'col'), may hold values from -6 to 6
- probe_modes: float32 [2, 2, 128, 128], replicated, may hold values from -5 to 5
- photons: bfloat16 [4, 64, 64, 128, 128], P('row', 'col'), may hold values from 0.099609375 to 10
- positions: int32 [4, 64, 64, 2], P('row', 'col'), may hold values from 0 to 511, as said below
- counts: int32 [4, 64], P('row', 'col'), may hold values from 8 to 64, as said below
Outputs:
- object_gradient: float32 [2, 2048, 32768], P(None, 'row', 'col')
- probe_gradient: float32 [2, 2, 128, 128], replicated
Inputs may be any that keep to these rules, and one draw needn't show every extreme that they name: `positions`: each tile's offsets lie inside that tile; slots at or beyond the tile's count hold offsets that are ignored. `counts`: some tile has all 64 slots valid and some has 8; most tiles have few.
All inputs are finite; a program needn't handle non-finite values.
Results may differ from a plain program's by a relative error of at most 0.0012.
The roundings to bfloat16 on the way count: a program that leaves them out, or rounds other values in their place, can miss the bound.
Values sent between devices are 32-bit elements; how exact they have to be, the bound alone decides.
No kernel may reach another device: no remote copies, remote signals or barrier semaphores. Data moves between devices by JAX's collectives and lax.ppermute only.
A program may use at most 64 MiB of HBM per device.

v0:
```python
import math

import jax
import jax.numpy as jnp
from jax import lax
from jax.sharding import PartitionSpec as P


def shifted(value, axis, by):
    size = lax.axis_size(axis)
    pairs = [(i, i + by) for i in range(size) if 0 <= i + by < size]
    return lax.ppermute(value, axis, pairs)


def fourier_tables(patch_len):
    index_range = jnp.arange(patch_len, dtype=jnp.int32)
    product = index_range[:, None] * index_range[None, :] % patch_len
    angle = product.astype(jnp.float32) * (2.0 * math.pi / patch_len)
    cosine = jnp.cos(angle) / math.sqrt(patch_len)
    sine_part = jnp.sin(angle) / math.sqrt(patch_len)
    plus_table = jnp.concatenate(
        [jnp.concatenate([cosine, sine_part], 1), jnp.concatenate([-sine_part, cosine], 1)], 0
    )
    minus_table = jnp.concatenate(
        [jnp.concatenate([cosine, -sine_part], 1), jnp.concatenate([sine_part, cosine], 1)], 0
    )
    return (plus_table.astype(jnp.bfloat16), minus_table.astype(jnp.bfloat16))


def wave_gradient(patches, photon_block, valid, probe_modes, plus_table, minus_table):
    batch, _, patch_len, _ = patches.shape
    modes = probe_modes.shape[1]
    object_real = patches[:, 0][:, None]
    object_imaginary = patches[:, 1][:, None]
    probe_real = probe_modes[0][None]
    probe_imaginary = probe_modes[1][None]
    wave_real = probe_real * object_real - probe_imaginary * object_imaginary
    wave_imaginary = probe_real * object_imaginary + probe_imaginary * object_real
    stacked = jnp.concatenate([wave_real, wave_imaginary], axis=2).astype(jnp.bfloat16)
    first_pass = jnp.einsum(
        "ik,bmkj->bmij", plus_table, stacked, preferred_element_type=jnp.float32
    ).astype(jnp.bfloat16)
    turned = (
        first_pass.reshape(batch, modes, 2, patch_len, patch_len)
        .transpose(0, 1, 3, 2, 4)
        .reshape(batch, modes, patch_len, 2 * patch_len)
    )
    far_field = jnp.einsum("bmik,kj->bmij", turned, minus_table, preferred_element_type=jnp.float32)
    power = jnp.sum(far_field * far_field, axis=1)
    intensity = power[..., :patch_len] + power[..., patch_len:]
    factor = (1.0 - photon_block.astype(jnp.float32) / (intensity + 1.0)) * valid[:, None, None]
    scaled = (far_field * jnp.concatenate([factor, factor], -1)[:, None]).astype(jnp.bfloat16)
    back_pass = jnp.einsum(
        "bmik,kj->bmij", scaled, plus_table, preferred_element_type=jnp.float32
    ).astype(jnp.bfloat16)
    unturned = (
        back_pass.reshape(batch, modes, patch_len, 2, patch_len)
        .transpose(0, 1, 3, 2, 4)
        .reshape(batch, modes, 2 * patch_len, patch_len)
    )
    exit_grad = jnp.einsum(
        "ik,bmkj->bmij", minus_table, unturned, preferred_element_type=jnp.float32
    )
    exit_real = exit_grad[:, :, :patch_len]
    exit_imaginary = exit_grad[:, :, patch_len:]
    patch_real = jnp.sum(probe_real * exit_real + probe_imaginary * exit_imaginary, axis=1)
    patch_imaginary = jnp.sum(probe_real * exit_imaginary - probe_imaginary * exit_real, axis=1)
    patch_gradient = jnp.stack([patch_real, patch_imaginary], axis=1)
    mode_real = jnp.sum(object_real * exit_real + object_imaginary * exit_imaginary, axis=0)
    mode_imaginary = jnp.sum(object_real * exit_imaginary - object_imaginary * exit_real, axis=0)
    return (patch_gradient, jnp.stack([mode_real, mode_imaginary], axis=0))


def take_patches(field, row_start, col_start, patch_len):
    zero_index = jnp.zeros((), jnp.int32)
    return jax.vmap(
        lambda r, c: lax.dynamic_slice(field, (zero_index, r, c), (2, patch_len, patch_len))
    )(row_start, col_start)


def add_patches(gradient, patch_gradient, row_start, col_start):
    patch_len = patch_gradient.shape[-1]
    zero_index = jnp.zeros((), jnp.int32)
    for k in range(patch_gradient.shape[0]):
        corner_at = (zero_index, row_start[k], col_start[k])
        present = lax.dynamic_slice(gradient, corner_at, (2, patch_len, patch_len))
        gradient = lax.dynamic_update_slice(gradient, present + patch_gradient[k], corner_at)
    return gradient


def own_slots(
    gradient,
    probe_sum,
    field,
    photon_rows,
    row_start,
    col_start,
    low_slot,
    high_slot,
    probe_modes,
    plus_table,
    minus_table,
):
    patch_len = probe_modes.shape[-1]

    def block_step(k, carry):
        grad_now, probe_now = carry
        start = (k * 8).astype(jnp.int32)
        row_block = lax.dynamic_slice_in_dim(row_start, start, 8)
        col_block = lax.dynamic_slice_in_dim(col_start, start, 8)
        slot_ids = start + jnp.arange(8, dtype=jnp.int32)
        valid = ((slot_ids >= low_slot) & (slot_ids < high_slot)).astype(jnp.float32)
        patches = take_patches(field, row_block, col_block, patch_len)
        photon_block = lax.dynamic_slice_in_dim(photon_rows, start, 8)
        patch_gradient, probe_part = wave_gradient(
            patches, photon_block, valid, probe_modes, plus_table, minus_table
        )
        return (add_patches(grad_now, patch_gradient, row_block, col_block), probe_now + probe_part)

    return lax.fori_loop(low_slot // 8, (high_slot + 7) // 8, block_step, (gradient, probe_sum))


def body(object_field, probe_modes, photons, positions, counts):
    patch_len = probe_modes.shape[-1]
    tile_rows = object_field.shape[1]
    tile_cols = object_field.shape[2]
    slot_count = photons.shape[2]
    plus_table, minus_table = fourier_tables(patch_len)
    row_start = positions[0, 0, :, 0]
    col_start = positions[0, 0, :, 1]
    count_here = counts[0, 0]
    photon_rows = photons[0, 0]
    col_devices = lax.axis_size("col")
    right_rim = shifted(object_field[:, :, :patch_len], "col", -1)
    widened = jnp.concatenate([object_field, right_rim], axis=2)
    below_rim = shifted(widened[:, :patch_len, :], "row", -1)
    extended = jnp.concatenate([widened, below_rim], axis=1)
    gradient = jnp.zeros(extended.shape, jnp.float32)
    probe_sum = jnp.zeros(probe_modes.shape, jnp.float32)
    zero_slot = jnp.zeros((), jnp.int32)
    gradient, probe_sum = own_slots(
        gradient,
        probe_sum,
        extended,
        photon_rows,
        row_start,
        col_start,
        zero_slot,
        count_here,
        probe_modes,
        plus_table,
        minus_table,
    )
    from_above = shifted(gradient[:, tile_rows:, :], "row", 1)
    interior = gradient[:, :tile_rows, :].at[:, :patch_len, :].add(from_above)
    from_left = shifted(interior[:, :, tile_cols:], "col", 1)
    object_gradient = interior[:, :, :tile_cols].at[:, :, :patch_len].add(from_left)
    total_probe = lax.psum(probe_sum, ("row", "col"))
    probe_gradient = total_probe / math.sqrt(lax.axis_size("row") * col_devices * slot_count)
    return (object_gradient, probe_gradient)


def solution(mesh):
    in_specs = (
        P(None, "row", "col"),
        P(),
        P("row", "col", None, None, None),
        P("row", "col", None, None),
        P("row", "col"),
    )
    out_specs = (P(None, "row", "col"), P())
    return jax.shard_map(body, mesh=mesh, in_specs=in_specs, out_specs=out_specs, check_vma=False)
```

profile of v0, /device:TPU:1, one launch (start us, length us, event | category | flops | bytes accessed | tf_op | source)
XLA Modules:
  0.0 1189.9 jit_solution(17489078435481141299)
XLA Ops:
  8.3 5.3 collective-permute-start
  15.4 4.9 collective-permute-done
  24.5 26.0 %collective-permute-done.1 = f32[2,128,640]{2,1,0:T(8,128)} collective-permute-done((f32[2,128,640]{2,1,0:T(8,128)}, f32[2,128,640]{2,1,0:T(8,128)}, u32[]{:S(2)}, u32[]{:S(2)}) %collective-permute-start.1) | collective-permute-done | bytes 655392 | tf_op jit(solution)/shard_map/ppermute | solution.py:12
  50.5 3.0 pad_maximum_fusion.2
  56.1 210.6 %while.17 = (s32[]{:T(128)}, f32[2,640,640]{1,2,0:T(8,128)}, f32[2,2,128,128]{2,3,1,0:T(8,128)}, s32[]{:T(128)}, s32[64]{0:T(128)S(1)}, /*index=5*/s32[64]{0:T(1...) while((s32[]{:T(128)}, f32[2,640,640]{1,2,0:T(8,128)}, ...), condition=%wide.region_6.7_spmd, body=%wide.region_0.6_spmd.sunk | while | flops 1086390528 | bytes 58197628 | solution.py:120
  56.3 23.0 %while.18 = (s32[]{:T(128)}, f32[2,640,640]{2,1,0:T(8,128)}, s32[8,3]{0,1:T(4,128)S(1)}, f32[8,2,128,128]{3,2,1,0:T(8,128)S(1)}, s32[]{:T(128)}) while((s32[]{:T(128)}, f32[2,640,640]{2,1,0:T(8,128)}, s32[8,3]{0,1:T(4,128)S(1)}, f32[8,2,128,128]{3,2,1,0:T(8,128)S(1)}, s32[]{:T(128)}) %tuple.95), condition=%wide.while_cond.2, body=%wide.while_body.2.sunk | while | flops 2 | bytes 262261 | solution.py:77
  56.9 2.3 bitcast_dynamic-update-slice_fusion.2
  59.7 2.3 bitcast_dynamic-update-slice_fusion.2
  62.6 2.3 bitcast_dynamic-update-slice_fusion.2
  77.0 2.3 bitcast_dynamic-update-slice_fusion.2
  96.7 3.7 dynamic_update_slice.32
  105.3 3.7 dynamic_update_slice.33
  114.0 3.5 dynamic_update_slice.34
  122.4 3.5 dynamic_update_slice.35
  130.5 3.7 dynamic_update_slice.36
  139.0 3.7 dynamic_update_slice.37
  147.4 3.7 dynamic_update_slice.38
  156.1 3.7 dynamic_update_slice.39
  161.6 23.0 %while.18 = (s32[]{:T(128)}, f32[2,640,640]{2,1,0:T(8,128)}, s32[8,3]{0,1:T(4,128)S(1)}, f32[8,2,128,128]{3,2,1,0:T(8,128)S(1)}, s32[]{:T(128)}) while((s32[]{:T(128)}, f32[2,640,640]{2,1,0:T(8,128)}, s32[8,3]{0,1:T(4,128)S(1)}, f32[8,2,128,128]{3,2,1,0:T(8,128)S(1)}, s32[]{:T(128)}) %tuple.95), condition=%wide.while_cond.2, body=%wide.while_body.2.sunk | while | flops 2 | bytes 262261 | solution.py:77
  162.2 2.3 bitcast_dynamic-update-slice_fusion.2
  202.1 3.7 dynamic_update_slice.32
  210.7 3.4 dynamic_update_slice.33
  219.1 3.7 dynamic_update_slice.34
  227.6 3.7 dynamic_update_slice.35
  235.9 3.7 dynamic_update_slice.36
  244.6 3.5 dynamic_update_slice.37
  252.7 3.7 dynamic_update_slice.38
  261.3 3.7 dynamic_update_slice.39
  266.7 3.4 copy.24
  273.1 11.7 collective-permute-done.2
  286.9 99.8 %collective-permute-start.3 = (f32[2,512,128]{2,1,0:T(8,128)S(1)}, f32[2,512,128]{2,1,0:T(8,128)S(1)}, u32[]{:S(2)}, u32[]{:S(2)}) collective-permute-start(f32[2,512,128]{2,1,0:T(8,128)S(1)} %slice.219), channel_id=1, source_target_pairs={{0,1},{1,2},{2,3},{3,4},{4,5},{5,6},{6,7},{7,8},{8,9},{9,10},{10,1... | collective-permute-start | bytes 1572872 | tf_op jit(solution)/shard_map/ppermute | solution.py:12
  388.6 788.6 %all-reduce.2.cloned.1.call-done = f32[2,2,128,128]{3,2,1,0:T(8,128)} async-done(((f32[2,2,128,128]{3,2,1,0:T(8,128)}), f32[2,2,128,128]{3,2,1,0:T(8,128)}) %all-reduce.2.cloned.1.call-update) | async-done | bytes 262160 | tf_op jit(solution)/shard_map/psum | solution.py:158
  (153 shorter events, 102.1 us)
Async XLA Ops:
  7.2 1170.0 %all-reduce.2.cloned.1.call-start = ((), (), s32[]{:S(2)}) async-start(), calls=%async_computation | async-start | bytes 524288 | tf_op jit(solution)/shard_map/psum | solution.py:158
  8.3 14.8 %copy-start.4 = (f32[2,2,128,128]{3,2,1,0:T(8,128)S(1)}, f32[2,2,128,128]{3,2,1,0:T(8,128)}, u32[]{:S(2)}) copy-start(f32[2,2,128,128]{3,2,1,0:T(8,128)} %param.12) | copy-start | bytes 786436
  8.3 11.9 %collective-permute-start = (f32[2,512,128]{2,1,0:T(8,128)S(1)}, f32[2,512,128]{2,1,0:T(8,128)S(1)}, u32[]{:S(2)}, u32[]{:S(2)}) collective-permute-start(f32[2,512,128]{2,1,0:T(8,128)S(1)} %slice.172), channel_id=1, source_target_pairs={{1,0},{2,1},{3,2},{4,3},{5,4},{6,5},{7,6},{8,7},{9,8},{10,9},{11,1... | collective-permute-start | bytes 1572872 | tf_op jit(solution)/shard_map/ppermute | solution.py:12
  15.4 9.1 copy-start.5
  21.1 29.3 %collective-permute-start.1 = (f32[2,128,640]{2,1,0:T(8,128)}, f32[2,128,640]{2,1,0:T(8,128)}, u32[]{:S(2)}, u32[]{:S(2)}) collective-permute-start(f32[2,128,640]{2,1,0:T(8,128)} %slice.213), channel_id=1, source_target_pairs={{64,0},{128,64},{192,128},{65,1},{129,65},{193,129},{66,2},{130,66... | collective-permute-start | bytes 1966088 | tf_op jit(solution)/shard_map/ppermute | solution.py:12
  56.1 23.7 %copy-start = (f32[2,2,128,128]{2,3,1,0:T(8,128)}, f32[2,2,128,128]{2,3,1,0:T(8,128)S(1)}, u32[]{:S(2)}) copy-start(f32[2,2,128,128]{2,3,1,0:T(8,128)S(1)} %get-tuple-element.435) | copy-start | bytes 786436 | tf_op jit(solution)/shard_map/while
  84.5 1.9 copy-start.2
  137.9 23.5 %copy-start.1 = (f32[2,2,128,128]{2,3,1,0:T(8,128)S(1)}, f32[2,2,128,128]{2,3,1,0:T(8,128)}, u32[]{:S(2)}) copy-start(f32[2,2,128,128]{2,3,1,0:T(8,128)} %copy-done) | copy-start | bytes 786436 | tf_op jit(solution)/shard_map/while
  161.5 23.7 %copy-start = (f32[2,2,128,128]{2,3,1,0:T(8,128)}, f32[2,2,128,128]{2,3,1,0:T(8,128)S(1)}, u32[]{:S(2)}) copy-start(f32[2,2,128,128]{2,3,1,0:T(8,128)S(1)} %get-tuple-element.435) | copy-start | bytes 786436 | tf_op jit(solution)/shard_map/while
  189.8 1.9 copy-start.2
  243.4 23.2 %copy-start.1 = (f32[2,2,128,128]{2,3,1,0:T(8,128)S(1)}, f32[2,2,128,128]{2,3,1,0:T(8,128)}, u32[]{:S(2)}) copy-start(f32[2,2,128,128]{2,3,1,0:T(8,128)} %copy-done) | copy-start | bytes 786436 | tf_op jit(solution)/shard_map/while
  270.1 14.8 %collective-permute-start.2 = (f32[2,128,640]{2,1,0:T(8,128)S(1)}, f32[2,128,640]{2,1,0:T(8,128)S(1)}, u32[]{:S(2)}, u32[]{:S(2)}) collective-permute-start(f32[2,128,640]{2,1,0:T(8,128)S(1)} %slice.216), channel_id=1, source_target_pairs={{0,64},{64,128},{128,192},{1,65},{65,129},{129,193},{2,66},{66,130... | collective-permute-start | bytes 1966088 | tf_op jit(solution)/shard_map/ppermute | solution.py:12
  286.9 893.7 %collective-permute-start.3 = (f32[2,512,128]{2,1,0:T(8,128)S(1)}, f32[2,512,128]{2,1,0:T(8,128)S(1)}, u32[]{:S(2)}, u32[]{:S(2)}) collective-permute-start(f32[2,512,128]{2,1,0:T(8,128)S(1)} %slice.219), channel_id=1, source_target_pairs={{0,1},{1,2},{2,3},{3,4},{4,5},{5,6},{6,7},{7,8},{8,9},{9,10},{10,1... | collective-permute-start | bytes 1572872 | tf_op jit(solution)/shard_map/ppermute | solution.py:12
  1181.7 1.3 copy-start.3
Sparse Core Ops, SparseCore 0:
  388.7 788.4 all-reduce.1
where the time goes:
time: 1210 us; the launch traced here: 1190 us
  waiting for transfers between devices  831 us (69%)
  local copies, waits for them, and re-layouts  135 us (11%)
  starting transfers between devices  108 us (9%)
  loops' own time  60.8 us (5%)
  other arithmetic  34.4 us (3%)
  between operations  14.8 us (1%)
    psum x1, waiting for transfers between devices, body(): total_probe = lax.psum(probe_sum, ('row', 'col'))  789 us
    ppermute x4, starting transfers between devices, shifted(): return lax.ppermute(value, axis, pairs)  108 us
    another operation x1, loops' own time, own_slots(): lax.fori_loop(low_slot // 8, (high_slot + 7) // 8, block_step, (gradient,...  60.5 us
    dynamic_update_slice x16, local copies, waits for them, and re-layouts, add_patches(): lax.dynamic_update_slice(gradient, present + patch_gradient[k], corner_at)  58.2 us
    gather x48, local copies, waits for them, and re-layouts  45.7 us
    ppermute x4, waiting for transfers between devices, shifted(): return lax.ppermute(value, axis, pairs)  42.6 us
  transfers between devices with their start and end apart: 5, of which 4 were waited for; matrix products, arithmetic and copies ran while one was open for 1% of the time, Pallas kernels for 0%

commit v1 on v0

v1 whole, which is shorter than its diff:
```python
import math

import jax
import jax.numpy as jnp
import numpy as np
from jax import lax
from jax.experimental import pallas as pl
from jax.experimental.pallas import tpu as pltpu
from jax.sharding import PartitionSpec as P

F32 = jnp.float32
BF16 = jnp.bfloat16
PATCH = 128
BLOCK = 4
BOTH = ("row", "col")


def fourier_tables(patch_len):
    index_range = np.arange(patch_len)
    product = (index_range[:, None] * index_range[None, :]) % patch_len
    angle = product.astype(np.float32) * np.float32(2.0 * math.pi / patch_len)
    cosine = (np.cos(angle) / np.float32(math.sqrt(patch_len))).astype(np.float32)
    sine = (np.sin(angle) / np.float32(math.sqrt(patch_len))).astype(np.float32)
    plus_table = np.block([[cosine, sine], [-sine, cosine]])
    minus_table = np.block([[cosine, -sine], [sine, cosine]])
    return jnp.asarray(plus_table, BF16), jnp.asarray(minus_table, BF16)


def dot(a, b):
    return jnp.dot(a, b, preferred_element_type=F32)


def slot_block(slots, valids, pos, field, grad, photons, probe, probe_sum, plus_ref, minus_ref):
    n = len(slots)
    lane = lax.broadcasted_iota(jnp.int32, (PATCH, PATCH), 1)
    plus = plus_ref[...]
    minus = minus_ref[...]
    places, patches, waves = [], [], []
    for s in slots:
        top = pos[0, s]
        left = pos[1, s]
        tile = left // PATCH
        shift = left % PATCH
        back = (PATCH - shift) % PATCH
        keep = lane >= shift
        patch = []
        for k in range(2):
            a = field[tile, k, pl.ds(top, PATCH), :]
            b = field[tile + 1, k, pl.ds(top, PATCH), :]
            patch.append(pltpu.roll(jnp.where(keep, a, b), back, 1))
        places.append((top, tile, shift, keep))
        patches.append(patch)
        for m in range(2):
            pr = probe[0, m]
            pi = probe[1, m]
            wr = (pr * patch[0] - pi * patch[1]).astype(BF16)
            wi = (pr * patch[1] + pi * patch[0]).astype(BF16)
            waves.append(jnp.concatenate([wr, wi], axis=0))
    first = dot(plus, jnp.concatenate(waves, axis=1)).astype(BF16)
    cols = [slice(q * PATCH, (q + 1) * PATCH) for q in range(2 * n)]
    turned = [jnp.concatenate([first[:PATCH, q], first[PATCH:, q]], axis=1) for q in cols]
    far = dot(jnp.concatenate(turned, axis=0), minus)
    scaled = []
    for i in range(n):
        f0 = far[2 * i * PATCH:(2 * i + 1) * PATCH]
        f1 = far[(2 * i + 1) * PATCH:(2 * i + 2) * PATCH]
        power = f0 * f0 + f1 * f1
        intensity = power[:, :PATCH] + power[:, PATCH:]
        factor = (1.0 - photons[slots[i]].astype(F32) / (intensity + 1.0)) * valids[i]
        for f in (f0, f1):
            re = (f[:, :PATCH] * factor).astype(BF16)
            im = (f[:, PATCH:] * factor).astype(BF16)
            scaled.append(jnp.concatenate([re, im], axis=1))
    back_pass = dot(jnp.concatenate(scaled, axis=0), plus).astype(BF16)
    unturned = [jnp.concatenate([back_pass[q, :PATCH], back_pass[q, PATCH:]], axis=0) for q in cols]
    exit_grad = dot(minus, jnp.concatenate(unturned, axis=1))
    for m in range(2):
        sum_re = sum_im = None
        for i in range(n):
            er = exit_grad[:PATCH, cols[2 * i + m]]
            ei = exit_grad[PATCH:, cols[2 * i + m]]
            o_re, o_im = patches[i]
            t_re = o_re * er + o_im * ei
            t_im = o_re * ei - o_im * er
            sum_re = t_re if sum_re is None else sum_re + t_re
            sum_im = t_im if sum_im is None else sum_im + t_im
        probe_sum[0, m] += sum_re
        probe_sum[1, m] += sum_im
    for i in range(n):
        g_re = g_im = None
        for m in range(2):
            er = exit_grad[:PATCH, cols[2 * i + m]]
            ei = exit_grad[PATCH:, cols[2 * i + m]]
            pr = probe[0, m]
            pi = probe[1, m]
            t_re = pr * er + pi * ei
            t_im = pr * ei - pi * er
            g_re = t_re if g_re is None else g_re + t_re
            g_im = t_im if g_im is None else g_im + t_im
        top, tile, shift, keep = places[i]
        for k, g in ((0, g_re), (1, g_im)):
            g = pltpu.roll(g, shift, 1)
            grad[tile, k, pl.ds(top, PATCH), :] += jnp.where(keep, g, 0.0)
            grad[tile + 1, k, pl.ds(top, PATCH), :] += jnp.where(keep, 0.0, g)


def run_slots(inner, rows, cols, pos, count, listed, field, grad, photons, probe, probe_sum, plus_ref, minus_ref):
    def list_step(s, found):
        listed[found] = s
        inside = (pos[0, s] <= rows - PATCH) & (pos[1, s] <= cols - PATCH)
        wanted = inside if inner else jnp.logical_not(inside)
        return found + wanted.astype(jnp.int32)

    found = lax.fori_loop(0, count, list_step, jnp.int32(0))

    def step(k, carry):
        at = [k * BLOCK + i for i in range(BLOCK)]
        slots = [listed[jnp.minimum(a, found - 1)] for a in at]
        valids = [jnp.where(a < found, 1.0, 0.0).astype(F32) for a in at]
        slot_block(slots, valids, pos, field, grad, photons, probe, probe_sum, plus_ref, minus_ref)
        return carry

    lax.fori_loop(0, (found + BLOCK - 1) // BLOCK, step, 0)


def tile_copies(hbm, vmem, rows, tiles, row_at, sems, first, out=False):
    copies = []
    for t in range(tiles):
        a = hbm.at[:, :, pl.ds(t * PATCH, PATCH)]
        b = vmem.at[t, :, pl.ds(row_at, rows), :]
        copies.append(pltpu.make_async_copy(b, a, sems.at[first + t]) if out else
                      pltpu.make_async_copy(a, b, sems.at[first + t]))
    return copies


def inner_kernel(pos, count, own, photons, probe, plus_ref, minus_ref, grad_out, probe_out,
                 field, grad, photon_buf, listed, sems):
    rows, cols = own.shape[1], own.shape[2]
    tiles = cols // PATCH
    loads = tile_copies(own, field, rows, tiles, 0, sems, 0)
    loads.append(pltpu.make_async_copy(photons, photon_buf, sems.at[tiles]))
    for c in loads:
        c.start()
    for t in range(tiles + 1):
        grad[t] = jnp.zeros(grad.shape[1:], F32)
    probe_out[...] = jnp.zeros(probe_out.shape, F32)
    field[tiles] = jnp.zeros(field.shape[1:], F32)
    for c in loads:
        c.wait()
    run_slots(True, rows, cols, pos, count[0], listed, field, grad, photon_buf, probe, probe_out,
              plus_ref, minus_ref)
    for t in range(tiles):
        pltpu.make_async_copy(grad.at[t], grad_out.at[t], sems.at[t]).start()
    for t in range(tiles):
        pltpu.make_async_copy(grad.at[t], grad_out.at[t], sems.at[t]).wait()


def border_kernel(pos, count, own, right, below, corner, photons, probe, plus_ref, minus_ref, grad_in, probe_in,
                  g_own, g_right, g_below, g_corner, probe_out, field, grad, photon_buf, listed, sems):
    rows, cols = own.shape[1], own.shape[2]
    tiles = cols // PATCH
    loads = tile_copies(own, field, rows, tiles, 0, sems, 0)
    loads += tile_copies(below, field, PATCH, tiles, rows, sems, tiles)
    n = 2 * tiles
    loads.append(pltpu.make_async_copy(right, field.at[tiles, :, pl.ds(0, rows), :], sems.at[n]))
    loads.append(pltpu.make_async_copy(corner, field.at[tiles, :, pl.ds(rows, PATCH), :], sems.at[n + 1]))
    loads.append(pltpu.make_async_copy(photons, photon_buf, sems.at[n + 2]))
    for t in range(tiles):
        loads.append(pltpu.make_async_copy(grad_in.at[t], grad.at[t, :, pl.ds(0, rows), :], sems.at[n + 3 + t]))
    for c in loads:
        c.start()
    grad[tiles] = jnp.zeros(grad.shape[1:], F32)
    for t in range(tiles):
        grad[t, :, pl.ds(rows, PATCH), :] = jnp.zeros((2, PATCH, PATCH), F32)
    probe_out[...] = probe_in[...]
    for c in loads:
        c.wait()
    run_slots(False, rows, cols, pos, count[0], listed, field, grad, photon_buf, probe, probe_out,
              plus_ref, minus_ref)
    stores = tile_copies(g_own, grad, rows, tiles, 0, sems, 0, out=True)
    stores += tile_copies(g_below, grad, PATCH, tiles, rows, sems, tiles, out=True)
    stores.append(pltpu.make_async_copy(grad.at[tiles, :, pl.ds(0, rows), :], g_right, sems.at[n]))
    stores.append(pltpu.make_async_copy(grad.at[tiles, :, pl.ds(rows, PATCH), :], g_corner, sems.at[n + 1]))
    for c in stores:
        c.start()
    for c in stores:
        c.wait()


def shape(*dims):
    return jax.ShapeDtypeStruct(dims, F32)


def bit_exchange(value, bit):
    size = lax.axis_size(BOTH)
    return lax.ppermute(value, BOTH, [(i, i ^ bit) for i in range(size)])


def total_over_devices(value):
    me = lax.axis_index(BOTH)
    x_low, x_high = (me // 16) % 2, (me // 32) % 2
    halving = ((1, me % 2), (16, (x_low + x_high) % 2), (48, x_high))
    whole = (4, 12, 2, 64, 128)
    lows = []
    for mask, label in halving:
        half = value.shape[0] // 2
        upper = label != 0
        keep = jnp.where(upper, value[half:], value[:half])
        send = jnp.where(upper, value[:half], value[half:])
        value = keep + bit_exchange(send, mask)
        lows.append(upper)
    for mask in whole:
        value = value + bit_exchange(value, mask)
    for (mask, _), upper in zip(halving[::-1], lows[::-1]):
        other = bit_exchange(value, mask)
        value = jnp.concatenate([jnp.where(upper, other, value), jnp.where(upper, value, other)], axis=0)
    return value


def body(object_field, probe_modes, photons, positions, counts):
    rows, cols = object_field.shape[1], object_field.shape[2]
    slot_count = photons.shape[2]
    tiles = cols // PATCH
    n_row, n_col = lax.axis_size("row"), lax.axis_size("col")
    plus_table, minus_table = fourier_tables(PATCH)
    pos = positions[0, 0].T
    count = counts[0]
    photon_rows = photons[0, 0]
    right = lax.ppermute(object_field[:, :, :PATCH], "col", [(i, i - 1) for i in range(1, n_col)])
    below = lax.ppermute(object_field[:, :PATCH, :], "row", [(i, i - 1) for i in range(1, n_row)])
    corner = lax.ppermute(below[:, :, :PATCH], "col", [(i, i - 1) for i in range(1, n_col)])

    smem = pl.BlockSpec(memory_space=pltpu.SMEM)
    vmem = pl.BlockSpec(memory_space=pltpu.VMEM)
    hbm = pl.BlockSpec(memory_space=pl.ANY)
    scratch = [
        pltpu.VMEM((tiles + 1, 2, rows + PATCH, PATCH), F32),
        pltpu.VMEM((tiles + 1, 2, rows + PATCH, PATCH), F32),
        pltpu.VMEM(photon_rows.shape, BF16),
        pltpu.SMEM((slot_count,), jnp.int32),
        pltpu.SemaphoreType.DMA((3 * tiles + 3,)),
    ]
    inner_scratch = [
        pltpu.VMEM((tiles + 1, 2, rows, PATCH), F32),
        pltpu.VMEM((tiles + 1, 2, rows, PATCH), F32),
    ] + scratch[2:]
    params = pltpu.CompilerParams(vmem_limit_bytes=40 * 2**20)
    work = 4 * 2 * 256 * 256 * 256 * slot_count // 2
    cost = pl.CostEstimate(flops=work, bytes_accessed=8 * 2**20, transcendentals=0)
    grad_1, probe_1 = pl.pallas_call(
        inner_kernel,
        out_shape=(shape(tiles, 2, rows, PATCH), shape(*probe_modes.shape)),
        in_specs=[smem, smem, hbm, hbm, vmem, vmem, vmem],
        out_specs=(hbm, vmem),
        scratch_shapes=inner_scratch,
        compiler_params=params,
        cost_estimate=cost,
        name="inner_slots",
    )(pos, count, object_field, photon_rows, probe_modes, plus_table, minus_table)
    g_own, g_right, g_below, g_corner, probe_2 = pl.pallas_call(
        border_kernel,
        out_shape=(
            shape(2, rows, cols), shape(2, rows, PATCH), shape(2, PATCH, cols), shape(2, PATCH, PATCH),
            shape(*probe_modes.shape),
        ),
        in_specs=[smem, smem, hbm, hbm, hbm, hbm, hbm, vmem, vmem, vmem, hbm, vmem],
        out_specs=(hbm, hbm, hbm, hbm, vmem),
        scratch_shapes=scratch,
        compiler_params=params,
        cost_estimate=cost,
        name="border_slots",
    )(pos, count, object_field, right, below, corner, photon_rows, probe_modes, plus_table, minus_table,
      grad_1, probe_1)

    down = [(i, i + 1) for i in range(n_row - 1)]
    along = [(i, i + 1) for i in range(n_col - 1)]
    diagonal = [
        (a * n_col + b, (a + 1) * n_col + b + 1) for a in range(n_row - 1) for b in range(n_col - 1)
    ]
    from_above = lax.ppermute(g_below, "row", down)
    from_left = lax.ppermute(g_right, "col", along)
    from_corner = lax.ppermute(g_corner, BOTH, diagonal)
    total_probe = total_over_devices(probe_2.reshape(-1, PATCH)).reshape(probe_modes.shape)
    probe_gradient = total_probe / math.sqrt(n_row * n_col * slot_count)
    object_gradient = g_own.at[:, :PATCH, :].add(from_above)
    object_gradient = object_gradient.at[:, :, :PATCH].add(from_left)
    object_gradient = object_gradient.at[:, :PATCH, :PATCH].add(from_corner)
    return (object_gradient, probe_gradient)


def solution(mesh):
    in_specs = (
        P(None, "row", "col"),
        P(),
        P("row", "col", None, None, None),
        P("row", "col", None, None),
        P("row", "col"),
    )
    out_specs = (P(None, "row", "col"), P())
    return jax.shard_map(body, mesh=mesh, in_specs=in_specs, out_specs=out_specs, check_vma=False)
```

time: 1210 us -> 149 us (0.12)
  the two profiles are of different devices: /device:TPU:1 before, /device:TPU:160 now
where the time goes in v1:
time: 149 us; the launch traced here: 148 us
  starting transfers between devices  60 us (40%)
  waiting for transfers between devices  56.2 us (38%)
  local copies, waits for them, and re-layouts  19.7 us (13%)
  Pallas kernels  8.88 us (6%)
  between operations  1.58 us (1%)
    ppermute x11, starting transfers between devices, bit_exchange(): return lax.ppermute(value, BOTH, [(i, i ^ bit) for i in range(size)])  34 us
    ppermute x11, waiting for transfers between devices, bit_exchange(): return lax.ppermute(value, BOTH, [(i, i ^ bit) for i in range(size)])  21.8 us
    unnamed x40, local copies, waits for them, and re-layouts  16 us
    ppermute x1, starting transfers between devices, body(): lax.ppermute(below[:, :, :PATCH], 'col', [(i, i - 1) for i in range(1, n_...  13.2 us
    ppermute x1, waiting for transfers between devices, body(): from_above = lax.ppermute(g_below, 'row', down)  10.6 us
    ppermute x1, waiting for transfers between devices, body(): lax.ppermute(object_field[:, :PATCH, :], 'row', [(i, i - 1) for i in rang...  9.66 us
    ppermute x1, waiting for transfers between devices, body(): from_left = lax.ppermute(g_right, 'col', along)  7.8 us
    ppermute x1, waiting for transfers between devices, body(): from_corner = lax.ppermute(g_corner, BOTH, diagonal)  6.33 us
  transfers between devices with their start and end apart: 17, of which 12 were waited for; matrix products, arithmetic and copies ran while one was open for 2% of the time, Pallas kernels for 3%

profile of v1, /device:TPU:160, one launch (start us, length us, event | category | flops | bytes accessed | tf_op | source)
XLA Modules:
  0.0 147.7 jit_solution(5502325061648600007)
XLA Ops:
  0.7 1.2 slice.113
  1.9 2.5 %collective-permute-start.1 = (f32[2,128,512]{2,1,0:T(8,128)S(1)}, f32[2,128,512]{2,1,0:T(8,128)S(1)}, u32[]{:S(2)}, u32[]{:S(2)}) collective-permute-start(f32[2,128,512]{2,1,0:T(8,128)S(1)} %slice.113), channel_id=1, source_target_pairs={{64,0},{128,64},{192,128},{65,1},{129,65},{193,129},{66,2},{130,66... | collective-permute-start | bytes 1572872 | tf_op jit(solution)/shard_map/ppermute | solution.py:230
  4.4 1.9 %slice.112 = f32[2,512,128]{2,1,0:T(8,128)} slice(f32[2,512,512]{2,1,0:T(8,128)} %own.3), slice={[0:2], [0:512], [0:128]} | slice | bytes 1048576 | tf_op jit(solution)/shard_map/slice | solution.py:229
  6.2 1.9 %collective-permute-start = (f32[2,512,128]{2,1,0:T(8,128)}, f32[2,512,128]{2,1,0:T(8,128)S(1)}, u32[]{:S(2)}, u32[]{:S(2)}) collective-permute-start(f32[2,512,128]{2,1,0:T(8,128)} %slice.112), channel_id=1, source_target_pairs={{1,0},{2,1},{3,2},{4,3},{5,4},{6,5},{7,6},{8,7},{9,8},{10,9},{11,1... | collective-permute-start | bytes 1572872 | tf_op jit(solution)/shard_map/ppermute | solution.py:229
  8.8 9.7 %collective-permute-done.1.below = f32[2,128,512]{2,1,0:T(8,128)S(1)} collective-permute-done((f32[2,128,512]{2,1,0:T(8,128)S(1)}, f32[2,128,512]{2,1,0:T(8,128)S(1)}, u32[]{:S(2)}, u32[]{:S(2)}) %collective-permute-start.1) | collective-permute-done | bytes 524320 | tf_op jit(solution)/shard_map/ppermute | solution.py:230
  19.1 13.2 %collective-permute-start.2 = (f32[2,128,128]{2,1,0:T(8,128)}, f32[2,128,128]{2,1,0:T(8,128)S(1)}, u32[]{:S(2)}, u32[]{:S(2)}) collective-permute-start(f32[2,128,128]{2,1,0:T(8,128)} %slice.124), channel_id=1, source_target_pairs={{1,0},{2,1},{3,2},{4,3},{5,4},{6,5},{7,6},{8,7},{9,8},{10,9},{11,1... | collective-permute-start | bytes 393224 | tf_op jit(solution)/shard_map/ppermute | solution.py:231
  32.4 1.6 %copy-done.1 = bf16[1,1,64,128,128]{4,3,2,1,0:T(8,128)(2,1)S(1)} copy-done((bf16[1,1,64,128,128]{4,3,2,1,0:T(8,128)(2,1)S(1)}, bf16[1,1,64,128,128]{4,3,2,1,0:T(8,128)(2,1)}, u32[]{:S(2)}) %copy-start.1) | copy-done | bytes 2097176
  35.8 4.5 %inner_slots.1 = (f32[4,2,512,128]{3,2,1,0:T(8,128)S(1)}, f32[2,2,128,128]{3,2,1,0:T(8,128)S(1)}) custom-call(s32[2,64]{1,0:T(2,128)S(1)} %bitcast.13, s32[1]{0:T(128)} %bitcast.9.count, f32[2,512,512]{2,1,0:T(8,128)S(1)} %copy-done, bf16[64,128,128]{2,1,0:T(8,128)(2,1)S(1)} %bitcast.11, f32[2,2,128,128]{3,2,1,0:T(8,128)S(1)} %copy-done.6, ...), custom_call_target="tpu_custom_call" | custom-call | flops 4294967296 | bytes 8388608 | tf_op jit(solution)/shard_map/inner_slots/pallas_call | solution.py:250
  40.3 1.3 copy-done.14
  43.7 1.6 %copy-done.2 = bf16[1,1,64,128,128]{4,3,2,1,0:T(8,128)(2,1)S(1)} copy-done((bf16[1,1,64,128,128]{4,3,2,1,0:T(8,128)(2,1)S(1)}, bf16[1,1,64,128,128]{4,3,2,1,0:T(8,128)(2,1)}, u32[]{:S(2)}) %copy-start.2) | copy-done | bytes 2097176
  49.1 1.6 %copy-done.15 = f32[4,2,512,128]{3,2,1,0:T(8,128)S(1)} copy-done((f32[4,2,512,128]{3,2,1,0:T(8,128)S(1)}, f32[4,2,512,128]{3,2,1,0:T(8,128)}, u32[]{:S(2)}) %copy-start.15) | copy-done | bytes 2097176
  51.6 4.4 %border_slots.1 = (f32[2,512,512]{2,1,0:T(8,128)}, f32[2,512,128]{2,1,0:T(8,128)S(1)}, f32[2,128,512]{2,1,0:T(8,128)S(1)}, f32[2,128,128]{2,1,0:T(8,128)S(1)}, f32[2,2,128,128]{3,2,1,0:T(8,128)S(1)}) custom-call(s32[2,64]{1,0:T(2,128)S(1)} %bitcast.14, s32[1]{0:T(128)} %bitcast.10.count, f32[2,512,512]{2,1,0:T(8,128)S(1)} %copy-done, ...), custom_call_target="tpu_custom_call" | custom-call | flops 4294967296 | bytes 8388608 | tf_op jit(solution)/shard_map/border_slots/pallas_call | solution.py:260
  56.8 1.3 collective-permute-done.6
  58.2 3.1 %collective-permute-start.7 = (f32[128,128]{1,0:T(8,128)S(1)}, f32[128,128]{1,0:T(8,128)S(1)}, u32[]{:S(2)}, u32[]{:S(2)}) collective-permute-start(f32[128,128]{1,0:T(8,128)S(1)} %slice_select_fusion.2), channel_id=1, source_target_pairs={{0,16},{1,17},{2,18},{3,19},{4,20},{5,21},{6,22},{7,23},{8,24},{9,... | collective-permute-start | bytes 196616 | tf_op jit(solution)/shard_map/ppermute | solution.py:196
  61.3 2.4 %collective-permute-done.7 = f32[128,128]{1,0:T(8,128)S(1)} collective-permute-done((f32[128,128]{1,0:T(8,128)S(1)}, f32[128,128]{1,0:T(8,128)S(1)}, u32[]{:S(2)}, u32[]{:S(2)}) %collective-permute-start.7) | collective-permute-done | bytes 65568 | tf_op jit(solution)/shard_map/ppermute | solution.py:196
  63.8 16.9 %collective-permute-start.8 = (f32[64,128]{1,0:T(8,128)S(1)}, f32[64,128]{1,0:T(8,128)S(1)}, u32[]{:S(2)}, u32[]{:S(2)}) collective-permute-start(f32[64,128]{1,0:T(8,128)S(1)} %slice_select_fusion.3), channel_id=1, source_target_pairs={{0,48},{1,49},{2,50},{3,51},{4,52},{5,53},{6,54},{7,55},{8,56},{9,... | collective-permute-start | bytes 98312 | tf_op jit(solution)/shard_map/ppermute | solution.py:196
  80.7 1.9 %collective-permute-done.8 = f32[64,128]{1,0:T(8,128)S(1)} collective-permute-done((f32[64,128]{1,0:T(8,128)S(1)}, f32[64,128]{1,0:T(8,128)S(1)}, u32[]{:S(2)}, u32[]{:S(2)}) %collective-permute-start.8) | collective-permute-done | bytes 32800 | tf_op jit(solution)/shard_map/ppermute | solution.py:196
  82.6 3.9 %collective-permute-done.9 = f32[64,128]{1,0:T(8,128)S(1)} collective-permute-done((f32[64,128]{1,0:T(8,128)S(1)}, f32[64,128]{1,0:T(8,128)S(1)}, u32[]{:S(2)}, u32[]{:S(2)}) %collective-permute-start.9) | collective-permute-done | bytes 32800 | tf_op jit(solution)/shard_map/ppermute | solution.py:196
  86.5 2.9 %collective-permute-start.10 = (f32[64,128]{1,0:T(8,128)S(1)}, f32[64,128]{1,0:T(8,128)S(1)}, u32[]{:S(2)}, u32[]{:S(2)}) collective-permute-start(f32[64,128]{1,0:T(8,128)S(1)} %add.78), channel_id=1, source_target_pairs={{0,12},{1,13},{2,14},{3,15},{4,8},{5,9},{6,10},{7,11},{8,4},{9,5},... | collective-permute-start | bytes 98312 | tf_op jit(solution)/shard_map/ppermute | solution.py:196
  89.4 2.2 %collective-permute-done.10 = f32[64,128]{1,0:T(8,128)S(1)} collective-permute-done((f32[64,128]{1,0:T(8,128)S(1)}, f32[64,128]{1,0:T(8,128)S(1)}, u32[]{:S(2)}, u32[]{:S(2)}) %collective-permute-start.10) | collective-permute-done | bytes 32800 | tf_op jit(solution)/shard_map/ppermute | solution.py:196
  91.6 2.5 %collective-permute-start.11 = (f32[64,128]{1,0:T(8,128)S(1)}, f32[64,128]{1,0:T(8,128)S(1)}, u32[]{:S(2)}, u32[]{:S(2)}) collective-permute-start(f32[64,128]{1,0:T(8,128)S(1)} %add.79), channel_id=1, source_target_pairs={{0,2},{1,3},{2,0},{3,1},{4,6},{5,7},{6,4},{7,5},{8,10},{9,11},{10,... | collective-permute-start | bytes 98312 | tf_op jit(solution)/shard_map/ppermute | solution.py:196
  94.1 1.9 %collective-permute-done.11 = f32[64,128]{1,0:T(8,128)S(1)} collective-permute-done((f32[64,128]{1,0:T(8,128)S(1)}, f32[64,128]{1,0:T(8,128)S(1)}, u32[]{:S(2)}, u32[]{:S(2)}) %collective-permute-start.11) | collective-permute-done | bytes 32800 | tf_op jit(solution)/shard_map/ppermute | solution.py:196
  96.0 4.8 %collective-permute-done.12 = f32[64,128]{1,0:T(8,128)S(1)} collective-permute-done((f32[64,128]{1,0:T(8,128)S(1)}, f32[64,128]{1,0:T(8,128)S(1)}, u32[]{:S(2)}, u32[]{:S(2)}) %collective-permute-start.12) | collective-permute-done | bytes 32800 | tf_op jit(solution)/shard_map/ppermute | solution.py:196
  100.8 4.5 %collective-permute-start.13 = (f32[64,128]{1,0:T(8,128)S(1)}, f32[64,128]{1,0:T(8,128)S(1)}, u32[]{:S(2)}, u32[]{:S(2)}) collective-permute-start(f32[64,128]{1,0:T(8,128)S(1)} %add.81), channel_id=1, source_target_pairs={{0,128},{1,129},{2,130},{3,131},{4,132},{5,133},{6,134},{7,135},{8... | collective-permute-start | bytes 98312 | tf_op jit(solution)/shard_map/ppermute | solution.py:196
  105.3 3.3 %collective-permute-done.13 = f32[64,128]{1,0:T(8,128)S(1)} collective-permute-done((f32[64,128]{1,0:T(8,128)S(1)}, f32[64,128]{1,0:T(8,128)S(1)}, u32[]{:S(2)}, u32[]{:S(2)}) %collective-permute-start.13) | collective-permute-done | bytes 32800 | tf_op jit(solution)/shard_map/ppermute | solution.py:196
  108.6 3.4 %collective-permute-start.14 = (f32[64,128]{1,0:T(8,128)S(1)}, f32[64,128]{1,0:T(8,128)S(1)}, u32[]{:S(2)}, u32[]{:S(2)}) collective-permute-start(f32[64,128]{1,0:T(8,128)S(1)} %add.82), channel_id=1, source_target_pairs={{0,48},{1,49},{2,50},{3,51},{4,52},{5,53},{6,54},{7,55},{8,56},{9,... | collective-permute-start | bytes 98312 | tf_op jit(solution)/shard_map/ppermute | solution.py:196
  112.0 1.9 %collective-permute-start.3 = (f32[2,128,512]{2,1,0:T(8,128)}, f32[2,128,512]{2,1,0:T(8,128)S(1)}, u32[]{:S(2)}, u32[]{:S(2)}) collective-permute-start(f32[2,128,512]{2,1,0:T(8,128)} %copy-done.3), channel_id=1, source_target_pairs={{0,64},{64,128},{128,192},{1,65},{65,129},{129,193},{2,66},{66,130... | collective-permute-start | bytes 1572872 | tf_op jit(solution)/shard_map/ppermute | solution.py:280
  114.1 1.9 %collective-permute-start.4 = (f32[2,512,128]{2,1,0:T(8,128)S(1)}, f32[2,512,128]{2,1,0:T(8,128)S(1)}, u32[]{:S(2)}, u32[]{:S(2)}) collective-permute-start(f32[2,512,128]{2,1,0:T(8,128)S(1)} %get-tuple-element.49), channel_id=1, source_target_pairs={{0,1},{1,2},{2,3},{3,4},{4,5},{5,6},{6,7},{7,8},{8,9},{9,10},{10,1... | collective-permute-start | bytes 1572872 | tf_op jit(solution)/shard_map/ppermute | solution.py:281
  116.0 4.5 %collective-permute-start.5 = (f32[2,128,128]{2,1,0:T(8,128)S(1)}, f32[2,128,128]{2,1,0:T(8,128)S(1)}, u32[]{:S(2)}, u32[]{:S(2)}) collective-permute-start(f32[2,128,128]{2,1,0:T(8,128)S(1)} %get-tuple-element.50), channel_id=1, source_target_pairs={{0,65},{1,66},{2,67},{3,68},{4,69},{5,70},{6,71},{7,72},{8,73},{9,... | collective-permute-start | bytes 393224 | tf_op jit(solution)/shard_map/ppermute | solution.py:282
  121.2 10.6 %collective-permute-done.3 = f32[2,128,512]{2,1,0:T(8,128)S(1)} collective-permute-done((f32[2,128,512]{2,1,0:T(8,128)}, f32[2,128,512]{2,1,0:T(8,128)S(1)}, u32[]{:S(2)}, u32[]{:S(2)}) %collective-permute-start.3) | collective-permute-done | bytes 524320 | tf_op jit(solution)/shard_map/ppermute | solution.py:280
  131.9 7.8 %collective-permute-done.4 = f32[2,512,128]{2,1,0:T(8,128)S(1)} collective-permute-done((f32[2,512,128]{2,1,0:T(8,128)S(1)}, f32[2,512,128]{2,1,0:T(8,128)S(1)}, u32[]{:S(2)}, u32[]{:S(2)}) %collective-permute-start.4) | collective-permute-done | bytes 524320 | tf_op jit(solution)/shard_map/ppermute | solution.py:281
  140.0 6.3 %collective-permute-done.5 = f32[2,128,128]{2,1,0:T(8,128)S(1)} collective-permute-done((f32[2,128,128]{2,1,0:T(8,128)S(1)}, f32[2,128,128]{2,1,0:T(8,128)S(1)}, u32[]{:S(2)}, u32[]{:S(2)}) %collective-permute-start.5) | collective-permute-done | bytes 131104 | tf_op jit(solution)/shard_map/ppermute | solution.py:282
  (67 shorter events, 12.7 us)
Async XLA Ops:
  0.6 31.7 %copy-start = (f32[2,512,512]{2,1,0:T(8,128)S(1)}, f32[2,512,512]{2,1,0:T(8,128)}, u32[]{:S(2)}) copy-start(f32[2,512,512]{2,1,0:T(8,128)} %own.3) | copy-start | bytes 6291460
  0.6 31.7 %copy-start.9 = (s32[1,1,64,2]{2,3,1,0:T(2,128)S(1)}, s32[1,1,64,2]{2,3,1,0:T(2,128)}, u32[]{:S(2)}) copy-start(s32[1,1,64,2]{2,3,1,0:T(2,128)} %param.16) | copy-start | bytes 1540
  0.7 31.7 %copy-start.6 = (f32[2,2,128,128]{3,2,1,0:T(8,128)S(1)}, f32[2,2,128,128]{3,2,1,0:T(8,128)}, u32[]{:S(2)}) copy-start(f32[2,2,128,128]{3,2,1,0:T(8,128)} %probe.3) | copy-start | bytes 786436
  1.9 16.6 %collective-permute-start.1 = (f32[2,128,512]{2,1,0:T(8,128)S(1)}, f32[2,128,512]{2,1,0:T(8,128)S(1)}, u32[]{:S(2)}, u32[]{:S(2)}) collective-permute-start(f32[2,128,512]{2,1,0:T(8,128)S(1)} %slice.113), channel_id=1, source_target_pairs={{64,0},{128,64},{192,128},{65,1},{129,65},{193,129},{66,2},{130,66... | collective-permute-start | bytes 1572872 | tf_op jit(solution)/shard_map/ppermute | solution.py:230
  6.2 36.1 %collective-permute-start = (f32[2,512,128]{2,1,0:T(8,128)}, f32[2,512,128]{2,1,0:T(8,128)S(1)}, u32[]{:S(2)}, u32[]{:S(2)}) collective-permute-start(f32[2,512,128]{2,1,0:T(8,128)} %slice.112), channel_id=1, source_target_pairs={{1,0},{2,1},{3,2},{4,3},{5,4},{6,5},{7,6},{8,7},{9,8},{10,9},{11,1... | collective-permute-start | bytes 1572872 | tf_op jit(solution)/shard_map/ppermute | solution.py:229
  19.1 24.0 %collective-permute-start.2 = (f32[2,128,128]{2,1,0:T(8,128)}, f32[2,128,128]{2,1,0:T(8,128)S(1)}, u32[]{:S(2)}, u32[]{:S(2)}) collective-permute-start(f32[2,128,128]{2,1,0:T(8,128)} %slice.124), channel_id=1, source_target_pairs={{1,0},{2,1},{3,2},{4,3},{5,4},{6,5},{7,6},{8,7},{9,8},{10,9},{11,1... | collective-permute-start | bytes 393224 | tf_op jit(solution)/shard_map/ppermute | solution.py:231
  32.4 1.6 %copy-start.1 = (bf16[1,1,64,128,128]{4,3,2,1,0:T(8,128)(2,1)S(1)}, bf16[1,1,64,128,128]{4,3,2,1,0:T(8,128)(2,1)}, u32[]{:S(2)}) copy-start(bf16[1,1,64,128,128]{4,3,2,1,0:T(8,128)(2,1)} %param.15) | copy-start | bytes 6291460
  34.0 0.9 copy-start.10
  34.9 0.9 copy-start.12
  40.3 1.3 copy-start.14
  43.7 1.6 %copy-start.2 = (bf16[1,1,64,128,128]{4,3,2,1,0:T(8,128)(2,1)S(1)}, bf16[1,1,64,128,128]{4,3,2,1,0:T(8,128)(2,1)}, u32[]{:S(2)}) copy-start(bf16[1,1,64,128,128]{4,3,2,1,0:T(8,128)(2,1)} %param.15) | copy-start | bytes 6291460
  45.3 1.0 copy-start.5
  46.4 0.9 copy-start.8
  47.3 0.9 copy-start.11
  49.1 1.6 %copy-start.15 = (f32[4,2,512,128]{3,2,1,0:T(8,128)S(1)}, f32[4,2,512,128]{3,2,1,0:T(8,128)}, u32[]{:S(2)}) copy-start(f32[4,2,512,128]{3,2,1,0:T(8,128)} %copy-done.14) | copy-start | bytes 6291460
  50.7 0.9 copy-start.17
  56.0 75.8 %copy-start.18 = (f32[2,512,512]{2,1,0:T(8,128)S(1)}, f32[2,512,512]{2,1,0:T(8,128)}, u32[]{:S(2)}) copy-start(f32[2,512,512]{2,1,0:T(8,128)} %get-tuple-element.47) | copy-start | bytes 6291460
  56.8 1.3 collective-permute-start.6
  58.2 5.5 %collective-permute-start.7 = (f32[128,128]{1,0:T(8,128)S(1)}, f32[128,128]{1,0:T(8,128)S(1)}, u32[]{:S(2)}, u32[]{:S(2)}) collective-permute-start(f32[128,128]{1,0:T(8,128)S(1)} %slice_select_fusion.2), channel_id=1, source_target_pairs={{0,16},{1,17},{2,18},{3,19},{4,20},{5,21},{6,22},{7,23},{8,24},{9,... | collective-permute-start | bytes 196616 | tf_op jit(solution)/shard_map/ppermute | solution.py:196
  63.8 18.8 %collective-permute-start.8 = (f32[64,128]{1,0:T(8,128)S(1)}, f32[64,128]{1,0:T(8,128)S(1)}, u32[]{:S(2)}, u32[]{:S(2)}) collective-permute-start(f32[64,128]{1,0:T(8,128)S(1)} %slice_select_fusion.3), channel_id=1, source_target_pairs={{0,48},{1,49},{2,50},{3,51},{4,52},{5,53},{6,54},{7,55},{8,56},{9,... | collective-permute-start | bytes 98312 | tf_op jit(solution)/shard_map/ppermute | solution.py:196
  82.6 3.9 %collective-permute-start.9 = (f32[64,128]{1,0:T(8,128)S(1)}, f32[64,128]{1,0:T(8,128)S(1)}, u32[]{:S(2)}, u32[]{:S(2)}) collective-permute-start(f32[64,128]{1,0:T(8,128)S(1)} %select_add_fusion.1), channel_id=1, source_target_pairs={{0,4},{1,5},{2,6},{3,7},{4,0},{5,1},{6,2},{7,3},{8,12},{9,13},{10,... | collective-permute-start | bytes 98312 | tf_op jit(solution)/shard_map/ppermute | solution.py:196
  86.5 5.1 %collective-permute-start.10 = (f32[64,128]{1,0:T(8,128)S(1)}, f32[64,128]{1,0:T(8,128)S(1)}, u32[]{:S(2)}, u32[]{:S(2)}) collective-permute-start(f32[64,128]{1,0:T(8,128)S(1)} %add.78), channel_id=1, source_target_pairs={{0,12},{1,13},{2,14},{3,15},{4,8},{5,9},{6,10},{7,11},{8,4},{9,5},... | collective-permute-start | bytes 98312 | tf_op jit(solution)/shard_map/ppermute | solution.py:196
  91.6 4.3 %collective-permute-start.11 = (f32[64,128]{1,0:T(8,128)S(1)}, f32[64,128]{1,0:T(8,128)S(1)}, u32[]{:S(2)}, u32[]{:S(2)}) collective-permute-start(f32[64,128]{1,0:T(8,128)S(1)} %add.79), channel_id=1, source_target_pairs={{0,2},{1,3},{2,0},{3,1},{4,6},{5,7},{6,4},{7,5},{8,10},{9,11},{10,... | collective-permute-start | bytes 98312 | tf_op jit(solution)/shard_map/ppermute | solution.py:196
  96.0 4.8 %collective-permute-start.12 = (f32[64,128]{1,0:T(8,128)S(1)}, f32[64,128]{1,0:T(8,128)S(1)}, u32[]{:S(2)}, u32[]{:S(2)}) collective-permute-start(f32[64,128]{1,0:T(8,128)S(1)} %add.80), channel_id=1, source_target_pairs={{0,64},{1,65},{2,66},{3,67},{4,68},{5,69},{6,70},{7,71},{8,72},{9,... | collective-permute-start | bytes 98312 | tf_op jit(solution)/shard_map/ppermute | solution.py:196
  100.8 7.8 %collective-permute-start.13 = (f32[64,128]{1,0:T(8,128)S(1)}, f32[64,128]{1,0:T(8,128)S(1)}, u32[]{:S(2)}, u32[]{:S(2)}) collective-permute-start(f32[64,128]{1,0:T(8,128)S(1)} %add.81), channel_id=1, source_target_pairs={{0,128},{1,129},{2,130},{3,131},{4,132},{5,133},{6,134},{7,135},{8... | collective-permute-start | bytes 98312 | tf_op jit(solution)/shard_map/ppermute | solution.py:196
  108.6 5.3 %collective-permute-start.14 = (f32[64,128]{1,0:T(8,128)S(1)}, f32[64,128]{1,0:T(8,128)S(1)}, u32[]{:S(2)}, u32[]{:S(2)}) collective-permute-start(f32[64,128]{1,0:T(8,128)S(1)} %add.82), channel_id=1, source_target_pairs={{0,48},{1,49},{2,50},{3,51},{4,52},{5,53},{6,54},{7,55},{8,56},{9,... | collective-permute-start | bytes 98312 | tf_op jit(solution)/shard_map/ppermute | solution.py:196
  112.0 19.8 %collective-permute-start.3 = (f32[2,128,512]{2,1,0:T(8,128)}, f32[2,128,512]{2,1,0:T(8,128)S(1)}, u32[]{:S(2)}, u32[]{:S(2)}) collective-permute-start(f32[2,128,512]{2,1,0:T(8,128)} %copy-done.3), channel_id=1, source_target_pairs={{0,64},{64,128},{128,192},{1,65},{65,129},{129,193},{2,66},{66,130... | collective-permute-start | bytes 1572872 | tf_op jit(solution)/shard_map/ppermute | solution.py:280
  114.0 6.5 %collective-permute-start.15 = (f32[128,128]{1,0:T(8,128)S(1)}, f32[128,128]{1,0:T(8,128)S(1)}, u32[]{:S(2)}, u32[]{:S(2)}) collective-permute-start(f32[128,128]{1,0:T(8,128)S(1)} %pad_maximum_fusion.1), channel_id=1, source_target_pairs={{0,16},{1,17},{2,18},{3,19},{4,20},{5,21},{6,22},{7,23},{8,24},{9,... | collective-permute-start | bytes 196616 | tf_op jit(solution)/shard_map/ppermute | solution.py:196
  114.1 25.7 %collective-permute-start.4 = (f32[2,512,128]{2,1,0:T(8,128)S(1)}, f32[2,512,128]{2,1,0:T(8,128)S(1)}, u32[]{:S(2)}, u32[]{:S(2)}) collective-permute-start(f32[2,512,128]{2,1,0:T(8,128)S(1)} %get-tuple-element.49), channel_id=1, source_target_pairs={{0,1},{1,2},{2,3},{3,4},{4,5},{5,6},{6,7},{7,8},{8,9},{9,10},{10,1... | collective-permute-start | bytes 1572872 | tf_op jit(solution)/shard_map/ppermute | solution.py:281
  116.0 30.3 %collective-permute-start.5 = (f32[2,128,128]{2,1,0:T(8,128)S(1)}, f32[2,128,128]{2,1,0:T(8,128)S(1)}, u32[]{:S(2)}, u32[]{:S(2)}) collective-permute-start(f32[2,128,128]{2,1,0:T(8,128)S(1)} %get-tuple-element.50), channel_id=1, source_target_pairs={{0,65},{1,66},{2,67},{3,68},{4,69},{5,70},{6,71},{7,72},{8,73},{9,... | collective-permute-start | bytes 393224 | tf_op jit(solution)/shard_map/ppermute | solution.py:282
  120.6 25.8 %collective-permute-start.16 = (f32[256,128]{1,0:T(8,128)S(1)}, f32[256,128]{1,0:T(8,128)S(1)}, u32[]{:S(2)}, u32[]{:S(2)}) collective-permute-start(f32[256,128]{1,0:T(8,128)S(1)} %pad_maximum_fusion), channel_id=1, source_target_pairs={{0,1},{1,0},{2,3},{3,2},{4,5},{5,4},{6,7},{7,6},{8,9},{9,8},{10,11... | collective-permute-start | bytes 393224 | tf_op jit(solution)/shard_map/ppermute | solution.py:196
  146.3 1.4 copy-start.19
  (5 other events, 3.8 us)

commit v2 on v1

--- a/solution.py
+++ b/solution.py
@@ -6,13 +6,19 @@
 from jax import lax
 from jax.experimental import pallas as pl
 from jax.experimental.pallas import tpu as pltpu
+from jax.sharding import Mesh
 from jax.sharding import PartitionSpec as P
 
 F32 = jnp.float32
 BF16 = jnp.bfloat16
 PATCH = 128
-BLOCK = 4
-BOTH = ("row", "col")
+BLOCK = 8
+VMEM_LIMIT = 63 * 2**20
+ROW = "z_hi"
+COL = ("x", "y", "z_lo", "core")
+BOTH = (ROW,) + COL
+PLANE = ("x", "y")
+DEPTH = ("z_hi", "z_lo")
 
 
 def fourier_tables(patch_len):
@@ -113,14 +119,21 @@
 
     found = lax.fori_loop(0, count, list_step, jnp.int32(0))
 
-    def step(k, carry):
-        at = [k * BLOCK + i for i in range(BLOCK)]
+    def step(k, carry, first=0, width=BLOCK):
+        at = [first + k * width + i for i in range(width)]
         slots = [listed[jnp.minimum(a, found - 1)] for a in at]
         valids = [jnp.where(a < found, 1.0, 0.0).astype(F32) for a in at]
         slot_block(slots, valids, pos, field, grad, photons, probe, probe_sum, plus_ref, minus_ref)
         return carry
 
-    lax.fori_loop(0, (found + BLOCK - 1) // BLOCK, step, 0)
+    rest = found % BLOCK
+    small = (rest > 0) & (rest <= BLOCK // 2)
+    blocks = found // BLOCK + ((rest > 0) & jnp.logical_not(small)).astype(jnp.int32)
+    lax.fori_loop(0, blocks, step, 0)
+
+    @pl.when(small)
+    def _():
+        step(0, 0, blocks * BLOCK, BLOCK // 2)
 
 
 def tile_copies(hbm, vmem, rows, tiles, row_at, sems, first, out=False):
@@ -131,6 +144,18 @@
         copies.append(pltpu.make_async_copy(b, a, sems.at[first + t]) if out else
                       pltpu.make_async_copy(a, b, sems.at[first + t]))
     return copies
+
+
+def rim_kernel(own, below, right, corner, sems):
+    copies = [
+        pltpu.make_async_copy(own.at[:, pl.ds(0, PATCH), :], below, sems.at[0]),
+        pltpu.make_async_copy(own.at[:, :, pl.ds(0, PATCH)], right, sems.at[1]),
+        pltpu.make_async_copy(own.at[:, pl.ds(0, PATCH), pl.ds(0, PATCH)], corner, sems.at[2]),
+    ]
+    for c in copies:
+        c.start()
+    for c in copies:
+        c.wait()
 
 
 def inner_kernel(pos, count, own, photons, probe, plus_ref, minus_ref, grad_out, probe_out,
@@ -187,48 +212,78 @@
         c.wait()
 
 
+def seam_kernel(grad_in, above, left, corner, grad, top_buf, left_buf, above_buf, beside_buf, corner_buf, sems):
+    rows, cols = grad.shape[1], grad.shape[2]
+    rest = rows - PATCH
+    top_rim = grad.at[:, pl.ds(0, PATCH), :]
+    left_rim = grad.at[:, pl.ds(PATCH, rest), pl.ds(0, PATCH)]
+    loads = [
+        pltpu.make_async_copy(top_rim, top_buf, sems.at[0]),
+        pltpu.make_async_copy(left_rim, left_buf, sems.at[1]),
+        pltpu.make_async_copy(above, above_buf, sems.at[2]),
+        pltpu.make_async_copy(left, beside_buf, sems.at[3]),
+        pltpu.make_async_copy(corner, corner_buf, sems.at[4]),
+    ]
+    for c in loads:
+        c.start()
+    for c in loads:
+        c.wait()
+    top_buf[:, :, PATCH:] += above_buf[:, :, PATCH:]
+    top_buf[:, :, :PATCH] += above_buf[:, :, :PATCH] + (beside_buf[:, :PATCH, :] + corner_buf[...])
+    left_buf[...] += beside_buf[:, PATCH:, :]
+    stores = [
+        pltpu.make_async_copy(top_buf, top_rim, sems.at[0]),
+        pltpu.make_async_copy(left_buf, left_rim, sems.at[1]),
+    ]
+    for c in stores:
+        c.start()
+    for c in stores:
+        c.wait()
+
+
 def shape(*dims):
     return jax.ShapeDtypeStruct(dims, F32)
 
 
-def bit_exchange(value, bit):
-    size = lax.axis_size(BOTH)
-    return lax.ppermute(value, BOTH, [(i, i ^ bit) for i in range(size)])
-
-
-def total_over_devices(value):
-    me = lax.axis_index(BOTH)
-    x_low, x_high = (me // 16) % 2, (me // 32) % 2
-    halving = ((1, me % 2), (16, (x_low + x_high) % 2), (48, x_high))
-    whole = (4, 12, 2, 64, 128)
-    lows = []
-    for mask, label in halving:
-        half = value.shape[0] // 2
-        upper = label != 0
-        keep = jnp.where(upper, value[half:], value[:half])
-        send = jnp.where(upper, value[:half], value[half:])
-        value = keep + bit_exchange(send, mask)
-        lows.append(upper)
-    for mask in whole:
-        value = value + bit_exchange(value, mask)
-    for (mask, _), upper in zip(halving[::-1], lows[::-1]):
-        other = bit_exchange(value, mask)
-        value = jnp.concatenate([jnp.where(upper, other, value), jnp.where(upper, value, other)], axis=0)
-    return value
+def everyone(value, axes, count):
+    sent = jnp.broadcast_to(value[None], (count,) + value.shape)
+    return lax.all_to_all(sent, axes, 0, 0, tiled=True)
+
+
+def total_over_devices(value, halos):
+    core = lax.axis_index("core")
+    plane = lax.axis_size(PLANE)
+    depth = lax.axis_size(DEPTH)
+    swap = [(0, 1), (1, 0)]
+    half = value.shape[0] // 2
+    upper = core != 0
+    keep = jnp.where(upper, value[half:], value[:half])
+    send = jnp.where(upper, value[:half], value[half:])
+    value = keep + lax.ppermute(send, "core", swap)
+    shares = lax.all_to_all(value.reshape(plane, -1, PATCH), PLANE, 0, 0, tiled=True)
+    share = jnp.sum(shares, axis=0)
+    share, _ = lax.optimization_barrier((share, halos))
+    share = jnp.sum(everyone(share, DEPTH, depth), axis=0)
+    value = everyone(share, PLANE, plane).reshape(half, PATCH)
+    other = lax.ppermute(value, "core", swap)
+    return jnp.concatenate([jnp.where(upper, other, value), jnp.where(upper, value, other)], axis=0)
 
 
 def body(object_field, probe_modes, photons, positions, counts):
     rows, cols = object_field.shape[1], object_field.shape[2]
     slot_count = photons.shape[2]
     tiles = cols // PATCH
-    n_row, n_col = lax.axis_size("row"), lax.axis_size("col")
+    n_row, n_col = lax.axis_size(ROW), lax.axis_size(COL)
     plus_table, minus_table = fourier_tables(PATCH)
     pos = positions[0, 0].T
     count = counts[0]
     photon_rows = photons[0, 0]
-    right = lax.ppermute(object_field[:, :, :PATCH], "col", [(i, i - 1) for i in range(1, n_col)])
-    below = lax.ppermute(object_field[:, :PATCH, :], "row", [(i, i - 1) for i in range(1, n_row)])
-    corner = lax.ppermute(below[:, :, :PATCH], "col", [(i, i - 1) for i in range(1, n_col)])
+    down = [(i, i + 1) for i in range(n_row - 1)]
+    along = [(i, i + 1) for i in range(n_col - 1)]
+    diagonal = [
+        (a * n_col + b, (a + 1) * n_col + b + 1) for a in range(n_row - 1) for b in range(n_col - 1)
+    ]
+    up, back, diagonal_back = ([(j, i) for i, j in pairs] for pairs in (down, along, diagonal))
 
     smem = pl.BlockSpec(memory_space=pltpu.SMEM)
     vmem = pl.BlockSpec(memory_space=pltpu.VMEM)
@@ -244,8 +299,21 @@
         pltpu.VMEM((tiles + 1, 2, rows, PATCH), F32),
         pltpu.VMEM((tiles + 1, 2, rows, PATCH), F32),
     ] + scratch[2:]
-    params = pltpu.CompilerParams(vmem_limit_bytes=40 * 2**20)
-    work = 4 * 2 * 256 * 256 * 256 * slot_count // 2
+    params = pltpu.CompilerParams(vmem_limit_bytes=VMEM_LIMIT)
+    rims = (shape(2, PATCH, cols), shape(2, rows, PATCH), shape(2, PATCH, PATCH))
+    below, right, corner = pl.pallas_call(
+        rim_kernel,
+        out_shape=rims,
+        in_specs=[hbm],
+        out_specs=(hbm, hbm, hbm),
+        scratch_shapes=[pltpu.SemaphoreType.DMA((3,))],
+        compiler_params=params,
+        name="rims",
+    )(object_field)
+    below = lax.ppermute(below, ROW, up)
+    right = lax.ppermute(right, COL, back)
+    corner = lax.ppermute(corner, BOTH, diagonal_back)
+    work = 24 * 10**9
     cost = pl.CostEstimate(flops=work, bytes_accessed=8 * 2**20, transcendentals=0)
     grad_1, probe_1 = pl.pallas_call(
         inner_kernel,
@@ -272,29 +340,39 @@
     )(pos, count, object_field, right, below, corner, photon_rows, probe_modes, plus_table, minus_table,
       grad_1, probe_1)
 
-    down = [(i, i + 1) for i in range(n_row - 1)]
-    along = [(i, i + 1) for i in range(n_col - 1)]
-    diagonal = [
-        (a * n_col + b, (a + 1) * n_col + b + 1) for a in range(n_row - 1) for b in range(n_col - 1)
-    ]
-    from_above = lax.ppermute(g_below, "row", down)
-    from_left = lax.ppermute(g_right, "col", along)
+    from_above = lax.ppermute(g_below, ROW, down)
+    from_left = lax.ppermute(g_right, COL, along)
     from_corner = lax.ppermute(g_corner, BOTH, diagonal)
-    total_probe = total_over_devices(probe_2.reshape(-1, PATCH)).reshape(probe_modes.shape)
-    probe_gradient = total_probe / math.sqrt(n_row * n_col * slot_count)
-    object_gradient = g_own.at[:, :PATCH, :].add(from_above)
-    object_gradient = object_gradient.at[:, :, :PATCH].add(from_left)
-    object_gradient = object_gradient.at[:, :PATCH, :PATCH].add(from_corner)
+    total_probe = total_over_devices(probe_2.reshape(-1, PATCH), (from_above, from_left, from_corner))
+    probe_gradient = total_probe.reshape(probe_modes.shape) / math.sqrt(n_row * n_col * slot_count)
+    object_gradient = pl.pallas_call(
+        seam_kernel,
+        out_shape=shape(2, rows, cols),
+        in_specs=[hbm] * 4,
+        out_specs=hbm,
+        scratch_shapes=[
+            pltpu.VMEM((2, PATCH, cols), F32),
+            pltpu.VMEM((2, rows - PATCH, PATCH), F32),
+            pltpu.VMEM((2, PATCH, cols), F32),
+            pltpu.VMEM((2, rows, PATCH), F32),
+            pltpu.VMEM((2, PATCH, PATCH), F32),
+            pltpu.SemaphoreType.DMA((5,)),
+        ],
+        input_output_aliases={0: 0},
+        compiler_params=params,
+        name="seams",
+    )(g_own, from_above, from_left, from_corner)
     return (object_gradient, probe_gradient)
 
 
 def solution(mesh):
+    fine = Mesh(mesh.devices.reshape(4, 4, 4, 2, 2), BOTH)
     in_specs = (
-        P(None, "row", "col"),
+        P(None, ROW, COL),
         P(),
-        P("row", "col", None, None, None),
-        P("row", "col", None, None),
-        P("row", "col"),
+        P(ROW, COL, None, None, None),
+        P(ROW, COL, None, None),
+        P(ROW, COL),
     )
-    out_specs = (P(None, "row", "col"), P())
-    return jax.shard_map(body, mesh=mesh, in_specs=in_specs, out_specs=out_specs, check_vma=False)
+    out_specs = (P(None, ROW, COL), P())
+    return jax.shard_map(body, mesh=fine, in_specs=in_specs, out_specs=out_specs, check_vma=False)

time: 149 us -> 162 us (1.087)
  the two profiles are of different devices: /device:TPU:160 before, /device:TPU:1 now
where the time goes in v2:
time: 162 us; the launch traced here: 161 us
  Pallas kernels  55.5 us (34%)
  blocking collectives  46.3 us (29%)
  starting transfers between devices  28.7 us (18%)
  waiting for transfers between devices  26.1 us (16%)
  other arithmetic  1.78 us (1%)
    pallas_call x1, Pallas kernels, body(): pl.pallas_call(rim_kernel, out_shape=rims, in_specs=[hbm], out_specs=(hbm...  36.9 us
    all_to_all x2, blocking collectives, everyone(): return lax.all_to_all(sent, axes, 0, 0, tiled=True)  30.1 us
    ppermute x1, waiting for transfers between devices, body(): corner = lax.ppermute(corner, BOTH, diagonal_back)  26.1 us
    all_to_all x1, blocking collectives, total_over_devices(): lax.all_to_all(value.reshape(plane, -1, PATCH), PLANE, 0, 0, tiled=True)  16.2 us
    pallas_call x1, Pallas kernels, body(): pl.pallas_call(border_kernel, out_shape=(shape(2, rows, cols), shape(2, r...  9.18 us
    ppermute x1, starting transfers between devices, total_over_devices(): other = lax.ppermute(value, 'core', swap)  7.18 us
    ppermute x1, starting transfers between devices, body(): from_above = lax.ppermute(g_below, ROW, down)  7.15 us
    pallas_call x1, Pallas kernels, body(): pl.pallas_call(inner_kernel, out_shape=(shape(tiles, 2, rows, PATCH), sha...  6.91 us
  transfers between devices with their start and end apart: 8, of which 1 were waited for; matrix products, arithmetic and copies ran while one was open for 1% of the time, Pallas kernels for 6%

profile of v2, /device:TPU:1, one launch (start us, length us, event | category | flops | bytes accessed | tf_op | source)
XLA Modules:
  0.0 160.7 jit_solution(9187633882390732117)
XLA Ops:
  0.6 36.9 %rims.1 = (f32[2,128,512]{2,1,0:T(8,128)}, f32[2,512,128]{2,1,0:T(8,128)}, f32[2,128,128]{2,1,0:T(8,128)}) custom-call(f32[2,512,512]{2,1,0:T(8,128)} %own.5), custom_call_target="tpu_custom_call" | custom-call | tf_op jit(solution)/shard_map/rims/pallas_call | solution.py:304
  37.5 5.1 %collective-permute-start = (f32[2,512,128]{2,1,0:T(8,128)}, f32[2,512,128]{2,1,0:T(8,128)S(1)}, u32[]{:S(2)}, u32[]{:S(2)}) collective-permute-start(f32[2,512,128]{2,1,0:T(8,128)} %get-tuple-element.13), channel_id=1, source_target_pairs={{1,0},{2,1},{3,2},{4,3},{5,4},{6,5},{7,6},{8,7},{9,8},{10,9},{11,1... | collective-permute-start | bytes 1572872 | tf_op jit(solution)/shard_map/ppermute | solution.py:314
  42.7 1.3 collective-permute-start.1
  44.0 1.3 collective-permute-start.2
  45.9 6.9 %inner_slots.1 = (f32[4,2,512,128]{3,2,1,0:T(8,128)}, f32[2,2,128,128]{3,2,1,0:T(8,128)}) custom-call(s32[2,64]{1,0:T(2,128)} %bitcast.21, s32[1]{0:T(128)} %bitcast.13.count, f32[2,512,512]{2,1,0:T(8,128)} %own.5, bf16[64,128,128]{2,1,0:T(8,128)(2,1)} %bitcast.19, f32[2,2,128,128]{3,2,1,0:T(8,128)} %probe.3, bf16[256,256]{1,0:T(8,128)(2,1)} %constant.15.clone.plus_ref, ...), custom_call_target="tpu_custom_call" | custom-call | flops 24000000000 | bytes 8388608 | tf_op jit(solution)/shard_map/inner_slots/pallas_call | solution.py:318
  52.8 26.1 %collective-permute-done.2.corner = f32[2,128,128]{2,1,0:T(8,128)S(1)} collective-permute-done((f32[2,128,128]{2,1,0:T(8,128)}, f32[2,128,128]{2,1,0:T(8,128)S(1)}, u32[]{:S(2)}, u32[]{:S(2)}) %collective-permute-start.2) | collective-permute-done | bytes 131104 | tf_op jit(solution)/shard_map/ppermute | solution.py:315
  78.9 0.0 collective-permute-done.right
  78.9 0.0 collective-permute-done.1.below
  78.9 0.6 copy-done.4
  79.5 0.2 copy-done.3
  79.8 9.2 %border_slots.1 = (f32[2,512,512]{2,1,0:T(8,128)}, f32[2,512,128]{2,1,0:T(8,128)}, f32[2,128,512]{2,1,0:T(8,128)}, f32[2,128,128]{2,1,0:T(8,128)}, f32[2,2,128,128]{3,2,1,0:T(8,128)}) custom-call(s32[2,64]{1,0:T(2,128)} %bitcast.22, s32[1]{0:T(128)} %bitcast.14.count, f32[2,512,512]{2,1,0:T(8,128)} %own.5, f32[2,512,128]{2,1,0:T(8,128)} %copy-done.3, ...), custom_call_target="tpu_custom_call" | custom-call | flops 24000000000 | bytes 8388608 | tf_op jit(solution)/shard_map/border_slots/pallas_call | solution.py:328
  88.9 7.2 %collective-permute-start.3 = (f32[2,128,512]{2,1,0:T(8,128)}, f32[2,128,512]{2,1,0:T(8,128)S(1)}, u32[]{:S(2)}, u32[]{:S(2)}) collective-permute-start(f32[2,128,512]{2,1,0:T(8,128)} %get-tuple-element.19), channel_id=1, source_target_pairs={{0,64},{64,128},{128,192},{1,65},{65,129},{129,193},{2,66},{66,130... | collective-permute-start | bytes 1572872 | tf_op jit(solution)/shard_map/ppermute | solution.py:343
  96.1 1.9 %collective-permute-start.4 = (f32[2,512,128]{2,1,0:T(8,128)}, f32[2,512,128]{2,1,0:T(8,128)S(1)}, u32[]{:S(2)}, u32[]{:S(2)}) collective-permute-start(f32[2,512,128]{2,1,0:T(8,128)} %get-tuple-element.20), channel_id=1, source_target_pairs={{0,1},{1,2},{2,3},{3,4},{4,5},{5,6},{6,7},{7,8},{8,9},{9,10},{10,1... | collective-permute-start | bytes 1572872 | tf_op jit(solution)/shard_map/ppermute | solution.py:344
  98.0 1.0 slice_select_fusion.1
  99.0 0.6 collective-permute-start.6
  99.6 4.1 %collective-permute-start.5 = (f32[2,128,128]{2,1,0:T(8,128)}, f32[2,128,128]{2,1,0:T(8,128)S(1)}, u32[]{:S(2)}, u32[]{:S(2)}) collective-permute-start(f32[2,128,128]{2,1,0:T(8,128)} %get-tuple-element.21), channel_id=1, source_target_pairs={{0,65},{1,66},{2,67},{3,68},{4,69},{5,70},{6,71},{7,72},{8,73},{9,... | collective-permute-start | bytes 393224 | tf_op jit(solution)/shard_map/ppermute | solution.py:345
  103.7 0.0 collective-permute-done.6
  103.8 16.2 %all_to_all.15 = f32[16,16,128]{2,1,0:T(8,128)S(1)} all-to-all(f32[16,16,128]{2,1,0:T(8,128)S(1)} %bitcast.16), channel_id=1, replica_groups=mesh['z_hi'=4,'x'=4,'y'=4,'z_lo'=2,'core'=2] {'x','y'}, dimensions={0} | all-to-all | bytes 262144 | tf_op jit(solution)/shard_map/all_to_all | solution.py:263
  120.0 0.0 collective-permute-done.5.corner
  120.0 0.0 copy-start.2
  120.0 0.0 collective-permute-done.3.above
  120.0 0.0 copy-start
  120.0 0.0 collective-permute-done.4.left
  120.0 0.0 copy-start.1
  120.1 16.0 %all_to_all.16 = f32[8,16,128]{2,1,0:T(8,128)S(1)} all-to-all(f32[8,16,128]{2,1,0:T(8,128)S(1)} %broadcast_in_dim.4), channel_id=1, replica_groups=mesh['z_hi'=4,'x'=4,'y'=4,'z_lo'=2,'core'=2] {'z_hi','z_lo'}, dimensions={0} | all-to-all | bytes 131072 | tf_op jit(solution)/shard_map/all_to_all | solution.py:250
  136.1 14.1 %all_to_all.17 = f32[16,16,128]{2,1,0:T(8,128)S(1)} all-to-all(f32[16,16,128]{2,1,0:T(8,128)S(1)} %broadcast_in_dim.5), channel_id=1, replica_groups=mesh['z_hi'=4,'x'=4,'y'=4,'z_lo'=2,'core'=2] {'x','y'}, dimensions={0} | all-to-all | bytes 262144 | tf_op jit(solution)/shard_map/all_to_all | solution.py:250
  150.2 0.0 copy-done.1
  150.2 7.2 %collective-permute-start.7 = (f32[256,128]{1,0:T(8,128)S(1)}, f32[256,128]{1,0:T(8,128)S(1)}, u32[]{:S(2)}, u32[]{:S(2)}) collective-permute-start(f32[256,128]{1,0:T(8,128)S(1)} %bitcast.15), channel_id=1, source_target_pairs={{0,1},{1,0},{2,3},{3,2},{4,5},{5,4},{6,7},{7,6},{8,9},{9,8},{10,11... | collective-permute-start | bytes 393224 | tf_op jit(solution)/shard_map/ppermute | solution.py:268
  157.4 0.0 copy-done.2
  157.4 2.5 %seams.1 = f32[2,512,512]{2,1,0:T(8,128)} custom-call(f32[2,512,512]{2,1,0:T(8,128)} %get-tuple-element.18.grad_in, f32[2,128,512]{2,1,0:T(8,128)} %copy-done, f32[2,512,128]{2,1,0:T(8,128)} %copy-done.1, f32[2,128,128]{2,1,0:T(8,128)} %copy-done.2), custom_call_target="tpu_custom_call", output_to_operand_aliasing={{}: (0, {})} | custom-call | tf_op jit(solution)/shard_map/seams/pallas_call | solution.py:348
  159.9 0.0 collective-permute-done.7
  160.0 0.7 maximum_multiply_fusion
  (9 shorter events, 0.1 us)
Async XLA Ops:
  37.5 41.4 %collective-permute-start = (f32[2,512,128]{2,1,0:T(8,128)}, f32[2,512,128]{2,1,0:T(8,128)S(1)}, u32[]{:S(2)}, u32[]{:S(2)}) collective-permute-start(f32[2,512,128]{2,1,0:T(8,128)} %get-tuple-element.13), channel_id=1, source_target_pairs={{1,0},{2,1},{3,2},{4,3},{5,4},{6,5},{7,6},{8,7},{9,8},{10,9},{11,1... | collective-permute-start | bytes 1572872 | tf_op jit(solution)/shard_map/ppermute | solution.py:314
  42.7 36.2 %collective-permute-start.1 = (f32[2,128,512]{2,1,0:T(8,128)}, f32[2,128,512]{2,1,0:T(8,128)}, u32[]{:S(2)}, u32[]{:S(2)}) collective-permute-start(f32[2,128,512]{2,1,0:T(8,128)} %get-tuple-element.14), channel_id=1, source_target_pairs={{64,0},{128,64},{192,128},{65,1},{129,65},{193,129},{66,2},{130,66... | collective-permute-start | bytes 1572872 | tf_op jit(solution)/shard_map/ppermute | solution.py:313
  44.0 34.9 %collective-permute-start.2 = (f32[2,128,128]{2,1,0:T(8,128)}, f32[2,128,128]{2,1,0:T(8,128)S(1)}, u32[]{:S(2)}, u32[]{:S(2)}) collective-permute-start(f32[2,128,128]{2,1,0:T(8,128)} %get-tuple-element.15), channel_id=1, source_target_pairs={{65,0},{66,1},{67,2},{68,3},{69,4},{70,5},{71,6},{72,7},{73,8},{74... | collective-permute-start | bytes 393224 | tf_op jit(solution)/shard_map/ppermute | solution.py:315
  78.9 0.7 copy-start.4
  78.9 0.8 copy-start.3
  88.9 31.1 %collective-permute-start.3 = (f32[2,128,512]{2,1,0:T(8,128)}, f32[2,128,512]{2,1,0:T(8,128)S(1)}, u32[]{:S(2)}, u32[]{:S(2)}) collective-permute-start(f32[2,128,512]{2,1,0:T(8,128)} %get-tuple-element.19), channel_id=1, source_target_pairs={{0,64},{64,128},{128,192},{1,65},{65,129},{129,193},{2,66},{66,130... | collective-permute-start | bytes 1572872 | tf_op jit(solution)/shard_map/ppermute | solution.py:343
  96.1 23.9 %collective-permute-start.4 = (f32[2,512,128]{2,1,0:T(8,128)}, f32[2,512,128]{2,1,0:T(8,128)S(1)}, u32[]{:S(2)}, u32[]{:S(2)}) collective-permute-start(f32[2,512,128]{2,1,0:T(8,128)} %get-tuple-element.20), channel_id=1, source_target_pairs={{0,1},{1,2},{2,3},{3,4},{4,5},{5,6},{6,7},{7,8},{8,9},{9,10},{10,1... | collective-permute-start | bytes 1572872 | tf_op jit(solution)/shard_map/ppermute | solution.py:344
  99.0 4.7 %collective-permute-start.6 = (f32[256,128]{1,0:T(8,128)S(1)}, f32[256,128]{1,0:T(8,128)S(1)}, u32[]{:S(2)}, u32[]{:S(2)}) collective-permute-start(f32[256,128]{1,0:T(8,128)S(1)} %bitcast.18), channel_id=1, source_target_pairs={{0,1},{1,0},{2,3},{3,2},{4,5},{5,4},{6,7},{7,6},{8,9},{9,8},{10,11... | collective-permute-start | bytes 393224 | tf_op jit(solution)/shard_map/ppermute | solution.py:262
  99.6 20.3 %collective-permute-start.5 = (f32[2,128,128]{2,1,0:T(8,128)}, f32[2,128,128]{2,1,0:T(8,128)S(1)}, u32[]{:S(2)}, u32[]{:S(2)}) collective-permute-start(f32[2,128,128]{2,1,0:T(8,128)} %get-tuple-element.21), channel_id=1, source_target_pairs={{0,65},{1,66},{2,67},{3,68},{4,69},{5,70},{6,71},{7,72},{8,73},{9,... | collective-permute-start | bytes 393224 | tf_op jit(solution)/shard_map/ppermute | solution.py:345
  120.0 37.4 %copy-start.2 = (f32[2,128,128]{2,1,0:T(8,128)}, f32[2,128,128]{2,1,0:T(8,128)S(1)}, u32[]{:S(2)}) copy-start(f32[2,128,128]{2,1,0:T(8,128)S(1)} %collective-permute-done.5.corner) | copy-start | bytes 393220
  120.0 37.4 %copy-start = (f32[2,128,512]{2,1,0:T(8,128)}, f32[2,128,512]{2,1,0:T(8,128)S(1)}, u32[]{:S(2)}) copy-start(f32[2,128,512]{2,1,0:T(8,128)S(1)} %collective-permute-done.3.above) | copy-start | bytes 1572868
  120.0 30.2 %copy-start.1 = (f32[2,512,128]{2,1,0:T(8,128)}, f32[2,512,128]{2,1,0:T(8,128)S(1)}, u32[]{:S(2)}) copy-start(f32[2,512,128]{2,1,0:T(8,128)S(1)} %collective-permute-done.4.left) | copy-start | bytes 1572868
  150.2 9.7 %collective-permute-start.7 = (f32[256,128]{1,0:T(8,128)S(1)}, f32[256,128]{1,0:T(8,128)S(1)}, u32[]{:S(2)}, u32[]{:S(2)}) collective-permute-start(f32[256,128]{1,0:T(8,128)S(1)} %bitcast.15), channel_id=1, source_target_pairs={{0,1},{1,0},{2,3},{3,2},{4,5},{5,4},{6,7},{7,6},{8,9},{9,8},{10,11... | collective-permute-start | bytes 393224 | tf_op jit(solution)/shard_map/ppermute | solution.py:268

commit v3 on v2

v3 whole, which is shorter than its diff:
```python
import functools
import math

import jax
import jax.numpy as jnp
import numpy as np
from jax import lax
from jax.experimental import pallas as pl
from jax.experimental.pallas import tpu as pltpu
from jax.sharding import Mesh
from jax.sharding import PartitionSpec as P

F32 = jnp.float32
BF16 = jnp.bfloat16
PATCH = 128
BLOCK = 8
VMEM_LIMIT = 63 * 2**20
ROW = "z_hi"
COL = ("x", "y", "z_lo", "core")
BOTH = (ROW,) + COL
PLANE = ("x", "y")
DEPTH = ("z_hi", "z_lo")


def waves_of(patch_len):
    index_range = np.arange(patch_len)
    product = (index_range[:, None] * index_range[None, :]) % patch_len
    angle = product.astype(np.float32) * np.float32(2.0 * math.pi / patch_len)
    pair = np.stack([np.cos(angle), np.sin(angle)]) / np.float32(math.sqrt(patch_len))
    return jnp.asarray(pair, F32)


def dot(a, b):
    return jnp.dot(a, b, preferred_element_type=F32)


def slot_block(at, slots, valids, pos, row_base, field, grad, photons, probe, probe_sum, plus_ref, minus_ref):
    n = len(slots)
    lane = lax.broadcasted_iota(jnp.int32, (PATCH, PATCH), 1)
    plus = plus_ref[...]
    minus = minus_ref[...]
    places, patches, waves = [], [], []
    for s in slots:
        top = pos[0, s] - row_base
        left = pos[1, s]
        tile = left // PATCH
        shift = left % PATCH
        back = (PATCH - shift) % PATCH
        keep = lane >= shift
        patch = []
        for k in range(2):
            a = field[tile, k, pl.ds(top, PATCH), :]
            b = field[tile + 1, k, pl.ds(top, PATCH), :]
            patch.append(pltpu.roll(jnp.where(keep, a, b), back, 1))
        places.append((top, tile, shift, keep))
        patches.append(patch)
        for m in range(2):
            pr = probe[0, m]
            pi = probe[1, m]
            wr = (pr * patch[0] - pi * patch[1]).astype(BF16)
            wi = (pr * patch[1] + pi * patch[0]).astype(BF16)
            waves.append(jnp.concatenate([wr, wi], axis=0))
    first = dot(plus, jnp.concatenate(waves, axis=1)).astype(BF16)
    cols = [slice(q * PATCH, (q + 1) * PATCH) for q in range(2 * n)]
    turned = [jnp.concatenate([first[:PATCH, q], first[PATCH:, q]], axis=1) for q in cols]
    far = dot(jnp.concatenate(turned, axis=0), minus)
    scaled = []
    for i in range(n):
        f0 = far[2 * i * PATCH:(2 * i + 1) * PATCH]
        f1 = far[(2 * i + 1) * PATCH:(2 * i + 2) * PATCH]
        power = f0 * f0 + f1 * f1
        intensity = power[:, :PATCH] + power[:, PATCH:]
        factor = (1.0 - photons[at[i]].astype(F32) / (intensity + 1.0)) * valids[i]
        for f in (f0, f1):
            re = (f[:, :PATCH] * factor).astype(BF16)
            im = (f[:, PATCH:] * factor).astype(BF16)
            scaled.append(jnp.concatenate([re, im], axis=1))
    back_pass = dot(jnp.concatenate(scaled, axis=0), plus).astype(BF16)
    unturned = [jnp.concatenate([back_pass[q, :PATCH], back_pass[q, PATCH:]], axis=0) for q in cols]
    exit_grad = dot(minus, jnp.concatenate(unturned, axis=1))
    for m in range(2):
        sum_re = sum_im = None
        for i in range(n):
            er = exit_grad[:PATCH, cols[2 * i + m]]
            ei = exit_grad[PATCH:, cols[2 * i + m]]
            o_re, o_im = patches[i]
            t_re = o_re * er + o_im * ei
            t_im = o_re * ei - o_im * er
            sum_re = t_re if sum_re is None else sum_re + t_re
            sum_im = t_im if sum_im is None else sum_im + t_im
        probe_sum[0, m] += sum_re
        probe_sum[1, m] += sum_im
    for i in range(n):
        g_re = g_im = None
        for m in range(2):
            er = exit_grad[:PATCH, cols[2 * i + m]]
            ei = exit_grad[PATCH:, cols[2 * i + m]]
            pr = probe[0, m]
            pi = probe[1, m]
            t_re = pr * er + pi * ei
            t_im = pr * ei - pi * er
            g_re = t_re if g_re is None else g_re + t_re
            g_im = t_im if g_im is None else g_im + t_im
        top, tile, shift, keep = places[i]
        for k, g in ((0, g_re), (1, g_im)):
            g = pltpu.roll(g, shift, 1)
            grad[tile, k, pl.ds(top, PATCH), :] += jnp.where(keep, g, 0.0)
            grad[tile + 1, k, pl.ds(top, PATCH), :] += jnp.where(keep, 0.0, g)


def fill_tables(waves, plus_ref, minus_ref):
    c = waves[0].astype(BF16)
    s = waves[1].astype(BF16)
    plus_ref[:PATCH, :PATCH] = c
    plus_ref[:PATCH, PATCH:] = s
    plus_ref[PATCH:, :PATCH] = -s
    plus_ref[PATCH:, PATCH:] = c
    minus_ref[:PATCH, :PATCH] = c
    minus_ref[:PATCH, PATCH:] = -s
    minus_ref[PATCH:, :PATCH] = s
    minus_ref[PATCH:, PATCH:] = c


def list_slots(wanted, pos, count, listed, photons, photon_buf, photon_sems):
    def list_step(s, found):
        chosen = wanted(pos[0, s])

        @pl.when(chosen)
        def _():
            listed[found] = s
            pltpu.make_async_copy(photons.at[s], photon_buf.at[found], photon_sems.at[found]).start()

        return found + chosen.astype(jnp.int32)

    return lax.fori_loop(0, count, list_step, jnp.int32(0))


def run_slots(found, pos, row_base, listed, field, grad, photons, photon_buf, photon_sems, probe, probe_sum,
              plus_ref, minus_ref):
    def step(k, carry, first=0, width=BLOCK):
        places = [first + k * width + i for i in range(width)]
        at = [jnp.minimum(p, found - 1) for p in places]
        slots = [listed[a] for a in at]
        valids = [jnp.where(p < found, 1.0, 0.0).astype(F32) for p in places]
        for p, a, s in zip(places, at, slots):
            @pl.when(p < found)
            def _(a=a, s=s):
                pltpu.make_async_copy(photons.at[s], photon_buf.at[a], photon_sems.at[a]).wait()

        slot_block(at, slots, valids, pos, row_base, field, grad, photon_buf, probe, probe_sum, plus_ref, minus_ref)
        return carry

    rest = found % BLOCK
    small = (rest > 0) & (rest <= BLOCK // 2)
    blocks = found // BLOCK + ((rest > 0) & jnp.logical_not(small)).astype(jnp.int32)
    lax.fori_loop(0, blocks, step, 0)

    @pl.when(small)
    def _():
        step(0, 0, blocks * BLOCK, BLOCK // 2)


def copies_of(pairs, sems):
    return [pltpu.make_async_copy(a, b, sems.at[i]) for i, (a, b) in enumerate(pairs)]


def start_all(copies):
    for c in copies:
        c.start()


def wait_all(copies):
    for c in copies:
        c.wait()


def by_tiles(array, tiles):
    return [array.at[:, :, pl.ds(t * PATCH, PATCH)] for t in range(tiles)]


def rim_kernel(own, below, right, corner, below_buf, right_buf, sems):
    rim = pl.ds(0, PATCH)
    loads = copies_of([(own.at[:, rim, :], below_buf), (own.at[:, :, rim], right_buf)], sems)
    stores = copies_of(
        [(below_buf, below), (right_buf, right), (below_buf.at[:, :, rim], corner)], sems
    )
    start_all(loads)
    wait_all(loads)
    start_all(stores)
    wait_all(stores)


def upper_kernel(pos, count, own, right, photons, probe_in, waves_in, g_own, g_right, probe_out,
                 field, grad, photon_buf, probe, waves, plus_ref, minus_ref, probe_sum, listed, sems, photon_sems):
    rows, cols = own.shape[1], own.shape[2]
    tiles = cols // PATCH
    loads = copies_of(
        [(waves_in, waves), (probe_in, probe)]
        + [(a, field.at[t]) for t, a in enumerate(by_tiles(own, tiles))]
        + [(right, field.at[tiles])],
        sems,
    )
    start_all(loads)
    found = list_slots(lambda top: top <= rows - PATCH, pos, count[0], listed, photons, photon_buf, photon_sems)
    grad[...] = jnp.zeros(grad.shape, F32)
    probe_sum[...] = jnp.zeros(probe_sum.shape, F32)
    loads[0].wait()
    fill_tables(waves, plus_ref, minus_ref)
    wait_all(loads[1:])
    run_slots(found, pos, 0, listed, field, grad, photons, photon_buf, photon_sems, probe, probe_sum,
              plus_ref, minus_ref)
    stores = copies_of(
        [(probe_sum, probe_out)]
        + [(grad.at[t], a) for t, a in enumerate(by_tiles(g_own, tiles))]
        + [(grad.at[tiles], g_right)],
        sems,
    )
    start_all(stores)
    wait_all(stores)


def lower_kernel(scale, pos, count, own, right, below, corner, photons, probe_in, waves_in, own_in, right_in, sum_in,
                 g_own, g_right, g_below, probe_out,
                 field, grad, photon_buf, probe, waves, plus_ref, minus_ref, probe_sum, listed, sems, photon_sems):
    rows, cols = own.shape[1], own.shape[2]
    tiles = cols // PATCH
    base = rows - PATCH
    last, upper, lower = pl.ds(base, PATCH), pl.ds(0, PATCH), pl.ds(PATCH, PATCH)

    def last_rows(array):
        return [array.at[:, last, pl.ds(t * PATCH, PATCH)] for t in range(tiles)]

    loads = copies_of(
        [(waves_in, waves), (probe_in, probe), (sum_in, probe_sum)]
        + [(a, field.at[t, :, upper, :]) for t, a in enumerate(last_rows(own) + [right.at[:, last, :]])]
        + [(a, field.at[t, :, lower, :]) for t, a in enumerate(by_tiles(below, tiles) + [corner])]
        + [(a, grad.at[t, :, upper, :]) for t, a in enumerate(last_rows(own_in) + [right_in.at[:, last, :]])],
        sems,
    )
    start_all(loads)
    found = list_slots(lambda top: top > base, pos, count[0], listed, photons, photon_buf, photon_sems)
    for t in range(tiles + 1):
        grad[t, :, lower, :] = jnp.zeros((2, PATCH, PATCH), F32)
    loads[0].wait()
    fill_tables(waves, plus_ref, minus_ref)
    wait_all(loads[1:])
    run_slots(found, pos, base, listed, field, grad, photons, photon_buf, photon_sems, probe, probe_sum,
              plus_ref, minus_ref)
    probe_sum[...] = probe_sum[...] * scale
    stores = copies_of(
        [(probe_sum, probe_out)]
        + [(grad.at[t, :, lower, :], a) for t, a in enumerate(by_tiles(g_below, tiles + 1))]
        + [(grad.at[t, :, upper, :], a) for t, a in enumerate(last_rows(g_own) + [g_right.at[:, last, :]])],
        sems,
    )
    start_all(stores)
    wait_all(stores)


def seam_kernel(grad_in, above, left, grad, top_buf, left_buf, above_buf, beside_buf, sems):
    rows, cols = grad.shape[1], grad.shape[2]
    rest = rows - PATCH
    top_rim = grad.at[:, pl.ds(0, PATCH), :]
    left_rim = grad.at[:, pl.ds(PATCH, rest), pl.ds(0, PATCH)]
    loads = copies_of(
        [(top_rim, top_buf), (left_rim, left_buf), (above.at[:, :, pl.ds(0, cols)], above_buf), (left, beside_buf)],
        sems,
    )
    start_all(loads)
    wait_all(loads)
    top_buf[:, :, PATCH:] += above_buf[:, :, PATCH:]
    top_buf[:, :, :PATCH] += above_buf[:, :, :PATCH] + beside_buf[:, :PATCH, :]
    left_buf[...] += beside_buf[:, PATCH:, :]
    stores = copies_of([(top_buf, top_rim), (left_buf, left_rim)], sems)
    start_all(stores)
    wait_all(stores)


def shape(*dims):
    return jax.ShapeDtypeStruct(dims, F32)


def everyone(value, axes, count):
    sent = jnp.broadcast_to(value[None], (count,) + value.shape)
    return lax.all_to_all(sent, axes, 0, 0, tiled=True)


def body(object_field, probe_modes, photons, positions, counts):
    rows, cols = object_field.shape[1], object_field.shape[2]
    slot_count = photons.shape[2]
    tiles = cols // PATCH
    n_row, n_col = lax.axis_size(ROW), lax.axis_size(COL)
    pos = positions[0, 0].T
    count = counts[0]
    photon_rows = photons[0, 0]
    waves = waves_of(PATCH)
    scale = 1.0 / math.sqrt(n_row * n_col * slot_count)
    down = [(i, i + 1) for i in range(n_row - 1)]
    along = [(i, i + 1) for i in range(n_col - 1)]
    up, back = ([(j, i) for i, j in pairs] for pairs in (down, along))
    diagonal_back = [
        ((a + 1) * n_col + b + 1, a * n_col + b) for a in range(n_row - 1) for b in range(n_col - 1)
    ]
    smem = pl.BlockSpec(memory_space=pltpu.SMEM)
    hbm = pl.BlockSpec(memory_space=pl.ANY)
    params = pltpu.CompilerParams(vmem_limit_bytes=VMEM_LIMIT)

    below, right, corner = pl.pallas_call(
        rim_kernel,
        out_shape=(shape(2, PATCH, cols), shape(2, rows, PATCH), shape(2, PATCH, PATCH)),
        in_specs=[hbm],
        out_specs=(hbm,) * 3,
        scratch_shapes=[
            pltpu.VMEM((2, PATCH, cols), F32),
            pltpu.VMEM((2, rows, PATCH), F32),
            pltpu.SemaphoreType.DMA((3,)),
        ],
        compiler_params=params,
        name="rims",
    )(object_field)
    below = lax.ppermute(below, ROW, up)
    right = lax.ppermute(right, COL, back)
    corner = lax.ppermute(corner, BOTH, diagonal_back)

    def scratch(height):
        return [
            pltpu.VMEM((tiles + 1, 2, height, PATCH), F32),
            pltpu.VMEM((tiles + 1, 2, height, PATCH), F32),
            pltpu.VMEM(photon_rows.shape, BF16),
            pltpu.VMEM(probe_modes.shape, F32),
            pltpu.VMEM(waves.shape, F32),
            pltpu.VMEM((2 * PATCH, 2 * PATCH), BF16),
            pltpu.VMEM((2 * PATCH, 2 * PATCH), BF16),
            pltpu.VMEM(probe_modes.shape, F32),
            pltpu.SMEM((slot_count,), jnp.int32),
            pltpu.SemaphoreType.DMA((3 * tiles + 6,)),
            pltpu.SemaphoreType.DMA((slot_count,)),
        ]

    own_shape, right_shape, probe_shape = shape(2, rows, cols), shape(2, rows, PATCH), shape(*probe_modes.shape)
    g_own, g_right, probe_1 = pl.pallas_call(
        upper_kernel,
        out_shape=(own_shape, right_shape, probe_shape),
        in_specs=[smem, smem] + [hbm] * 5,
        out_specs=(hbm,) * 3,
        scratch_shapes=scratch(rows),
        compiler_params=params,
        cost_estimate=pl.CostEstimate(flops=24 * 10**9, bytes_accessed=8 * 2**20, transcendentals=0),
        name="upper_slots",
    )(pos, count, object_field, right, photon_rows, probe_modes, waves)
    g_own, g_right, g_below, probe_2 = pl.pallas_call(
        functools.partial(lower_kernel, scale),
        out_shape=(own_shape, right_shape, shape(2, PATCH, cols + PATCH), probe_shape),
        in_specs=[smem, smem] + [hbm] * 10,
        out_specs=(hbm,) * 4,
        scratch_shapes=scratch(2 * PATCH),
        input_output_aliases={9: 0, 10: 1},
        compiler_params=params,
        cost_estimate=pl.CostEstimate(flops=8 * 10**9, bytes_accessed=4 * 2**20, transcendentals=0),
        name="lower_slots",
    )(pos, count, object_field, right, below, corner, photon_rows, probe_modes, waves, g_own, g_right, probe_1)

    core, plane, depth = lax.axis_index("core"), lax.axis_size(PLANE), lax.axis_size(DEPTH)
    swap = [(0, 1), (1, 0)]
    above = lax.ppermute(g_below, ROW, down)
    value = probe_2.reshape(-1, PATCH)
    half = value.shape[0] // 2
    upper = core != 0
    keep = jnp.where(upper, value[half:], value[:half])
    send = jnp.where(upper, value[:half], value[half:])
    value = keep + lax.ppermute(send, "core", swap)
    shares = lax.all_to_all(value.reshape(plane, -1, PATCH), PLANE, 0, 0, tiled=True)
    share = jnp.sum(shares, axis=0)
    share, above = lax.optimization_barrier((share, above))
    g_right = g_right.at[:, :PATCH, :].add(above[:, :, cols:])
    left = lax.ppermute(g_right, COL, along)
    share = jnp.sum(everyone(share, DEPTH, depth), axis=0)
    value = everyone(share, PLANE, plane).reshape(half, PATCH)
    other = lax.ppermute(value, "core", swap)
    value = jnp.concatenate([jnp.where(upper, other, value), jnp.where(upper, value, other)], axis=0)
    probe_gradient = value.reshape(probe_modes.shape)

    object_gradient = pl.pallas_call(
        seam_kernel,
        out_shape=own_shape,
        in_specs=[hbm] * 3,
        out_specs=hbm,
        scratch_shapes=[
            pltpu.VMEM((2, PATCH, cols), F32),
            pltpu.VMEM((2, rows - PATCH, PATCH), F32),
            pltpu.VMEM((2, PATCH, cols), F32),
            pltpu.VMEM((2, rows, PATCH), F32),
            pltpu.SemaphoreType.DMA((4,)),
        ],
        input_output_aliases={0: 0},
        compiler_params=params,
        name="seams",
    )(g_own, above, left)
    return (object_gradient, probe_gradient)


def solution(mesh):
    fine = Mesh(mesh.devices.reshape(4, 4, 4, 2, 2), BOTH)
    in_specs = (
        P(None, ROW, COL),
        P(),
        P(ROW, COL, None, None, None),
        P(ROW, COL, None, None),
        P(ROW, COL),
    )
    out_specs = (P(None, ROW, COL), P())
    return jax.shard_map(body, mesh=fine, in_specs=in_specs, out_specs=out_specs, check_vma=False)
```

time: 162 us -> 123 us (0.76)
  the two profiles are of different devices: /device:TPU:1 before, /device:TPU:2 now
where the time goes in v3:
time: 123 us; the launch traced here: 124 us
  starting transfers between devices  43.6 us (35%)
  blocking collectives  37.2 us (30%)
  waiting for transfers between devices  20.5 us (17%)
  Pallas kernels  17.6 us (14%)
  other arithmetic  1.81 us (1%)
  local copies, waits for them, and re-layouts  1.48 us (1%)
  between operations  1.41 us (1%)
    all_to_all x1, blocking collectives, everyone(): return lax.all_to_all(sent, axes, 0, 0, tiled=True)  21.3 us
    all_to_all x1, blocking collectives, body(): lax.all_to_all(value.reshape(plane, -1, PATCH), PLANE, 0, 0, tiled=True)  15.9 us
    ppermute x1, starting transfers between devices, body(): above = lax.ppermute(g_below, ROW, down)  12.5 us
    ppermute x1, starting transfers between devices, body(): value = keep + lax.ppermute(send, 'core', swap)  11.3 us
    all_to_all x1, starting transfers between devices, everyone(): return lax.all_to_all(sent, axes, 0, 0, tiled=True)  9.58 us
    pallas_call x1, Pallas kernels, body(): pl.pallas_call(functools.partial(lower_kernel, scale), out_shape=(own_sha...  6.65 us
    pallas_call x1, Pallas kernels, body(): pl.pallas_call(upper_kernel, out_shape=(own_shape, right_shape, probe_sha...  6.26 us
    ppermute x1, starting transfers between devices, body(): right = lax.ppermute(right, COL, back)  5.69 us
  transfers between devices with their start and end apart: 8, of which 7 were waited for; matrix products, arithmetic and copies ran while one was open for 1% of the time, Pallas kernels for 5%

profile of v3, /device:TPU:2, one launch (start us, length us, event | category | flops | bytes accessed | tf_op | source)
XLA Modules:
  0.0 123.6 jit_solution(6435153183979369041)
XLA Ops:
  0.6 2.2 %rims.1 = (f32[2,128,512]{2,1,0:T(8,128)}, f32[2,512,128]{2,1,0:T(8,128)}, f32[2,128,128]{2,1,0:T(8,128)}) custom-call(f32[2,512,512]{2,1,0:T(8,128)} %own.5), custom_call_target="tpu_custom_call" | custom-call | tf_op jit(solution)/shard_map/rims/pallas_call | solution.py:308
  2.9 5.7 %collective-permute-start = (f32[2,512,128]{2,1,0:T(8,128)}, f32[2,512,128]{2,1,0:T(8,128)S(1)}, u32[]{:S(2)}, u32[]{:S(2)}) collective-permute-start(f32[2,512,128]{2,1,0:T(8,128)} %get-tuple-element.26), channel_id=1, source_target_pairs={{1,0},{2,1},{3,2},{4,3},{5,4},{6,5},{7,6},{8,7},{9,8},{10,9},{11,1... | collective-permute-start | bytes 1572872 | tf_op jit(solution)/shard_map/ppermute | solution.py:322
  8.6 1.3 %collective-permute-start.1 = (f32[2,128,512]{2,1,0:T(8,128)}, f32[2,128,512]{2,1,0:T(8,128)}, u32[]{:S(2)}, u32[]{:S(2)}) collective-permute-start(f32[2,128,512]{2,1,0:T(8,128)} %get-tuple-element.27), channel_id=1, source_target_pairs={{64,0},{128,64},{192,128},{65,1},{129,65},{193,129},{66,2},{130,66... | collective-permute-start | bytes 1572872 | tf_op jit(solution)/shard_map/ppermute | solution.py:321
  9.9 1.3 %collective-permute-start.2 = (f32[2,128,128]{2,1,0:T(8,128)}, f32[2,128,128]{2,1,0:T(8,128)S(1)}, u32[]{:S(2)}, u32[]{:S(2)}) collective-permute-start(f32[2,128,128]{2,1,0:T(8,128)} %get-tuple-element.28), channel_id=1, source_target_pairs={{65,0},{66,1},{67,2},{68,3},{69,4},{70,5},{71,6},{72,7},{73,8},{74... | collective-permute-start | bytes 393224 | tf_op jit(solution)/shard_map/ppermute | solution.py:323
  11.8 3.7 %collective-permute-done.right = f32[2,512,128]{2,1,0:T(8,128)S(1)} collective-permute-done((f32[2,512,128]{2,1,0:T(8,128)}, f32[2,512,128]{2,1,0:T(8,128)S(1)}, u32[]{:S(2)}, u32[]{:S(2)}) %collective-permute-start) | collective-permute-done | bytes 524320 | tf_op jit(solution)/shard_map/ppermute | solution.py:322
  15.5 0.0 copy-start.2
  15.5 0.8 copy-done.2
  16.3 6.3 %upper_slots.1 = (f32[2,512,512]{2,1,0:T(8,128)}, f32[2,512,128]{2,1,0:T(8,128)}, f32[2,2,128,128]{3,2,1,0:T(8,128)}) custom-call(s32[2,64]{1,0:T(2,128)} %bitcast.21, s32[1]{0:T(128)} %bitcast.13.count, f32[2,512,512]{2,1,0:T(8,128)} %own.5, f32[2,512,128]{2,1,0:T(8,128)} %copy-done.2, bf16[64,128,128]{2,1,0:T(8,128)(2,1)} %bitcast.19, ...), custom_call_target="tpu_custom_call" | custom-call | flops 24000000000 | bytes 8388608 | tf_op jit(solution)/shard_map/upper_slots/pallas_call | solution.py:341
  22.6 2.9 %collective-permute-done.2.corner = f32[2,128,128]{2,1,0:T(8,128)S(1)} collective-permute-done((f32[2,128,128]{2,1,0:T(8,128)}, f32[2,128,128]{2,1,0:T(8,128)S(1)}, u32[]{:S(2)}, u32[]{:S(2)}) %collective-permute-start.2) | collective-permute-done | bytes 131104 | tf_op jit(solution)/shard_map/ppermute | solution.py:323
  25.6 1.8 %collective-permute-done.1.below = f32[2,128,512]{2,1,0:T(8,128)} collective-permute-done((f32[2,128,512]{2,1,0:T(8,128)}, f32[2,128,512]{2,1,0:T(8,128)}, u32[]{:S(2)}, u32[]{:S(2)}) %collective-permute-start.1) | collective-permute-done | bytes 524320 | tf_op jit(solution)/shard_map/ppermute | solution.py:321
  27.4 0.0 copy-done.3
  27.4 6.7 %lower_slots.1 = (f32[2,512,512]{2,1,0:T(8,128)}, f32[2,512,128]{2,1,0:T(8,128)}, f32[2,128,640]{2,1,0:T(8,128)}, f32[2,2,128,128]{3,2,1,0:T(8,128)}) custom-call(s32[2,64]{1,0:T(2,128)} %bitcast.22, s32[1]{0:T(128)} %bitcast.14.count, f32[2,512,512]{2,1,0:T(8,128)} %own.5, f32[2,512,128]{2,1,0:T(8,128)} %copy-done.2, ...), custom_call_target="tpu_custom_call", output_to_operand_aliasing={{0}: (9, {}), {1}: (10, {})} | custom-call | flops 8000000000 | bytes 4194304 | tf_op jit(solution)/shard_map/lower_slots/pallas_call | solution.py:351
  34.1 0.0 copy-start.1
  34.1 12.5 %collective-permute-start.4 = (f32[2,128,640]{2,1,0:T(8,128)}, f32[2,128,640]{2,1,0:T(8,128)S(1)}, u32[]{:S(2)}, u32[]{:S(2)}) collective-permute-start(f32[2,128,640]{2,1,0:T(8,128)} %get-tuple-element.34), channel_id=1, source_target_pairs={{0,64},{64,128},{128,192},{1,65},{65,129},{129,193},{2,66},{66,130... | collective-permute-start | bytes 1966088 | tf_op jit(solution)/shard_map/ppermute | solution.py:365
  46.6 1.0 slice_select_fusion.1
  47.6 11.3 %collective-permute-start.3 = (f32[256,128]{1,0:T(8,128)S(1)}, f32[256,128]{1,0:T(8,128)S(1)}, u32[]{:S(2)}, u32[]{:S(2)}) collective-permute-start(f32[256,128]{1,0:T(8,128)S(1)} %bitcast.18), channel_id=1, source_target_pairs={{0,1},{1,0},{2,3},{3,2},{4,5},{5,4},{6,7},{7,6},{8,9},{9,8},{10,11... | collective-permute-start | bytes 393224 | tf_op jit(solution)/shard_map/ppermute | solution.py:371
  58.9 1.0 collective-permute-done.3
  59.9 15.9 %all_to_all.15 = f32[16,16,128]{2,1,0:T(8,128)S(1)} all-to-all(f32[16,16,128]{2,1,0:T(8,128)S(1)} %bitcast.16), channel_id=1, replica_groups=mesh['z_hi'=4,'x'=4,'y'=4,'z_lo'=2,'core'=2] {'x','y'}, dimensions={0} | all-to-all | bytes 262144 | tf_op jit(solution)/shard_map/all_to_all | solution.py:372
  75.8 0.0 collective-permute-done.4.above
  75.8 0.0 copy-start
  75.8 21.3 %all_to_all.16 = f32[8,16,128]{2,1,0:T(8,128)S(1)} all-to-all(f32[8,16,128]{2,1,0:T(8,128)S(1)} %broadcast_in_dim.4), channel_id=1, replica_groups=mesh['z_hi'=4,'x'=4,'y'=4,'z_lo'=2,'core'=2] {'z_hi','z_lo'}, dimensions={0} | all-to-all | bytes 131072 | tf_op jit(solution)/shard_map/all_to_all | solution.py:285
  97.1 0.7 broadcast_in_dim.5
  97.8 9.6 %all-to-all-start.2 = ((f32[16,16,128]{2,1,0:T(8,128)}), f32[16,16,128]{2,1,0:T(8,128)S(1)}, u32[]{:S(2)}, u32[]{:S(2)}) async-start(f32[16,16,128]{2,1,0:T(8,128)} %broadcast_in_dim.5), calls=%async_computation.2 | async-start | bytes 262144 | tf_op jit(solution)/shard_map/all_to_all | solution.py:285
  107.4 0.0 copy-done.1
  107.4 1.9 %collective-permute-start.5 = (f32[2,512,128]{2,1,0:T(8,128)S(1)}, f32[2,512,128]{2,1,0:T(8,128)}, u32[]{:S(2)}, u32[]{:S(2)}) collective-permute-start(f32[2,512,128]{2,1,0:T(8,128)S(1)} %add_dynamic-update-slice_fusion), channel_id=1, source_target_pairs={{0,1},{1,2},{2,3},{3,4},{4,5},{5,6},{6,7},{7,8},{8,9},{9,10},{10,1... | collective-permute-start | bytes 1572872 | tf_op jit(solution)/shard_map/ppermute | solution.py:376
  109.4 4.4 %all-to-all-done.2 = f32[16,16,128]{2,1,0:T(8,128)S(1)} async-done(((f32[16,16,128]{2,1,0:T(8,128)}), f32[16,16,128]{2,1,0:T(8,128)S(1)}, u32[]{:S(2)}, u32[]{:S(2)}) %all-to-all-start.2) | async-done | bytes 131104 | tf_op jit(solution)/shard_map/all_to_all | solution.py:285
  113.8 0.0 collective-permute-start.6
  113.8 1.3 %collective-permute-done.6 = f32[256,128]{1,0:T(8,128)S(1)} collective-permute-done((f32[256,128]{1,0:T(8,128)S(1)}, f32[256,128]{1,0:T(8,128)S(1)}, u32[]{:S(2)}, u32[]{:S(2)}) %collective-permute-start.6) | collective-permute-done | bytes 131104 | tf_op jit(solution)/shard_map/ppermute | solution.py:379
  115.2 0.7 pad_maximum_fusion
  115.9 5.2 %collective-permute-done.5.left = f32[2,512,128]{2,1,0:T(8,128)} collective-permute-done((f32[2,512,128]{2,1,0:T(8,128)S(1)}, f32[2,512,128]{2,1,0:T(8,128)}, u32[]{:S(2)}, u32[]{:S(2)}) %collective-permute-start.5) | collective-permute-done | bytes 524320 | tf_op jit(solution)/shard_map/ppermute | solution.py:376
  121.1 0.0 copy-done
  121.1 2.5 %seams.1 = f32[2,512,512]{2,1,0:T(8,128)} custom-call(f32[2,512,512]{2,1,0:T(8,128)} %get-tuple-element.32.grad_in, f32[2,128,640]{2,1,0:T(8,128)} %copy-done, f32[2,512,128]{2,1,0:T(8,128)} %collective-permute-done.5.left), custom_call_target="tpu_custom_call", output_to_operand_aliasing={{}: (0, {})} | custom-call | tf_op jit(solution)/shard_map/seams/pallas_call | solution.py:383
  (7 shorter events, 0.1 us)
Async XLA Ops:
  2.9 12.7 %collective-permute-start = (f32[2,512,128]{2,1,0:T(8,128)}, f32[2,512,128]{2,1,0:T(8,128)S(1)}, u32[]{:S(2)}, u32[]{:S(2)}) collective-permute-start(f32[2,512,128]{2,1,0:T(8,128)} %get-tuple-element.26), channel_id=1, source_target_pairs={{1,0},{2,1},{3,2},{4,3},{5,4},{6,5},{7,6},{8,7},{9,8},{10,9},{11,1... | collective-permute-start | bytes 1572872 | tf_op jit(solution)/shard_map/ppermute | solution.py:322
  8.6 18.8 %collective-permute-start.1 = (f32[2,128,512]{2,1,0:T(8,128)}, f32[2,128,512]{2,1,0:T(8,128)}, u32[]{:S(2)}, u32[]{:S(2)}) collective-permute-start(f32[2,128,512]{2,1,0:T(8,128)} %get-tuple-element.27), channel_id=1, source_target_pairs={{64,0},{128,64},{192,128},{65,1},{129,65},{193,129},{66,2},{130,66... | collective-permute-start | bytes 1572872 | tf_op jit(solution)/shard_map/ppermute | solution.py:321
  9.9 15.7 %collective-permute-start.2 = (f32[2,128,128]{2,1,0:T(8,128)}, f32[2,128,128]{2,1,0:T(8,128)S(1)}, u32[]{:S(2)}, u32[]{:S(2)}) collective-permute-start(f32[2,128,128]{2,1,0:T(8,128)} %get-tuple-element.28), channel_id=1, source_target_pairs={{65,0},{66,1},{67,2},{68,3},{69,4},{70,5},{71,6},{72,7},{73,8},{74... | collective-permute-start | bytes 393224 | tf_op jit(solution)/shard_map/ppermute | solution.py:323
  15.5 0.8 copy-start.2
  25.6 1.9 %copy-start.3 = (f32[2,128,128]{2,1,0:T(8,128)}, f32[2,128,128]{2,1,0:T(8,128)S(1)}, u32[]{:S(2)}) copy-start(f32[2,128,128]{2,1,0:T(8,128)S(1)} %collective-permute-done.2.corner) | copy-start | bytes 393220
  34.1 73.3 %copy-start.1 = (f32[2,512,128]{2,1,0:T(8,128)S(1)}, f32[2,512,128]{2,1,0:T(8,128)}, u32[]{:S(2)}) copy-start(f32[2,512,128]{2,1,0:T(8,128)} %get-tuple-element.36) | copy-start | bytes 1572868
  34.1 41.7 %collective-permute-start.4 = (f32[2,128,640]{2,1,0:T(8,128)}, f32[2,128,640]{2,1,0:T(8,128)S(1)}, u32[]{:S(2)}, u32[]{:S(2)}) collective-permute-start(f32[2,128,640]{2,1,0:T(8,128)} %get-tuple-element.34), channel_id=1, source_target_pairs={{0,64},{64,128},{128,192},{1,65},{65,129},{129,193},{2,66},{66,130... | collective-permute-start | bytes 1966088 | tf_op jit(solution)/shard_map/ppermute | solution.py:365
  47.6 12.3 %collective-permute-start.3 = (f32[256,128]{1,0:T(8,128)S(1)}, f32[256,128]{1,0:T(8,128)S(1)}, u32[]{:S(2)}, u32[]{:S(2)}) collective-permute-start(f32[256,128]{1,0:T(8,128)S(1)} %bitcast.18), channel_id=1, source_target_pairs={{0,1},{1,0},{2,3},{3,2},{4,5},{5,4},{6,7},{7,6},{8,9},{9,8},{10,11... | collective-permute-start | bytes 393224 | tf_op jit(solution)/shard_map/ppermute | solution.py:371
  75.8 45.2 %copy-start = (f32[2,128,640]{2,1,0:T(8,128)}, f32[2,128,640]{2,1,0:T(8,128)S(1)}, u32[]{:S(2)}) copy-start(f32[2,128,640]{2,1,0:T(8,128)S(1)} %collective-permute-done.4.above) | copy-start | bytes 1966084
  97.8 16.0 %all-to-all-start.2 = ((f32[16,16,128]{2,1,0:T(8,128)}), f32[16,16,128]{2,1,0:T(8,128)S(1)}, u32[]{:S(2)}, u32[]{:S(2)}) async-start(f32[16,16,128]{2,1,0:T(8,128)} %broadcast_in_dim.5), calls=%async_computation.2 | async-start | bytes 262144 | tf_op jit(solution)/shard_map/all_to_all | solution.py:285
  107.4 13.6 %collective-permute-start.5 = (f32[2,512,128]{2,1,0:T(8,128)S(1)}, f32[2,512,128]{2,1,0:T(8,128)}, u32[]{:S(2)}, u32[]{:S(2)}) collective-permute-start(f32[2,512,128]{2,1,0:T(8,128)S(1)} %add_dynamic-update-slice_fusion), channel_id=1, source_target_pairs={{0,1},{1,2},{2,3},{3,4},{4,5},{5,6},{6,7},{7,8},{8,9},{9,10},{10,1... | collective-permute-start | bytes 1572872 | tf_op jit(solution)/shard_map/ppermute | solution.py:376
  113.8 1.3 %collective-permute-start.6 = (f32[256,128]{1,0:T(8,128)S(1)}, f32[256,128]{1,0:T(8,128)S(1)}, u32[]{:S(2)}, u32[]{:S(2)}) collective-permute-start(f32[256,128]{1,0:T(8,128)S(1)} %bitcast.15), channel_id=1, source_target_pairs={{0,1},{1,0},{2,3},{3,2},{4,5},{5,4},{6,7},{7,6},{8,9},{9,8},{10,11... | collective-permute-start | bytes 393224 | tf_op jit(solution)/shard_map/ppermute | solution.py:379

commit v4 on v3

--- a/solution.py
+++ b/solution.py
@@ -219,8 +219,8 @@
     wait_all(stores)
 
 
-def lower_kernel(scale, pos, count, own, right, below, corner, photons, probe_in, waves_in, own_in, right_in, sum_in,
-                 g_own, g_right, g_below, probe_out,
+def lower_kernel(scale, pos, count, core, own, right, below, corner, photons, probe_in, waves_in, own_in, right_in, sum_in,
+                 g_own, g_right, g_below, g_corner, kept, sent,
                  field, grad, photon_buf, probe, waves, plus_ref, minus_ref, probe_sum, listed, sems, photon_sems):
     rows, cols = own.shape[1], own.shape[2]
     tiles = cols // PATCH
@@ -248,8 +248,8 @@
               plus_ref, minus_ref)
     probe_sum[...] = probe_sum[...] * scale
     stores = copies_of(
-        [(probe_sum, probe_out)]
-        + [(grad.at[t, :, lower, :], a) for t, a in enumerate(by_tiles(g_below, tiles + 1))]
+        [(probe_sum.at[core[0]], kept), (probe_sum.at[1 - core[0]], sent)]
+        + [(grad.at[t, :, lower, :], a) for t, a in enumerate(by_tiles(g_below, tiles) + [g_corner])]
         + [(grad.at[t, :, upper, :], a) for t, a in enumerate(last_rows(g_own) + [g_right.at[:, last, :]])],
         sems,
     )
@@ -257,23 +257,28 @@
     wait_all(stores)
 
 
-def seam_kernel(grad_in, above, left, grad, top_buf, left_buf, above_buf, beside_buf, sems):
+def seam_kernel(core, grad_in, above, left, corner, value, other, grad, probe,
+                top_buf, left_buf, above_buf, beside_buf, corner_buf, probe_buf, sems):
     rows, cols = grad.shape[1], grad.shape[2]
     rest = rows - PATCH
     top_rim = grad.at[:, pl.ds(0, PATCH), :]
     left_rim = grad.at[:, pl.ds(PATCH, rest), pl.ds(0, PATCH)]
     loads = copies_of(
-        [(top_rim, top_buf), (left_rim, left_buf), (above.at[:, :, pl.ds(0, cols)], above_buf), (left, beside_buf)],
+        [(top_rim, top_buf), (left_rim, left_buf), (above, above_buf), (left, beside_buf), (corner, corner_buf),
+         (value, probe_buf.at[core[0]]), (other, probe_buf.at[1 - core[0]])],
         sems,
     )
     start_all(loads)
     wait_all(loads)
+    join = pltpu.make_async_copy(probe_buf, probe, sems.at[2])
+    join.start()
     top_buf[:, :, PATCH:] += above_buf[:, :, PATCH:]
-    top_buf[:, :, :PATCH] += above_buf[:, :, :PATCH] + beside_buf[:, :PATCH, :]
+    top_buf[:, :, :PATCH] += above_buf[:, :, :PATCH] + (beside_buf[:, :PATCH, :] + corner_buf[...])
     left_buf[...] += beside_buf[:, PATCH:, :]
     stores = copies_of([(top_buf, top_rim), (left_buf, left_rim)], sems)
     start_all(stores)
     wait_all(stores)
+    join.wait()
 
 
 def shape(*dims):
@@ -298,16 +303,19 @@
     down = [(i, i + 1) for i in range(n_row - 1)]
     along = [(i, i + 1) for i in range(n_col - 1)]
     up, back = ([(j, i) for i, j in pairs] for pairs in (down, along))
-    diagonal_back = [
-        ((a + 1) * n_col + b + 1, a * n_col + b) for a in range(n_row - 1) for b in range(n_col - 1)
+    diagonal = [
+        (a * n_col + b, (a + 1) * n_col + b + 1) for a in range(n_row - 1) for b in range(n_col - 1)
     ]
+    diagonal_back = [(j, i) for i, j in diagonal]
+    core = lax.axis_index("core")[None]
     smem = pl.BlockSpec(memory_space=pltpu.SMEM)
     hbm = pl.BlockSpec(memory_space=pl.ANY)
     params = pltpu.CompilerParams(vmem_limit_bytes=VMEM_LIMIT)
 
+    rim_shape = shape(2, PATCH, PATCH)
     below, right, corner = pl.pallas_call(
         rim_kernel,
-        out_shape=(shape(2, PATCH, cols), shape(2, rows, PATCH), shape(2, PATCH, PATCH)),
+        out_shape=(shape(2, PATCH, cols), shape(2, rows, PATCH), rim_shape),
         in_specs=[hbm],
         out_specs=(hbm,) * 3,
         scratch_shapes=[
@@ -348,54 +356,50 @@
         cost_estimate=pl.CostEstimate(flops=24 * 10**9, bytes_accessed=8 * 2**20, transcendentals=0),
         name="upper_slots",
     )(pos, count, object_field, right, photon_rows, probe_modes, waves)
-    g_own, g_right, g_below, probe_2 = pl.pallas_call(
+    g_own, g_right, g_below, g_corner, kept, sent = pl.pallas_call(
         functools.partial(lower_kernel, scale),
-        out_shape=(own_shape, right_shape, shape(2, PATCH, cols + PATCH), probe_shape),
-        in_specs=[smem, smem] + [hbm] * 10,
-        out_specs=(hbm,) * 4,
+        out_shape=(own_shape, right_shape, shape(2, PATCH, cols), rim_shape, rim_shape, rim_shape),
+        in_specs=[smem] * 3 + [hbm] * 10,
+        out_specs=(hbm,) * 6,
         scratch_shapes=scratch(2 * PATCH),
-        input_output_aliases={9: 0, 10: 1},
+        input_output_aliases={10: 0, 11: 1},
         compiler_params=params,
         cost_estimate=pl.CostEstimate(flops=8 * 10**9, bytes_accessed=4 * 2**20, transcendentals=0),
         name="lower_slots",
-    )(pos, count, object_field, right, below, corner, photon_rows, probe_modes, waves, g_own, g_right, probe_1)
-
-    core, plane, depth = lax.axis_index("core"), lax.axis_size(PLANE), lax.axis_size(DEPTH)
+    )(pos, count, core, object_field, right, below, corner, photon_rows, probe_modes, waves, g_own, g_right, probe_1)
+
+    plane, depth = lax.axis_size(PLANE), lax.axis_size(DEPTH)
     swap = [(0, 1), (1, 0)]
     above = lax.ppermute(g_below, ROW, down)
-    value = probe_2.reshape(-1, PATCH)
-    half = value.shape[0] // 2
-    upper = core != 0
-    keep = jnp.where(upper, value[half:], value[:half])
-    send = jnp.where(upper, value[:half], value[half:])
-    value = keep + lax.ppermute(send, "core", swap)
+    value = kept + lax.ppermute(sent, "core", swap)
     shares = lax.all_to_all(value.reshape(plane, -1, PATCH), PLANE, 0, 0, tiled=True)
     share = jnp.sum(shares, axis=0)
+    share, g_right, g_corner = lax.optimization_barrier((share, g_right, g_corner))
+    left = lax.ppermute(g_right, COL, along)
+    from_corner = lax.ppermute(g_corner, BOTH, diagonal)
+    share = jnp.sum(everyone(share, DEPTH, depth), axis=0)
     share, above = lax.optimization_barrier((share, above))
-    g_right = g_right.at[:, :PATCH, :].add(above[:, :, cols:])
-    left = lax.ppermute(g_right, COL, along)
-    share = jnp.sum(everyone(share, DEPTH, depth), axis=0)
-    value = everyone(share, PLANE, plane).reshape(half, PATCH)
+    value = everyone(share, PLANE, plane).reshape(kept.shape)
     other = lax.ppermute(value, "core", swap)
-    value = jnp.concatenate([jnp.where(upper, other, value), jnp.where(upper, value, other)], axis=0)
-    probe_gradient = value.reshape(probe_modes.shape)
-
-    object_gradient = pl.pallas_call(
+
+    object_gradient, probe_gradient = pl.pallas_call(
         seam_kernel,
-        out_shape=own_shape,
-        in_specs=[hbm] * 3,
-        out_specs=hbm,
+        out_shape=(own_shape, probe_shape),
+        in_specs=[smem] + [hbm] * 6,
+        out_specs=(hbm, hbm),
         scratch_shapes=[
             pltpu.VMEM((2, PATCH, cols), F32),
             pltpu.VMEM((2, rows - PATCH, PATCH), F32),
             pltpu.VMEM((2, PATCH, cols), F32),
             pltpu.VMEM((2, rows, PATCH), F32),
-            pltpu.SemaphoreType.DMA((4,)),
+            pltpu.VMEM((2, PATCH, PATCH), F32),
+            pltpu.VMEM(probe_modes.shape, F32),
+            pltpu.SemaphoreType.DMA((7,)),
         ],
-        input_output_aliases={0: 0},
-        compiler_params=params,
+        input_output_aliases={1: 0},
+        compiler_params=pltpu.CompilerParams(vmem_limit_bytes=8 * 2**20),
         name="seams",
-    )(g_own, above, left)
+    )(core, g_own, above, left, from_corner, value, other)
     return (object_gradient, probe_gradient)
 
 

time: 123 us -> 109 us (0.89)
  the two profiles are of different devices: /device:TPU:2 before, /device:TPU:1 now
where the time goes in v4:
time: 109 us
  starting transfers between devices  38.4 us (35%)
  blocking collectives  25.5 us (23%)
  waiting for transfers between devices  23.5 us (22%)
  Pallas kernels  17.3 us (16%)
  local copies, waits for them, and re-layouts  2.1 us (2%)
  between operations  1.41 us (1%)
    all_to_all x1, blocking collectives, body(): lax.all_to_all(value.reshape(plane, -1, PATCH), PLANE, 0, 0, tiled=True)  14.9 us
    ppermute x1, waiting for transfers between devices, body(): right = lax.ppermute(right, COL, back)  13.1 us
    all_to_all x1, blocking collectives, everyone(): return lax.all_to_all(sent, axes, 0, 0, tiled=True)  10.6 us
    ppermute x1, starting transfers between devices, body(): left = lax.ppermute(g_right, COL, along)  10.1 us
    ppermute x1, starting transfers between devices, body(): above = lax.ppermute(g_below, ROW, down)  9.87 us
    all_to_all x1, starting transfers between devices, everyone(): return lax.all_to_all(sent, axes, 0, 0, tiled=True)  9.37 us
    pallas_call x1, Pallas kernels, body(): pl.pallas_call(upper_kernel, out_shape=(own_shape, right_shape, probe_sha...  7.21 us
    pallas_call x1, Pallas kernels, body(): pl.pallas_call(functools.partial(lower_kernel, scale), out_shape=(own_sha...  5.63 us
  transfers between devices with their start and end apart: 9, of which 4 were waited for; matrix products, arithmetic and copies ran while one was open for 1% of the time, Pallas kernels for 7%

profile of v4, /device:TPU:1, one launch (start us, length us, event | category | flops | bytes accessed | tf_op | source)
XLA Modules:
  0.0 109.2 jit_solution(9305018940214420054)
XLA Ops:
  0.6 2.2 %rims.1 = (f32[2,128,512]{2,1,0:T(8,128)}, f32[2,512,128]{2,1,0:T(8,128)}, f32[2,128,128]{2,1,0:T(8,128)}) custom-call(f32[2,512,512]{2,1,0:T(8,128)} %own.5), custom_call_target="tpu_custom_call" | custom-call | tf_op jit(solution)/shard_map/rims/pallas_call | solution.py:316
  2.9 5.1 %collective-permute-start = (f32[2,512,128]{2,1,0:T(8,128)}, f32[2,512,128]{2,1,0:T(8,128)S(1)}, u32[]{:S(2)}, u32[]{:S(2)}) collective-permute-start(f32[2,512,128]{2,1,0:T(8,128)} %get-tuple-element.19), channel_id=1, source_target_pairs={{1,0},{2,1},{3,2},{4,3},{5,4},{6,5},{7,6},{8,7},{9,8},{10,9},{11,1... | collective-permute-start | bytes 1572872 | tf_op jit(solution)/shard_map/ppermute | solution.py:330
  8.0 1.3 %collective-permute-start.2 = (f32[2,128,128]{2,1,0:T(8,128)}, f32[2,128,128]{2,1,0:T(8,128)S(1)}, u32[]{:S(2)}, u32[]{:S(2)}) collective-permute-start(f32[2,128,128]{2,1,0:T(8,128)} %get-tuple-element.21), channel_id=1, source_target_pairs={{65,0},{66,1},{67,2},{68,3},{69,4},{70,5},{71,6},{72,7},{73,8},{74... | collective-permute-start | bytes 393224 | tf_op jit(solution)/shard_map/ppermute | solution.py:331
  9.3 1.3 %collective-permute-start.1 = (f32[2,128,512]{2,1,0:T(8,128)}, f32[2,128,512]{2,1,0:T(8,128)}, u32[]{:S(2)}, u32[]{:S(2)}) collective-permute-start(f32[2,128,512]{2,1,0:T(8,128)} %get-tuple-element.20), channel_id=1, source_target_pairs={{64,0},{128,64},{192,128},{65,1},{129,65},{193,129},{66,2},{130,66... | collective-permute-start | bytes 1572872 | tf_op jit(solution)/shard_map/ppermute | solution.py:329
  11.3 13.1 %collective-permute-done.right = f32[2,512,128]{2,1,0:T(8,128)S(1)} collective-permute-done((f32[2,512,128]{2,1,0:T(8,128)}, f32[2,512,128]{2,1,0:T(8,128)S(1)}, u32[]{:S(2)}, u32[]{:S(2)}) %collective-permute-start) | collective-permute-done | bytes 524320 | tf_op jit(solution)/shard_map/ppermute | solution.py:330
  24.3 0.0 copy-start
  24.4 0.8 copy-done
  25.1 7.2 %upper_slots.1 = (f32[2,512,512]{2,1,0:T(8,128)}, f32[2,512,128]{2,1,0:T(8,128)}, f32[2,2,128,128]{3,2,1,0:T(8,128)}) custom-call(s32[2,64]{1,0:T(2,128)} %bitcast.15, s32[1]{0:T(128)} %bitcast.8.count, f32[2,512,512]{2,1,0:T(8,128)} %own.5, f32[2,512,128]{2,1,0:T(8,128)} %copy-done, bf16[64,128,128]{2,1,0:T(8,128)(2,1)} %bitcast.13, ...), custom_call_target="tpu_custom_call" | custom-call | flops 24000000000 | bytes 8388608 | tf_op jit(solution)/shard_map/upper_slots/pallas_call | solution.py:349
  32.3 3.6 %collective-permute-done.2.corner = f32[2,128,128]{2,1,0:T(8,128)S(1)} collective-permute-done((f32[2,128,128]{2,1,0:T(8,128)}, f32[2,128,128]{2,1,0:T(8,128)S(1)}, u32[]{:S(2)}, u32[]{:S(2)}) %collective-permute-start.2) | collective-permute-done | bytes 131104 | tf_op jit(solution)/shard_map/ppermute | solution.py:331
  36.0 0.0 copy-start.1
  36.0 0.0 collective-permute-done.1.below
  36.0 0.6 copy-done.1
  36.6 5.6 %lower_slots.1 = (f32[2,512,512]{2,1,0:T(8,128)}, f32[2,512,128]{2,1,0:T(8,128)}, f32[2,128,512]{2,1,0:T(8,128)}, f32[2,128,128]{2,1,0:T(8,128)}, f32[2,128,128]{2,1,0:T(8,128)}, /*index=5*/f32[2,128,128]{2,1,0:T(8,128)}) custom-call(s32[2,64]{1,0:T(2,128)} %bitcast.16, s32[1]{0:T(128)} %bitcast.9.count, ...), custom_call_target="tpu_custom_call", output_to_operand_aliasing={{0}: (10, {}), {1}: (11, {})} | custom-call | flops 8000000000 | bytes 4194304 | tf_op jit(solution)/shard_map/lower_slots/pallas_call | solution.py:359
  42.3 0.1 collective-permute-start.3
  42.4 9.9 %collective-permute-start.4 = (f32[2,128,512]{2,1,0:T(8,128)}, f32[2,128,512]{2,1,0:T(8,128)S(1)}, u32[]{:S(2)}, u32[]{:S(2)}) collective-permute-start(f32[2,128,512]{2,1,0:T(8,128)} %get-tuple-element.31), channel_id=1, source_target_pairs={{0,64},{64,128},{128,192},{1,65},{65,129},{129,193},{2,66},{66,130... | collective-permute-start | bytes 1572872 | tf_op jit(solution)/shard_map/ppermute | solution.py:373
  52.3 0.0 collective-permute-done.3
  52.3 0.9 add.3
  53.2 14.9 %all_to_all.15 = f32[16,16,128]{2,1,0:T(8,128)S(1)} all-to-all(f32[16,16,128]{2,1,0:T(8,128)S(1)} %bitcast.12), channel_id=1, replica_groups=mesh['z_hi'=4,'x'=4,'y'=4,'z_lo'=2,'core'=2] {'x','y'}, dimensions={0} | all-to-all | bytes 262144 | tf_op jit(solution)/shard_map/all_to_all | solution.py:375
  68.1 10.1 %collective-permute-start.5 = (f32[2,512,128]{2,1,0:T(8,128)}, f32[2,512,128]{2,1,0:T(8,128)S(1)}, u32[]{:S(2)}, u32[]{:S(2)}) collective-permute-start(f32[2,512,128]{2,1,0:T(8,128)} %get-tuple-element.33), channel_id=1, source_target_pairs={{0,1},{1,2},{2,3},{3,4},{4,5},{5,6},{6,7},{7,8},{8,9},{9,10},{10,1... | collective-permute-start | bytes 1572872 | tf_op jit(solution)/shard_map/ppermute | solution.py:378
  78.2 10.6 %all_to_all.16 = f32[8,16,128]{2,1,0:T(8,128)S(1)} all-to-all(f32[8,16,128]{2,1,0:T(8,128)S(1)} %broadcast_in_dim.7), channel_id=1, replica_groups=mesh['z_hi'=4,'x'=4,'y'=4,'z_lo'=2,'core'=2] {'z_hi','z_lo'}, dimensions={0} | all-to-all | bytes 131072 | tf_op jit(solution)/shard_map/all_to_all | solution.py:290
  88.8 0.0 collective-permute-done.4.above
  88.9 0.7 broadcast_in_dim.8
  89.5 9.4 %all-to-all-start.2 = ((f32[16,16,128]{2,1,0:T(8,128)}), f32[16,16,128]{2,1,0:T(8,128)S(1)}, u32[]{:S(2)}, u32[]{:S(2)}) async-start(f32[16,16,128]{2,1,0:T(8,128)} %broadcast_in_dim.8), calls=%async_computation.2 | async-start | bytes 262144 | tf_op jit(solution)/shard_map/all_to_all | solution.py:290
  98.9 1.3 %collective-permute-start.6 = (f32[2,128,128]{2,1,0:T(8,128)}, f32[2,128,128]{2,1,0:T(8,128)S(1)}, u32[]{:S(2)}, u32[]{:S(2)}) collective-permute-start(f32[2,128,128]{2,1,0:T(8,128)} %get-tuple-element.34), channel_id=1, source_target_pairs={{0,65},{1,66},{2,67},{3,68},{4,69},{5,70},{6,71},{7,72},{8,73},{9,... | collective-permute-start | bytes 393224 | tf_op jit(solution)/shard_map/ppermute | solution.py:379
  100.2 5.4 %all-to-all-done.2 = f32[16,16,128]{2,1,0:T(8,128)S(1)} async-done(((f32[16,16,128]{2,1,0:T(8,128)}), f32[16,16,128]{2,1,0:T(8,128)S(1)}, u32[]{:S(2)}, u32[]{:S(2)}) %all-to-all-start.2) | async-done | bytes 131104 | tf_op jit(solution)/shard_map/all_to_all | solution.py:290
  105.6 0.0 collective-permute-start.7
  105.6 0.0 collective-permute-done.6.corner
  105.6 0.0 collective-permute-done.5.left
  105.6 1.3 %collective-permute-done.7.other = f32[2,128,128]{2,1,0:T(8,128)S(1)} collective-permute-done((f32[2,128,128]{2,1,0:T(8,128)S(1)}, f32[2,128,128]{2,1,0:T(8,128)S(1)}, u32[]{:S(2)}, u32[]{:S(2)}) %collective-permute-start.7) | collective-permute-done | bytes 131104 | tf_op jit(solution)/shard_map/ppermute | solution.py:383
  106.9 2.2 %seams.1 = (f32[2,512,512]{2,1,0:T(8,128)}, f32[2,2,128,128]{3,2,1,0:T(8,128)}) custom-call(s32[1]{0:T(128)} %bitcast.core, f32[2,512,512]{2,1,0:T(8,128)} %get-tuple-element.25.grad_in, f32[2,128,512]{2,1,0:T(8,128)S(1)} %collective-permute-done.4.above, f32[2,512,128]{2,1,0:T(8,128)S(1)} %collective-permute-done.5.left, ...), custom_call_target="tpu_custom_call", output_to_operand_aliasing={{0}: (1, {})} | custom-call | tf_op jit(solution)/shard_map/seams/pallas_call | solution.py:385
  (3 shorter events, 0.0 us)
Async XLA Ops:
  2.9 21.5 %collective-permute-start = (f32[2,512,128]{2,1,0:T(8,128)}, f32[2,512,128]{2,1,0:T(8,128)S(1)}, u32[]{:S(2)}, u32[]{:S(2)}) collective-permute-start(f32[2,512,128]{2,1,0:T(8,128)} %get-tuple-element.19), channel_id=1, source_target_pairs={{1,0},{2,1},{3,2},{4,3},{5,4},{6,5},{7,6},{8,7},{9,8},{10,9},{11,1... | collective-permute-start | bytes 1572872 | tf_op jit(solution)/shard_map/ppermute | solution.py:330
  8.0 28.0 %collective-permute-start.2 = (f32[2,128,128]{2,1,0:T(8,128)}, f32[2,128,128]{2,1,0:T(8,128)S(1)}, u32[]{:S(2)}, u32[]{:S(2)}) collective-permute-start(f32[2,128,128]{2,1,0:T(8,128)} %get-tuple-element.21), channel_id=1, source_target_pairs={{65,0},{66,1},{67,2},{68,3},{69,4},{70,5},{71,6},{72,7},{73,8},{74... | collective-permute-start | bytes 393224 | tf_op jit(solution)/shard_map/ppermute | solution.py:331
  9.3 26.7 %collective-permute-start.1 = (f32[2,128,512]{2,1,0:T(8,128)}, f32[2,128,512]{2,1,0:T(8,128)}, u32[]{:S(2)}, u32[]{:S(2)}) collective-permute-start(f32[2,128,512]{2,1,0:T(8,128)} %get-tuple-element.20), channel_id=1, source_target_pairs={{64,0},{128,64},{192,128},{65,1},{129,65},{193,129},{66,2},{130,66... | collective-permute-start | bytes 1572872 | tf_op jit(solution)/shard_map/ppermute | solution.py:329
  24.3 0.8 copy-start
  36.0 0.7 copy-start.1
  42.3 10.0 %collective-permute-start.3 = (f32[2,128,128]{2,1,0:T(8,128)}, f32[2,128,128]{2,1,0:T(8,128)S(1)}, u32[]{:S(2)}, u32[]{:S(2)}) collective-permute-start(f32[2,128,128]{2,1,0:T(8,128)} %get-tuple-element.27), channel_id=1, source_target_pairs={{0,1},{1,0},{2,3},{3,2},{4,5},{5,4},{6,7},{7,6},{8,9},{9,8},{10,11... | collective-permute-start | bytes 393224 | tf_op jit(solution)/shard_map/ppermute | solution.py:374
  42.4 46.5 %collective-permute-start.4 = (f32[2,128,512]{2,1,0:T(8,128)}, f32[2,128,512]{2,1,0:T(8,128)S(1)}, u32[]{:S(2)}, u32[]{:S(2)}) collective-permute-start(f32[2,128,512]{2,1,0:T(8,128)} %get-tuple-element.31), channel_id=1, source_target_pairs={{0,64},{64,128},{128,192},{1,65},{65,129},{129,193},{2,66},{66,130... | collective-permute-start | bytes 1572872 | tf_op jit(solution)/shard_map/ppermute | solution.py:373
  68.1 37.5 %collective-permute-start.5 = (f32[2,512,128]{2,1,0:T(8,128)}, f32[2,512,128]{2,1,0:T(8,128)S(1)}, u32[]{:S(2)}, u32[]{:S(2)}) collective-permute-start(f32[2,512,128]{2,1,0:T(8,128)} %get-tuple-element.33), channel_id=1, source_target_pairs={{0,1},{1,2},{2,3},{3,4},{4,5},{5,6},{6,7},{7,8},{8,9},{9,10},{10,1... | collective-permute-start | bytes 1572872 | tf_op jit(solution)/shard_map/ppermute | solution.py:378
  89.5 16.1 %all-to-all-start.2 = ((f32[16,16,128]{2,1,0:T(8,128)}), f32[16,16,128]{2,1,0:T(8,128)S(1)}, u32[]{:S(2)}, u32[]{:S(2)}) async-start(f32[16,16,128]{2,1,0:T(8,128)} %broadcast_in_dim.8), calls=%async_computation.2 | async-start | bytes 262144 | tf_op jit(solution)/shard_map/all_to_all | solution.py:290
  98.9 6.7 %collective-permute-start.6 = (f32[2,128,128]{2,1,0:T(8,128)}, f32[2,128,128]{2,1,0:T(8,128)S(1)}, u32[]{:S(2)}, u32[]{:S(2)}) collective-permute-start(f32[2,128,128]{2,1,0:T(8,128)} %get-tuple-element.34), channel_id=1, source_target_pairs={{0,65},{1,66},{2,67},{3,68},{4,69},{5,70},{6,71},{7,72},{8,73},{9,... | collective-permute-start | bytes 393224 | tf_op jit(solution)/shard_map/ppermute | solution.py:379
  105.6 1.3 %collective-permute-start.7 = (f32[2,128,128]{2,1,0:T(8,128)S(1)}, f32[2,128,128]{2,1,0:T(8,128)S(1)}, u32[]{:S(2)}, u32[]{:S(2)}) collective-permute-start(f32[2,128,128]{2,1,0:T(8,128)S(1)} %bitcast.10), channel_id=1, source_target_pairs={{0,1},{1,0},{2,3},{3,2},{4,5},{5,4},{6,7},{7,6},{8,9},{9,8},{10,11... | collective-permute-start | bytes 393224 | tf_op jit(solution)/shard_map/ppermute | solution.py:383

commit v5 on v4

--- a/solution.py
+++ b/solution.py
@@ -178,12 +178,10 @@
     return [array.at[:, :, pl.ds(t * PATCH, PATCH)] for t in range(tiles)]
 
 
-def rim_kernel(own, below, right, corner, below_buf, right_buf, sems):
+def rim_kernel(own, below, right, below_buf, right_buf, sems):
     rim = pl.ds(0, PATCH)
     loads = copies_of([(own.at[:, rim, :], below_buf), (own.at[:, :, rim], right_buf)], sems)
-    stores = copies_of(
-        [(below_buf, below), (right_buf, right), (below_buf.at[:, :, rim], corner)], sems
-    )
+    stores = copies_of([(below_buf, below), (right_buf, right)], sems)
     start_all(loads)
     wait_all(loads)
     start_all(stores)
@@ -220,7 +218,7 @@
 
 
 def lower_kernel(scale, pos, count, core, own, right, below, corner, photons, probe_in, waves_in, own_in, right_in, sum_in,
-                 g_own, g_right, g_below, g_corner, kept, sent,
+                 g_own, g_right, g_below, kept, sent,
                  field, grad, photon_buf, probe, waves, plus_ref, minus_ref, probe_sum, listed, sems, photon_sems):
     rows, cols = own.shape[1], own.shape[2]
     tiles = cols // PATCH
@@ -249,7 +247,7 @@
     probe_sum[...] = probe_sum[...] * scale
     stores = copies_of(
         [(probe_sum.at[core[0]], kept), (probe_sum.at[1 - core[0]], sent)]
-        + [(grad.at[t, :, lower, :], a) for t, a in enumerate(by_tiles(g_below, tiles) + [g_corner])]
+        + [(grad.at[t, :, lower, :], a) for t, a in enumerate(by_tiles(g_below, tiles + 1))]
         + [(grad.at[t, :, upper, :], a) for t, a in enumerate(last_rows(g_own) + [g_right.at[:, last, :]])],
         sems,
     )
@@ -257,14 +255,14 @@
     wait_all(stores)
 
 
-def seam_kernel(core, grad_in, above, left, corner, value, other, grad, probe,
-                top_buf, left_buf, above_buf, beside_buf, corner_buf, probe_buf, sems):
+def seam_kernel(core, grad_in, above, left, value, other, grad, probe,
+                top_buf, left_buf, above_buf, beside_buf, probe_buf, sems):
     rows, cols = grad.shape[1], grad.shape[2]
     rest = rows - PATCH
     top_rim = grad.at[:, pl.ds(0, PATCH), :]
     left_rim = grad.at[:, pl.ds(PATCH, rest), pl.ds(0, PATCH)]
     loads = copies_of(
-        [(top_rim, top_buf), (left_rim, left_buf), (above, above_buf), (left, beside_buf), (corner, corner_buf),
+        [(top_rim, top_buf), (left_rim, left_buf), (above.at[:, :, pl.ds(0, cols)], above_buf), (left, beside_buf),
          (value, probe_buf.at[core[0]]), (other, probe_buf.at[1 - core[0]])],
         sems,
     )
@@ -273,7 +271,7 @@
     join = pltpu.make_async_copy(probe_buf, probe, sems.at[2])
     join.start()
     top_buf[:, :, PATCH:] += above_buf[:, :, PATCH:]
-    top_buf[:, :, :PATCH] += above_buf[:, :, :PATCH] + (beside_buf[:, :PATCH, :] + corner_buf[...])
+    top_buf[:, :, :PATCH] += above_buf[:, :, :PATCH] + beside_buf[:, :PATCH, :]
     left_buf[...] += beside_buf[:, PATCH:, :]
     stores = copies_of([(top_buf, top_rim), (left_buf, left_rim)], sems)
     start_all(stores)
@@ -303,32 +301,28 @@
     down = [(i, i + 1) for i in range(n_row - 1)]
     along = [(i, i + 1) for i in range(n_col - 1)]
     up, back = ([(j, i) for i, j in pairs] for pairs in (down, along))
-    diagonal = [
-        (a * n_col + b, (a + 1) * n_col + b + 1) for a in range(n_row - 1) for b in range(n_col - 1)
-    ]
-    diagonal_back = [(j, i) for i, j in diagonal]
     core = lax.axis_index("core")[None]
     smem = pl.BlockSpec(memory_space=pltpu.SMEM)
     hbm = pl.BlockSpec(memory_space=pl.ANY)
     params = pltpu.CompilerParams(vmem_limit_bytes=VMEM_LIMIT)
 
     rim_shape = shape(2, PATCH, PATCH)
-    below, right, corner = pl.pallas_call(
+    below, right = pl.pallas_call(
         rim_kernel,
-        out_shape=(shape(2, PATCH, cols), shape(2, rows, PATCH), rim_shape),
+        out_shape=(shape(2, PATCH, cols), shape(2, rows, PATCH)),
         in_specs=[hbm],
-        out_specs=(hbm,) * 3,
+        out_specs=(hbm,) * 2,
         scratch_shapes=[
             pltpu.VMEM((2, PATCH, cols), F32),
             pltpu.VMEM((2, rows, PATCH), F32),
-            pltpu.SemaphoreType.DMA((3,)),
+            pltpu.SemaphoreType.DMA((2,)),
         ],
         compiler_params=params,
         name="rims",
     )(object_field)
+    right = lax.ppermute(right, COL, back)
+    below, right = lax.optimization_barrier((below, right))
     below = lax.ppermute(below, ROW, up)
-    right = lax.ppermute(right, COL, back)
-    corner = lax.ppermute(corner, BOTH, diagonal_back)
 
     def scratch(height):
         return [
@@ -356,11 +350,13 @@
         cost_estimate=pl.CostEstimate(flops=24 * 10**9, bytes_accessed=8 * 2**20, transcendentals=0),
         name="upper_slots",
     )(pos, count, object_field, right, photon_rows, probe_modes, waves)
-    g_own, g_right, g_below, g_corner, kept, sent = pl.pallas_call(
+    below, probe_1 = lax.optimization_barrier((below, probe_1))
+    corner = lax.ppermute(below[:, :, :PATCH], COL, back)
+    g_own, g_right, g_below, kept, sent = pl.pallas_call(
         functools.partial(lower_kernel, scale),
-        out_shape=(own_shape, right_shape, shape(2, PATCH, cols), rim_shape, rim_shape, rim_shape),
+        out_shape=(own_shape, right_shape, shape(2, PATCH, cols + PATCH), rim_shape, rim_shape),
         in_specs=[smem] * 3 + [hbm] * 10,
-        out_specs=(hbm,) * 6,
+        out_specs=(hbm,) * 5,
         scratch_shapes=scratch(2 * PATCH),
         input_output_aliases={10: 0, 11: 1},
         compiler_params=params,
@@ -374,32 +370,29 @@
     value = kept + lax.ppermute(sent, "core", swap)
     shares = lax.all_to_all(value.reshape(plane, -1, PATCH), PLANE, 0, 0, tiled=True)
     share = jnp.sum(shares, axis=0)
-    share, g_right, g_corner = lax.optimization_barrier((share, g_right, g_corner))
-    left = lax.ppermute(g_right, COL, along)
-    from_corner = lax.ppermute(g_corner, BOTH, diagonal)
     share = jnp.sum(everyone(share, DEPTH, depth), axis=0)
     share, above = lax.optimization_barrier((share, above))
+    left = lax.ppermute(g_right.at[:, :PATCH, :].add(above[:, :, cols:]), COL, along)
     value = everyone(share, PLANE, plane).reshape(kept.shape)
     other = lax.ppermute(value, "core", swap)
 
     object_gradient, probe_gradient = pl.pallas_call(
         seam_kernel,
         out_shape=(own_shape, probe_shape),
-        in_specs=[smem] + [hbm] * 6,
+        in_specs=[smem] + [hbm] * 5,
         out_specs=(hbm, hbm),
         scratch_shapes=[
             pltpu.VMEM((2, PATCH, cols), F32),
             pltpu.VMEM((2, rows - PATCH, PATCH), F32),
             pltpu.VMEM((2, PATCH, cols), F32),
             pltpu.VMEM((2, rows, PATCH), F32),
-            pltpu.VMEM((2, PATCH, PATCH), F32),
             pltpu.VMEM(probe_modes.shape, F32),
-            pltpu.SemaphoreType.DMA((7,)),
+            pltpu.SemaphoreType.DMA((6,)),
         ],
         input_output_aliases={1: 0},
         compiler_params=pltpu.CompilerParams(vmem_limit_bytes=8 * 2**20),
         name="seams",
-    )(core, g_own, above, left, from_corner, value, other)
+    )(core, g_own, above, left, value, other)
     return (object_gradient, probe_gradient)
 
 

time: 109 us -> 121 us (1.11)
  blocking collectives: 25.5 us -> 50.4 us
  starting transfers between devices: 38.4 us -> 19.5 us
  waiting for transfers between devices: 23.5 us -> 28.2 us
  other arithmetic: 0.96 us -> 2.53 us
    all_to_all x1 -> x2, blocking collectives: 10.6 us -> 28.5 us  [everyone(): return lax.all_to_all(sent, axes, 0, 0, tiled=True)]
    ppermute x1, waiting for transfers between devices: 0.01 us -> 15.1 us  [body(): below = lax.ppermute(below, ROW, up)]
    all_to_all x1 -> x0, starting transfers between devices: 9.37 us -> none  [everyone(): return lax.all_to_all(sent, axes, 0, 0, tiled=True)]
    all_to_all x1, blocking collectives: 14.9 us -> 22 us  [body(): lax.all_to_all(value.reshape(plane, -1, PATCH), PLANE, 0, 0, tiled=True)]
    ppermute x1, waiting for transfers between devices: 13.1 us -> 6.2 us  [body(): right = lax.ppermute(right, COL, back)]
    ppermute x3 -> x2, starting transfers between devices: 12.7 us -> 6.84 us  [the longest x1 4.92 us: body(): lax.ppermute(g_right.at[:, :PATCH, :].add(above[:, :, cols:]), COL, along)]
    all_to_all x1 -> x0, waiting for transfers between devices: 5.39 us -> none  [everyone(): return lax.all_to_all(sent, axes, 0, 0, tiled=True)]
    ppermute x1, starting transfers between devices: 9.87 us -> 5 us  [body(): above = lax.ppermute(g_below, ROW, down)]
  transfers between devices with their start and end apart: 9 -> 7, of which waited for: 4 -> 5; matrix products, arithmetic and copies ran while one was open for 1% -> 1% of each run, Pallas kernels for 7% -> 6%
where the time goes in v5:
time: 121 us
  blocking collectives  50.4 us (42%)
  waiting for transfers between devices  28.2 us (23%)
  starting transfers between devices  19.5 us (16%)
  Pallas kernels  17.3 us (14%)
  other arithmetic  2.53 us (2%)
  local copies, waits for them, and re-layouts  1.48 us (1%)
  between operations  1.4 us (1%)
    all_to_all x2, blocking collectives, everyone(): return lax.all_to_all(sent, axes, 0, 0, tiled=True)  28.5 us
    all_to_all x1, blocking collectives, body(): lax.all_to_all(value.reshape(plane, -1, PATCH), PLANE, 0, 0, tiled=True)  22 us
    ppermute x1, waiting for transfers between devices, body(): below = lax.ppermute(below, ROW, up)  15.1 us
    pallas_call x1, Pallas kernels, body(): pl.pallas_call(upper_kernel, out_shape=(own_shape, right_shape, probe_sha...  7.21 us
    ppermute x1, waiting for transfers between devices, body(): right = lax.ppermute(right, COL, back)  6.2 us
    pallas_call x1, Pallas kernels, body(): pl.pallas_call(functools.partial(lower_kernel, scale), out_shape=(own_sha...  5.66 us
    ppermute x1, starting transfers between devices, body(): right = lax.ppermute(right, COL, back)  5.15 us
    ppermute x1, starting transfers between devices, body(): above = lax.ppermute(g_below, ROW, down)  5 us
  transfers between devices with their start and end apart: 7, of which 5 were waited for; matrix products, arithmetic and copies ran while one was open for 1% of the time, Pallas kernels for 6%

profile of v5, /device:TPU:1, one launch (start us, length us, event | category | flops | bytes accessed | tf_op | source)
XLA Modules:
  0.0 120.7 jit_solution(302360107515981117)
XLA Ops:
  0.6 2.2 %rims.1 = (f32[2,128,512]{2,1,0:T(8,128)}, f32[2,512,128]{2,1,0:T(8,128)}) custom-call(f32[2,512,512]{2,1,0:T(8,128)} %own.5), custom_call_target="tpu_custom_call" | custom-call | tf_op jit(solution)/shard_map/rims/pallas_call | solution.py:310
  2.8 5.1 %collective-permute-start = (f32[2,512,128]{2,1,0:T(8,128)}, f32[2,512,128]{2,1,0:T(8,128)S(1)}, u32[]{:S(2)}, u32[]{:S(2)}) collective-permute-start(f32[2,512,128]{2,1,0:T(8,128)} %get-tuple-element.31), channel_id=1, source_target_pairs={{1,0},{2,1},{3,2},{4,3},{5,4},{6,5},{7,6},{8,7},{9,8},{10,9},{11,1... | collective-permute-start | bytes 1572872 | tf_op jit(solution)/shard_map/ppermute | solution.py:323
  8.6 6.2 %collective-permute-done.right = f32[2,512,128]{2,1,0:T(8,128)S(1)} collective-permute-done((f32[2,512,128]{2,1,0:T(8,128)}, f32[2,512,128]{2,1,0:T(8,128)S(1)}, u32[]{:S(2)}, u32[]{:S(2)}) %collective-permute-start) | collective-permute-done | bytes 524320 | tf_op jit(solution)/shard_map/ppermute | solution.py:323
  14.8 0.0 copy-start.1
  14.8 0.8 copy-done.1
  15.6 1.3 %collective-permute-start.1 = (f32[2,128,512]{2,1,0:T(8,128)}, f32[2,128,512]{2,1,0:T(8,128)S(1)}, u32[]{:S(2)}, u32[]{:S(2)}) collective-permute-start(f32[2,128,512]{2,1,0:T(8,128)} %get-tuple-element.33), channel_id=1, source_target_pairs={{64,0},{128,64},{192,128},{65,1},{129,65},{193,129},{66,2},{130,66... | collective-permute-start | bytes 1572872 | tf_op jit(solution)/shard_map/ppermute | solution.py:325
  16.9 7.2 %upper_slots.1 = (f32[2,512,512]{2,1,0:T(8,128)}, f32[2,512,128]{2,1,0:T(8,128)}, f32[2,2,128,128]{3,2,1,0:T(8,128)}) custom-call(s32[2,64]{1,0:T(2,128)} %bitcast.15, s32[1]{0:T(128)} %bitcast.8.count, f32[2,512,512]{2,1,0:T(8,128)} %own.5, f32[2,512,128]{2,1,0:T(8,128)} %copy-done.1, bf16[64,128,128]{2,1,0:T(8,128)(2,1)} %bitcast.13, ...), custom_call_target="tpu_custom_call" | custom-call | flops 24000000000 | bytes 8388608 | tf_op jit(solution)/shard_map/upper_slots/pallas_call | solution.py:343
  24.1 15.1 %collective-permute-done.1.below = f32[2,128,512]{2,1,0:T(8,128)S(1)} collective-permute-done((f32[2,128,512]{2,1,0:T(8,128)}, f32[2,128,512]{2,1,0:T(8,128)S(1)}, u32[]{:S(2)}, u32[]{:S(2)}) %collective-permute-start.1) | collective-permute-done | bytes 524320 | tf_op jit(solution)/shard_map/ppermute | solution.py:325
  39.2 0.0 copy-start
  39.2 1.9 %collective-permute-start.2 = (f32[2,128,128]{2,1,0:T(8,128)S(1)}, f32[2,128,128]{2,1,0:T(8,128)S(1)}, u32[]{:S(2)}, u32[]{:S(2)}) collective-permute-start(f32[2,128,128]{2,1,0:T(8,128)S(1)} %slice.30), channel_id=1, source_target_pairs={{1,0},{2,1},{3,2},{4,3},{5,4},{6,5},{7,6},{8,7},{9,8},{10,9},{11,1... | collective-permute-start | bytes 393224 | tf_op jit(solution)/shard_map/ppermute | solution.py:354
  41.2 4.4 %collective-permute-done.2.corner = f32[2,128,128]{2,1,0:T(8,128)S(1)} collective-permute-done((f32[2,128,128]{2,1,0:T(8,128)S(1)}, f32[2,128,128]{2,1,0:T(8,128)S(1)}, u32[]{:S(2)}, u32[]{:S(2)}) %collective-permute-start.2) | collective-permute-done | bytes 131104 | tf_op jit(solution)/shard_map/ppermute | solution.py:354
  45.5 0.0 copy-start.2
  45.5 0.0 copy-done
  45.5 0.6 copy-done.2
  46.2 5.7 %lower_slots.1 = (f32[2,512,512]{2,1,0:T(8,128)}, f32[2,512,128]{2,1,0:T(8,128)}, f32[2,128,640]{2,1,0:T(8,128)}, f32[2,128,128]{2,1,0:T(8,128)}, f32[2,128,128]{2,1,0:T(8,128)}) custom-call(s32[2,64]{1,0:T(2,128)} %bitcast.16, s32[1]{0:T(128)} %bitcast.9.count, s32[1]{0:T(128)} %bitcast.core, ...), custom_call_target="tpu_custom_call", output_to_operand_aliasing={{0}: (10, {}), {1}: (11, {})} | custom-call | flops 8000000000 | bytes 4194304 | tf_op jit(solution)/shard_map/lower_slots/pallas_call | solution.py:355
  51.8 5.0 %collective-permute-start.4 = (f32[2,128,640]{2,1,0:T(8,128)}, f32[2,128,640]{2,1,0:T(8,128)S(1)}, u32[]{:S(2)}, u32[]{:S(2)}) collective-permute-start(f32[2,128,640]{2,1,0:T(8,128)} %get-tuple-element.42), channel_id=1, source_target_pairs={{0,64},{64,128},{128,192},{1,65},{65,129},{129,193},{2,66},{66,130... | collective-permute-start | bytes 1966088 | tf_op jit(solution)/shard_map/ppermute | solution.py:369
  56.8 0.1 collective-permute-start.3
  56.9 1.5 %collective-permute-done.3 = f32[2,128,128]{2,1,0:T(8,128)S(1)} collective-permute-done((f32[2,128,128]{2,1,0:T(8,128)}, f32[2,128,128]{2,1,0:T(8,128)S(1)}, u32[]{:S(2)}, u32[]{:S(2)}) %collective-permute-start.3) | collective-permute-done | bytes 131104 | tf_op jit(solution)/shard_map/ppermute | solution.py:370
  58.5 0.9 add.10
  59.4 22.0 %all_to_all.15 = f32[16,16,128]{2,1,0:T(8,128)S(1)} all-to-all(f32[16,16,128]{2,1,0:T(8,128)S(1)} %bitcast.12), channel_id=1, replica_groups=mesh['z_hi'=4,'x'=4,'y'=4,'z_lo'=2,'core'=2] {'x','y'}, dimensions={0} | all-to-all | bytes 262144 | tf_op jit(solution)/shard_map/all_to_all | solution.py:371
  81.4 11.8 %all_to_all.16 = f32[8,16,128]{2,1,0:T(8,128)S(1)} all-to-all(f32[8,16,128]{2,1,0:T(8,128)S(1)} %broadcast_in_dim.7), channel_id=1, replica_groups=mesh['z_hi'=4,'x'=4,'y'=4,'z_lo'=2,'core'=2] {'z_hi','z_lo'}, dimensions={0} | all-to-all | bytes 131072 | tf_op jit(solution)/shard_map/all_to_all | solution.py:288
  93.2 0.0 collective-permute-done.4.above
  93.2 1.6 %add_dynamic-update-slice_fusion = f32[2,512,128]{2,1,0:T(8,128)} fusion(f32[2,512,128]{2,1,0:T(8,128)} %get-tuple-element.44, f32[2,128,640]{2,1,0:T(8,128)S(1)} %collective-permute-done.4.above), kind=kLoop, calls=%fused_computation | loop fusion | flops 32768 | bytes 393216 | tf_op jit(solution)/shard_map/scatter-add | solution.py:375
  94.8 4.9 %collective-permute-start.5 = (f32[2,512,128]{2,1,0:T(8,128)}, f32[2,512,128]{2,1,0:T(8,128)S(1)}, u32[]{:S(2)}, u32[]{:S(2)}) collective-permute-start(f32[2,512,128]{2,1,0:T(8,128)} %add_dynamic-update-slice_fusion), channel_id=1, source_target_pairs={{0,1},{1,2},{2,3},{3,4},{4,5},{5,6},{6,7},{7,8},{8,9},{9,10},{10,1... | collective-permute-start | bytes 1572872 | tf_op jit(solution)/shard_map/ppermute | solution.py:375
  99.7 16.7 %all_to_all.17 = f32[16,16,128]{2,1,0:T(8,128)S(1)} all-to-all(f32[16,16,128]{2,1,0:T(8,128)S(1)} %broadcast_in_dim.8), channel_id=1, replica_groups=mesh['z_hi'=4,'x'=4,'y'=4,'z_lo'=2,'core'=2] {'x','y'}, dimensions={0} | all-to-all | bytes 262144 | tf_op jit(solution)/shard_map/all_to_all | solution.py:288
  116.4 1.1 collective-permute-start.6
  117.5 1.0 collective-permute-done.6.other
  118.5 0.0 collective-permute-done.5.left
  118.5 2.2 %seams.1 = (f32[2,512,512]{2,1,0:T(8,128)}, f32[2,2,128,128]{3,2,1,0:T(8,128)}) custom-call(s32[1]{0:T(128)} %bitcast.core, f32[2,512,512]{2,1,0:T(8,128)} %get-tuple-element.39.grad_in, f32[2,128,640]{2,1,0:T(8,128)S(1)} %collective-permute-done.4.above, f32[2,512,128]{2,1,0:T(8,128)S(1)} %collective-permute-done.5.left, ...), custom_call_target="tpu_custom_call", output_to_operand_aliasing={{0}: (1, {})} | custom-call | tf_op jit(solution)/shard_map/seams/pallas_call | solution.py:379
  (5 shorter events, 0.1 us)
Async XLA Ops:
  2.8 12.0 %collective-permute-start = (f32[2,512,128]{2,1,0:T(8,128)}, f32[2,512,128]{2,1,0:T(8,128)S(1)}, u32[]{:S(2)}, u32[]{:S(2)}) collective-permute-start(f32[2,512,128]{2,1,0:T(8,128)} %get-tuple-element.31), channel_id=1, source_target_pairs={{1,0},{2,1},{3,2},{4,3},{5,4},{6,5},{7,6},{8,7},{9,8},{10,9},{11,1... | collective-permute-start | bytes 1572872 | tf_op jit(solution)/shard_map/ppermute | solution.py:323
  14.8 0.8 copy-start.1
  15.6 23.6 %collective-permute-start.1 = (f32[2,128,512]{2,1,0:T(8,128)}, f32[2,128,512]{2,1,0:T(8,128)S(1)}, u32[]{:S(2)}, u32[]{:S(2)}) collective-permute-start(f32[2,128,512]{2,1,0:T(8,128)} %get-tuple-element.33), channel_id=1, source_target_pairs={{64,0},{128,64},{192,128},{65,1},{129,65},{193,129},{66,2},{130,66... | collective-permute-start | bytes 1572872 | tf_op jit(solution)/shard_map/ppermute | solution.py:325
  39.2 6.3 %copy-start = (f32[2,128,512]{2,1,0:T(8,128)}, f32[2,128,512]{2,1,0:T(8,128)S(1)}, u32[]{:S(2)}) copy-start(f32[2,128,512]{2,1,0:T(8,128)S(1)} %collective-permute-done.1.below) | copy-start | bytes 1572868
  39.2 6.3 %collective-permute-start.2 = (f32[2,128,128]{2,1,0:T(8,128)S(1)}, f32[2,128,128]{2,1,0:T(8,128)S(1)}, u32[]{:S(2)}, u32[]{:S(2)}) collective-permute-start(f32[2,128,128]{2,1,0:T(8,128)S(1)} %slice.30), channel_id=1, source_target_pairs={{1,0},{2,1},{3,2},{4,3},{5,4},{6,5},{7,6},{8,7},{9,8},{10,9},{11,1... | collective-permute-start | bytes 393224 | tf_op jit(solution)/shard_map/ppermute | solution.py:354
  45.5 0.6 copy-start.2
  51.8 41.4 %collective-permute-start.4 = (f32[2,128,640]{2,1,0:T(8,128)}, f32[2,128,640]{2,1,0:T(8,128)S(1)}, u32[]{:S(2)}, u32[]{:S(2)}) collective-permute-start(f32[2,128,640]{2,1,0:T(8,128)} %get-tuple-element.42), channel_id=1, source_target_pairs={{0,64},{64,128},{128,192},{1,65},{65,129},{129,193},{2,66},{66,130... | collective-permute-start | bytes 1966088 | tf_op jit(solution)/shard_map/ppermute | solution.py:369
  56.8 1.6 %collective-permute-start.3 = (f32[2,128,128]{2,1,0:T(8,128)}, f32[2,128,128]{2,1,0:T(8,128)S(1)}, u32[]{:S(2)}, u32[]{:S(2)}) collective-permute-start(f32[2,128,128]{2,1,0:T(8,128)} %get-tuple-element.41), channel_id=1, source_target_pairs={{0,1},{1,0},{2,3},{3,2},{4,5},{5,4},{6,7},{7,6},{8,9},{9,8},{10,11... | collective-permute-start | bytes 393224 | tf_op jit(solution)/shard_map/ppermute | solution.py:370
  94.8 23.7 %collective-permute-start.5 = (f32[2,512,128]{2,1,0:T(8,128)}, f32[2,512,128]{2,1,0:T(8,128)S(1)}, u32[]{:S(2)}, u32[]{:S(2)}) collective-permute-start(f32[2,512,128]{2,1,0:T(8,128)} %add_dynamic-update-slice_fusion), channel_id=1, source_target_pairs={{0,1},{1,2},{2,3},{3,4},{4,5},{5,6},{6,7},{7,8},{8,9},{9,10},{10,1... | collective-permute-start | bytes 1572872 | tf_op jit(solution)/shard_map/ppermute | solution.py:375
  116.4 2.1 %collective-permute-start.6 = (f32[2,128,128]{2,1,0:T(8,128)S(1)}, f32[2,128,128]{2,1,0:T(8,128)S(1)}, u32[]{:S(2)}, u32[]{:S(2)}) collective-permute-start(f32[2,128,128]{2,1,0:T(8,128)S(1)} %bitcast.10), channel_id=1, source_target_pairs={{0,1},{1,0},{2,3},{3,2},{4,5},{5,4},{6,7},{7,6},{8,9},{9,8},{10,11... | collective-permute-start | bytes 393224 | tf_op jit(solution)/shard_map/ppermute | solution.py:377

commit v6 on v4

--- a/solution.py
+++ b/solution.py
@@ -257,7 +257,7 @@
     wait_all(stores)
 
 
-def seam_kernel(core, grad_in, above, left, corner, value, other, grad, probe,
+def seam_kernel(grad_in, above, left, corner, parts, grad, probe,
                 top_buf, left_buf, above_buf, beside_buf, corner_buf, probe_buf, sems):
     rows, cols = grad.shape[1], grad.shape[2]
     rest = rows - PATCH
@@ -265,7 +265,7 @@
     left_rim = grad.at[:, pl.ds(PATCH, rest), pl.ds(0, PATCH)]
     loads = copies_of(
         [(top_rim, top_buf), (left_rim, left_buf), (above, above_buf), (left, beside_buf), (corner, corner_buf),
-         (value, probe_buf.at[core[0]]), (other, probe_buf.at[1 - core[0]])],
+         (parts.at[:, 0], probe_buf.at[0]), (parts.at[:, 1], probe_buf.at[1])],
         sems,
     )
     start_all(loads)
@@ -374,18 +374,17 @@
     value = kept + lax.ppermute(sent, "core", swap)
     shares = lax.all_to_all(value.reshape(plane, -1, PATCH), PLANE, 0, 0, tiled=True)
     share = jnp.sum(shares, axis=0)
-    share, g_right, g_corner = lax.optimization_barrier((share, g_right, g_corner))
+    share = jnp.sum(everyone(share, DEPTH, depth), axis=0)
+    share, above, g_right, g_corner = lax.optimization_barrier((share, above, g_right, g_corner))
     left = lax.ppermute(g_right, COL, along)
     from_corner = lax.ppermute(g_corner, BOTH, diagonal)
-    share = jnp.sum(everyone(share, DEPTH, depth), axis=0)
-    share, above = lax.optimization_barrier((share, above))
-    value = everyone(share, PLANE, plane).reshape(kept.shape)
-    other = lax.ppermute(value, "core", swap)
+    parts = everyone(share, PLANE + ("core",), 2 * plane)
+    parts = parts.reshape(plane, 2, *share.shape)
 
     object_gradient, probe_gradient = pl.pallas_call(
         seam_kernel,
-        out_shape=(own_shape, probe_shape),
-        in_specs=[smem] + [hbm] * 6,
+        out_shape=(own_shape, shape(2, plane, *share.shape)),
+        in_specs=[hbm] * 5,
         out_specs=(hbm, hbm),
         scratch_shapes=[
             pltpu.VMEM((2, PATCH, cols), F32),
@@ -393,14 +392,14 @@
             pltpu.VMEM((2, PATCH, cols), F32),
             pltpu.VMEM((2, rows, PATCH), F32),
             pltpu.VMEM((2, PATCH, PATCH), F32),
-            pltpu.VMEM(probe_modes.shape, F32),
+            pltpu.VMEM((2, plane) + share.shape, F32),
             pltpu.SemaphoreType.DMA((7,)),
         ],
-        input_output_aliases={1: 0},
+        input_output_aliases={0: 0},
         compiler_params=pltpu.CompilerParams(vmem_limit_bytes=8 * 2**20),
         name="seams",
-    )(core, g_own, above, left, from_corner, value, other)
-    return (object_gradient, probe_gradient)
+    )(g_own, above, left, from_corner, parts)
+    return (object_gradient, probe_gradient.reshape(probe_modes.shape))
 
 
 def solution(mesh):

time: 109 us -> 107 us (0.982); the launches traced: 109 us -> 106 us
  starting transfers between devices: 38.4 us -> 22.9 us
  Pallas kernels: 17.3 us -> 28.2 us
  blocking collectives: 25.5 us -> 31.2 us
  waiting for transfers between devices: 23.5 us -> 18.8 us
    pallas_call x1, Pallas kernels: 7.21 us -> 15.7 us  [body(): pl.pallas_call(upper_kernel, out_shape=(own_shape, right_shape, probe_sha...]
    ppermute x1, starting transfers between devices: 9.87 us -> 1.52 us  [body(): above = lax.ppermute(g_below, ROW, down)]
    all_to_all x1, starting transfers between devices: 9.37 us -> 3.7 us  [everyone(): return lax.all_to_all(sent, axes, 0, 0, tiled=True)]
    ppermute x1, starting transfers between devices: 10.1 us -> 4.83 us  [body(): left = lax.ppermute(g_right, COL, along)]
    ppermute x1, starting transfers between devices: 1.3 us -> 5.06 us  [body(): from_corner = lax.ppermute(g_corner, BOTH, diagonal)]
    ppermute x1, waiting for transfers between devices: 3.64 us -> 0.01 us  [body(): corner = lax.ppermute(corner, BOTH, diagonal_back)]
    all_to_all x1, waiting for transfers between devices: 5.39 us -> 1.89 us  [everyone(): return lax.all_to_all(sent, axes, 0, 0, tiled=True)]
    all_to_all x1, blocking collectives: 10.6 us -> 13.8 us  [everyone(): return lax.all_to_all(sent, axes, 0, 0, tiled=True)]
  transfers between devices with their start and end apart: 9 -> 8, of which waited for: 4 -> 4; matrix products, arithmetic and copies ran while one was open for 1% -> 2% of each run, Pallas kernels for 7% -> 15%
where the time goes in v6:
time: 107 us; the launch traced here: 106 us
  blocking collectives  31.2 us (29%)
  Pallas kernels  28.2 us (26%)
  starting transfers between devices  22.9 us (21%)
  waiting for transfers between devices  18.8 us (18%)
  local copies, waits for them, and re-layouts  2.16 us (2%)
  between operations  1.42 us (1%)
    all_to_all x1, blocking collectives, body(): lax.all_to_all(value.reshape(plane, -1, PATCH), PLANE, 0, 0, tiled=True)  17.3 us
    pallas_call x1, Pallas kernels, body(): pl.pallas_call(upper_kernel, out_shape=(own_shape, right_shape, probe_sha...  15.7 us
    all_to_all x1, blocking collectives, everyone(): return lax.all_to_all(sent, axes, 0, 0, tiled=True)  13.8 us
    ppermute x1, waiting for transfers between devices, body(): right = lax.ppermute(right, COL, back)  13.1 us
    pallas_call x1, Pallas kernels, body(): pl.pallas_call(functools.partial(lower_kernel, scale), out_shape=(own_sha...  8.05 us
    ppermute x1, starting transfers between devices, body(): right = lax.ppermute(right, COL, back)  5.15 us
    ppermute x1, starting transfers between devices, body(): from_corner = lax.ppermute(g_corner, BOTH, diagonal)  5.06 us
    ppermute x1, starting transfers between devices, body(): left = lax.ppermute(g_right, COL, along)  4.83 us
  transfers between devices with their start and end apart: 8, of which 4 were waited for; matrix products, arithmetic and copies ran while one was open for 2% of the time, Pallas kernels for 15%

profile of v6, /device:TPU:1, one launch (start us, length us, event | category | flops | bytes accessed | tf_op | source)
XLA Modules:
  0.0 105.7 jit_solution(2286334234262715937)
XLA Ops:
  0.6 2.2 %rims.1 = (f32[2,128,512]{2,1,0:T(8,128)}, f32[2,512,128]{2,1,0:T(8,128)}, f32[2,128,128]{2,1,0:T(8,128)}) custom-call(f32[2,512,512]{2,1,0:T(8,128)} %own.5), custom_call_target="tpu_custom_call" | custom-call | tf_op jit(solution)/shard_map/rims/pallas_call | solution.py:316
  2.9 5.1 %collective-permute-start = (f32[2,512,128]{2,1,0:T(8,128)}, f32[2,512,128]{2,1,0:T(8,128)S(1)}, u32[]{:S(2)}, u32[]{:S(2)}) collective-permute-start(f32[2,512,128]{2,1,0:T(8,128)} %get-tuple-element.20), channel_id=1, source_target_pairs={{1,0},{2,1},{3,2},{4,3},{5,4},{6,5},{7,6},{8,7},{9,8},{10,9},{11,1... | collective-permute-start | bytes 1572872 | tf_op jit(solution)/shard_map/ppermute | solution.py:330
  8.0 1.3 %collective-permute-start.2 = (f32[2,128,128]{2,1,0:T(8,128)}, f32[2,128,128]{2,1,0:T(8,128)S(1)}, u32[]{:S(2)}, u32[]{:S(2)}) collective-permute-start(f32[2,128,128]{2,1,0:T(8,128)} %get-tuple-element.22), channel_id=1, source_target_pairs={{65,0},{66,1},{67,2},{68,3},{69,4},{70,5},{71,6},{72,7},{73,8},{74... | collective-permute-start | bytes 393224 | tf_op jit(solution)/shard_map/ppermute | solution.py:331
  9.3 1.3 %collective-permute-start.1 = (f32[2,128,512]{2,1,0:T(8,128)}, f32[2,128,512]{2,1,0:T(8,128)}, u32[]{:S(2)}, u32[]{:S(2)}) collective-permute-start(f32[2,128,512]{2,1,0:T(8,128)} %get-tuple-element.21), channel_id=1, source_target_pairs={{64,0},{128,64},{192,128},{65,1},{129,65},{193,129},{66,2},{130,66... | collective-permute-start | bytes 1572872 | tf_op jit(solution)/shard_map/ppermute | solution.py:329
  11.3 13.1 %collective-permute-done.right = f32[2,512,128]{2,1,0:T(8,128)S(1)} collective-permute-done((f32[2,512,128]{2,1,0:T(8,128)}, f32[2,512,128]{2,1,0:T(8,128)S(1)}, u32[]{:S(2)}, u32[]{:S(2)}) %collective-permute-start) | collective-permute-done | bytes 524320 | tf_op jit(solution)/shard_map/ppermute | solution.py:330
  24.3 0.0 copy-start
  24.4 0.8 copy-done
  25.1 15.7 %upper_slots.1 = (f32[2,512,512]{2,1,0:T(8,128)}, f32[2,512,128]{2,1,0:T(8,128)}, f32[2,2,128,128]{3,2,1,0:T(8,128)}) custom-call(s32[2,64]{1,0:T(2,128)} %bitcast.16, s32[1]{0:T(128)} %bitcast.9.count, f32[2,512,512]{2,1,0:T(8,128)} %own.5, f32[2,512,128]{2,1,0:T(8,128)} %copy-done, bf16[64,128,128]{2,1,0:T(8,128)(2,1)} %bitcast.13, ...), custom_call_target="tpu_custom_call" | custom-call | flops 24000000000 | bytes 8388608 | tf_op jit(solution)/shard_map/upper_slots/pallas_call | solution.py:349
  40.9 0.0 collective-permute-done.2.corner
  40.9 0.0 copy-start.1
  40.9 0.0 collective-permute-done.1.below
  40.9 0.6 copy-done.1
  41.5 8.0 %lower_slots.1 = (f32[2,512,512]{2,1,0:T(8,128)}, f32[2,512,128]{2,1,0:T(8,128)}, f32[2,128,512]{2,1,0:T(8,128)}, f32[2,128,128]{2,1,0:T(8,128)}, f32[2,128,128]{2,1,0:T(8,128)}, /*index=5*/f32[2,128,128]{2,1,0:T(8,128)}) custom-call(s32[2,64]{1,0:T(2,128)} %bitcast.17, s32[1]{0:T(128)} %bitcast.10.count, ...), custom_call_target="tpu_custom_call", output_to_operand_aliasing={{0}: (10, {}), {1}: (11, {})} | custom-call | flops 8000000000 | bytes 4194304 | tf_op jit(solution)/shard_map/lower_slots/pallas_call | solution.py:359
  49.6 1.5 %collective-permute-start.4 = (f32[2,128,512]{2,1,0:T(8,128)}, f32[2,128,512]{2,1,0:T(8,128)S(1)}, u32[]{:S(2)}, u32[]{:S(2)}) collective-permute-start(f32[2,128,512]{2,1,0:T(8,128)} %get-tuple-element.29), channel_id=1, source_target_pairs={{0,64},{64,128},{128,192},{1,65},{65,129},{129,193},{2,66},{66,130... | collective-permute-start | bytes 1572872 | tf_op jit(solution)/shard_map/ppermute | solution.py:373
  51.1 0.1 collective-permute-start.3
  51.2 1.5 %collective-permute-done.3 = f32[2,128,128]{2,1,0:T(8,128)S(1)} collective-permute-done((f32[2,128,128]{2,1,0:T(8,128)}, f32[2,128,128]{2,1,0:T(8,128)S(1)}, u32[]{:S(2)}, u32[]{:S(2)}) %collective-permute-start.3) | collective-permute-done | bytes 131104 | tf_op jit(solution)/shard_map/ppermute | solution.py:374
  52.8 0.9 add.3
  53.7 17.3 %all_to_all.15 = f32[16,16,128]{2,1,0:T(8,128)S(1)} all-to-all(f32[16,16,128]{2,1,0:T(8,128)S(1)} %bitcast.12), channel_id=1, replica_groups=mesh['z_hi'=4,'x'=4,'y'=4,'z_lo'=2,'core'=2] {'x','y'}, dimensions={0} | all-to-all | bytes 262144 | tf_op jit(solution)/shard_map/all_to_all | solution.py:375
  71.1 13.8 %all_to_all.16 = f32[8,16,128]{2,1,0:T(8,128)S(1)} all-to-all(f32[8,16,128]{2,1,0:T(8,128)S(1)} %broadcast_in_dim.7), channel_id=1, replica_groups=mesh['z_hi'=4,'x'=4,'y'=4,'z_lo'=2,'core'=2] {'z_hi','z_lo'}, dimensions={0} | all-to-all | bytes 131072 | tf_op jit(solution)/shard_map/all_to_all | solution.py:290
  84.9 0.0 collective-permute-done.4.above
  84.9 4.8 %collective-permute-start.5 = (f32[2,512,128]{2,1,0:T(8,128)}, f32[2,512,128]{2,1,0:T(8,128)S(1)}, u32[]{:S(2)}, u32[]{:S(2)}) collective-permute-start(f32[2,512,128]{2,1,0:T(8,128)} %get-tuple-element.33), channel_id=1, source_target_pairs={{0,1},{1,2},{2,3},{3,4},{4,5},{5,6},{6,7},{7,8},{8,9},{9,10},{10,1... | collective-permute-start | bytes 1572872 | tf_op jit(solution)/shard_map/ppermute | solution.py:379
  89.8 0.7 broadcast_in_dim.8
  90.5 3.7 %all-to-all-start.2 = ((f32[32,16,128]{2,1,0:T(8,128)}), f32[32,16,128]{2,1,0:T(8,128)S(1)}, u32[]{:S(2)}, u32[]{:S(2)}) async-start(f32[32,16,128]{2,1,0:T(8,128)} %broadcast_in_dim.8), calls=%async_computation.2 | async-start | bytes 524288 | tf_op jit(solution)/shard_map/all_to_all | solution.py:290
  94.2 5.1 %collective-permute-start.6 = (f32[2,128,128]{2,1,0:T(8,128)}, f32[2,128,128]{2,1,0:T(8,128)S(1)}, u32[]{:S(2)}, u32[]{:S(2)}) collective-permute-start(f32[2,128,128]{2,1,0:T(8,128)} %get-tuple-element.34), channel_id=1, source_target_pairs={{0,65},{1,66},{2,67},{3,68},{4,69},{5,70},{6,71},{7,72},{8,73},{9,... | collective-permute-start | bytes 393224 | tf_op jit(solution)/shard_map/ppermute | solution.py:380
  99.3 2.2 %collective-permute-done.6.corner = f32[2,128,128]{2,1,0:T(8,128)S(1)} collective-permute-done((f32[2,128,128]{2,1,0:T(8,128)}, f32[2,128,128]{2,1,0:T(8,128)S(1)}, u32[]{:S(2)}, u32[]{:S(2)}) %collective-permute-start.6) | collective-permute-done | bytes 131104 | tf_op jit(solution)/shard_map/ppermute | solution.py:380
  101.5 1.9 %all-to-all-done.2 = f32[32,16,128]{2,1,0:T(8,128)S(1)} async-done(((f32[32,16,128]{2,1,0:T(8,128)}), f32[32,16,128]{2,1,0:T(8,128)S(1)}, u32[]{:S(2)}, u32[]{:S(2)}) %all-to-all-start.2) | async-done | bytes 262176 | tf_op jit(solution)/shard_map/all_to_all | solution.py:290
  103.4 0.0 collective-permute-done.5.left
  103.4 2.2 %seams.1 = (f32[2,512,512]{2,1,0:T(8,128)}, f32[2,16,16,128]{3,2,1,0:T(8,128)}) custom-call(f32[2,512,512]{2,1,0:T(8,128)} %get-tuple-element.26.grad_in, f32[2,128,512]{2,1,0:T(8,128)S(1)} %collective-permute-done.4.above, f32[2,512,128]{2,1,0:T(8,128)S(1)} %collective-permute-done.5.left, ...), custom_call_target="tpu_custom_call", output_to_operand_aliasing={{0}: (0, {})} | custom-call | tf_op jit(solution)/shard_map/seams/pallas_call | solution.py:384
  (3 shorter events, 0.0 us)
Async XLA Ops:
  2.9 21.5 %collective-permute-start = (f32[2,512,128]{2,1,0:T(8,128)}, f32[2,512,128]{2,1,0:T(8,128)S(1)}, u32[]{:S(2)}, u32[]{:S(2)}) collective-permute-start(f32[2,512,128]{2,1,0:T(8,128)} %get-tuple-element.20), channel_id=1, source_target_pairs={{1,0},{2,1},{3,2},{4,3},{5,4},{6,5},{7,6},{8,7},{9,8},{10,9},{11,1... | collective-permute-start | bytes 1572872 | tf_op jit(solution)/shard_map/ppermute | solution.py:330
  8.0 32.9 %collective-permute-start.2 = (f32[2,128,128]{2,1,0:T(8,128)}, f32[2,128,128]{2,1,0:T(8,128)S(1)}, u32[]{:S(2)}, u32[]{:S(2)}) collective-permute-start(f32[2,128,128]{2,1,0:T(8,128)} %get-tuple-element.22), channel_id=1, source_target_pairs={{65,0},{66,1},{67,2},{68,3},{69,4},{70,5},{71,6},{72,7},{73,8},{74... | collective-permute-start | bytes 393224 | tf_op jit(solution)/shard_map/ppermute | solution.py:331
  9.3 31.6 %collective-permute-start.1 = (f32[2,128,512]{2,1,0:T(8,128)}, f32[2,128,512]{2,1,0:T(8,128)}, u32[]{:S(2)}, u32[]{:S(2)}) collective-permute-start(f32[2,128,512]{2,1,0:T(8,128)} %get-tuple-element.21), channel_id=1, source_target_pairs={{64,0},{128,64},{192,128},{65,1},{129,65},{193,129},{66,2},{130,66... | collective-permute-start | bytes 1572872 | tf_op jit(solution)/shard_map/ppermute | solution.py:329
  24.3 0.8 copy-start
  40.9 0.7 copy-start.1
  49.6 35.3 %collective-permute-start.4 = (f32[2,128,512]{2,1,0:T(8,128)}, f32[2,128,512]{2,1,0:T(8,128)S(1)}, u32[]{:S(2)}, u32[]{:S(2)}) collective-permute-start(f32[2,128,512]{2,1,0:T(8,128)} %get-tuple-element.29), channel_id=1, source_target_pairs={{0,64},{64,128},{128,192},{1,65},{65,129},{129,193},{2,66},{66,130... | collective-permute-start | bytes 1572872 | tf_op jit(solution)/shard_map/ppermute | solution.py:373
  51.1 1.6 %collective-permute-start.3 = (f32[2,128,128]{2,1,0:T(8,128)}, f32[2,128,128]{2,1,0:T(8,128)S(1)}, u32[]{:S(2)}, u32[]{:S(2)}) collective-permute-start(f32[2,128,128]{2,1,0:T(8,128)} %get-tuple-element.28), channel_id=1, source_target_pairs={{0,1},{1,0},{2,3},{3,2},{4,5},{5,4},{6,7},{7,6},{8,9},{9,8},{10,11... | collective-permute-start | bytes 393224 | tf_op jit(solution)/shard_map/ppermute | solution.py:374
  84.9 18.5 %collective-permute-start.5 = (f32[2,512,128]{2,1,0:T(8,128)}, f32[2,512,128]{2,1,0:T(8,128)S(1)}, u32[]{:S(2)}, u32[]{:S(2)}) collective-permute-start(f32[2,512,128]{2,1,0:T(8,128)} %get-tuple-element.33), channel_id=1, source_target_pairs={{0,1},{1,2},{2,3},{3,4},{4,5},{5,6},{6,7},{7,8},{8,9},{9,10},{10,1... | collective-permute-start | bytes 1572872 | tf_op jit(solution)/shard_map/ppermute | solution.py:379
  90.5 12.9 %all-to-all-start.2 = ((f32[32,16,128]{2,1,0:T(8,128)}), f32[32,16,128]{2,1,0:T(8,128)S(1)}, u32[]{:S(2)}, u32[]{:S(2)}) async-start(f32[32,16,128]{2,1,0:T(8,128)} %broadcast_in_dim.8), calls=%async_computation.2 | async-start | bytes 524288 | tf_op jit(solution)/shard_map/all_to_all | solution.py:290
  94.2 7.3 %collective-permute-start.6 = (f32[2,128,128]{2,1,0:T(8,128)}, f32[2,128,128]{2,1,0:T(8,128)S(1)}, u32[]{:S(2)}, u32[]{:S(2)}) collective-permute-start(f32[2,128,128]{2,1,0:T(8,128)} %get-tuple-element.34), channel_id=1, source_target_pairs={{0,65},{1,66},{2,67},{3,68},{4,69},{5,70},{6,71},{7,72},{8,73},{9,... | collective-permute-start | bytes 393224 | tf_op jit(solution)/shard_map/ppermute | solution.py:380

commit v7 on v6

--- a/solution.py
+++ b/solution.py
@@ -18,7 +18,7 @@
 ROW = "z_hi"
 COL = ("x", "y", "z_lo", "core")
 BOTH = (ROW,) + COL
-PLANE = ("x", "y")
+PLANE = ("x", "y", "core")
 DEPTH = ("z_hi", "z_lo")
 
 
@@ -219,8 +219,8 @@
     wait_all(stores)
 
 
-def lower_kernel(scale, pos, count, core, own, right, below, corner, photons, probe_in, waves_in, own_in, right_in, sum_in,
-                 g_own, g_right, g_below, g_corner, kept, sent,
+def lower_kernel(scale, pos, count, own, right, below, corner, photons, probe_in, waves_in, own_in, right_in, sum_in,
+                 g_own, g_right, g_below, g_corner, probe_out,
                  field, grad, photon_buf, probe, waves, plus_ref, minus_ref, probe_sum, listed, sems, photon_sems):
     rows, cols = own.shape[1], own.shape[2]
     tiles = cols // PATCH
@@ -248,7 +248,7 @@
               plus_ref, minus_ref)
     probe_sum[...] = probe_sum[...] * scale
     stores = copies_of(
-        [(probe_sum.at[core[0]], kept), (probe_sum.at[1 - core[0]], sent)]
+        [(probe_sum, probe_out)]
         + [(grad.at[t, :, lower, :], a) for t, a in enumerate(by_tiles(g_below, tiles) + [g_corner])]
         + [(grad.at[t, :, upper, :], a) for t, a in enumerate(last_rows(g_own) + [g_right.at[:, last, :]])],
         sems,
@@ -265,7 +265,7 @@
     left_rim = grad.at[:, pl.ds(PATCH, rest), pl.ds(0, PATCH)]
     loads = copies_of(
         [(top_rim, top_buf), (left_rim, left_buf), (above, above_buf), (left, beside_buf), (corner, corner_buf),
-         (parts.at[:, 0], probe_buf.at[0]), (parts.at[:, 1], probe_buf.at[1])],
+         (parts, probe_buf)],
         sems,
     )
     start_all(loads)
@@ -307,7 +307,6 @@
         (a * n_col + b, (a + 1) * n_col + b + 1) for a in range(n_row - 1) for b in range(n_col - 1)
     ]
     diagonal_back = [(j, i) for i, j in diagonal]
-    core = lax.axis_index("core")[None]
     smem = pl.BlockSpec(memory_space=pltpu.SMEM)
     hbm = pl.BlockSpec(memory_space=pl.ANY)
     params = pltpu.CompilerParams(vmem_limit_bytes=VMEM_LIMIT)
@@ -353,37 +352,34 @@
         out_specs=(hbm,) * 3,
         scratch_shapes=scratch(rows),
         compiler_params=params,
-        cost_estimate=pl.CostEstimate(flops=24 * 10**9, bytes_accessed=8 * 2**20, transcendentals=0),
+        cost_estimate=pl.CostEstimate(flops=10**9, bytes_accessed=2**20, transcendentals=0),
         name="upper_slots",
     )(pos, count, object_field, right, photon_rows, probe_modes, waves)
-    g_own, g_right, g_below, g_corner, kept, sent = pl.pallas_call(
+    g_own, g_right, g_below, g_corner, probe_2 = pl.pallas_call(
         functools.partial(lower_kernel, scale),
-        out_shape=(own_shape, right_shape, shape(2, PATCH, cols), rim_shape, rim_shape, rim_shape),
-        in_specs=[smem] * 3 + [hbm] * 10,
-        out_specs=(hbm,) * 6,
+        out_shape=(own_shape, right_shape, shape(2, PATCH, cols), rim_shape, probe_shape),
+        in_specs=[smem] * 2 + [hbm] * 10,
+        out_specs=(hbm,) * 5,
         scratch_shapes=scratch(2 * PATCH),
-        input_output_aliases={10: 0, 11: 1},
+        input_output_aliases={9: 0, 10: 1},
         compiler_params=params,
-        cost_estimate=pl.CostEstimate(flops=8 * 10**9, bytes_accessed=4 * 2**20, transcendentals=0),
+        cost_estimate=pl.CostEstimate(flops=10**9, bytes_accessed=2**20, transcendentals=0),
         name="lower_slots",
-    )(pos, count, core, object_field, right, below, corner, photon_rows, probe_modes, waves, g_own, g_right, probe_1)
+    )(pos, count, object_field, right, below, corner, photon_rows, probe_modes, waves, g_own, g_right, probe_1)
 
     plane, depth = lax.axis_size(PLANE), lax.axis_size(DEPTH)
-    swap = [(0, 1), (1, 0)]
     above = lax.ppermute(g_below, ROW, down)
-    value = kept + lax.ppermute(sent, "core", swap)
-    shares = lax.all_to_all(value.reshape(plane, -1, PATCH), PLANE, 0, 0, tiled=True)
+    left = lax.ppermute(g_right, COL, along)
+    from_corner = lax.ppermute(g_corner, BOTH, diagonal)
+    shares = lax.all_to_all(probe_2.reshape(plane, -1, PATCH), PLANE, 0, 0, tiled=True)
     share = jnp.sum(shares, axis=0)
     share = jnp.sum(everyone(share, DEPTH, depth), axis=0)
-    share, above, g_right, g_corner = lax.optimization_barrier((share, above, g_right, g_corner))
-    left = lax.ppermute(g_right, COL, along)
-    from_corner = lax.ppermute(g_corner, BOTH, diagonal)
-    parts = everyone(share, PLANE + ("core",), 2 * plane)
-    parts = parts.reshape(plane, 2, *share.shape)
+    share, above, left, from_corner = lax.optimization_barrier((share, above, left, from_corner))
+    parts = everyone(share, PLANE, plane)
 
     object_gradient, probe_gradient = pl.pallas_call(
         seam_kernel,
-        out_shape=(own_shape, shape(2, plane, *share.shape)),
+        out_shape=(own_shape, shape(*parts.shape)),
         in_specs=[hbm] * 5,
         out_specs=(hbm, hbm),
         scratch_shapes=[
@@ -392,8 +388,8 @@
             pltpu.VMEM((2, PATCH, cols), F32),
             pltpu.VMEM((2, rows, PATCH), F32),
             pltpu.VMEM((2, PATCH, PATCH), F32),
-            pltpu.VMEM((2, plane) + share.shape, F32),
-            pltpu.SemaphoreType.DMA((7,)),
+            pltpu.VMEM(parts.shape, F32),
+            pltpu.SemaphoreType.DMA((6,)),
         ],
         input_output_aliases={0: 0},
         compiler_params=pltpu.CompilerParams(vmem_limit_bytes=8 * 2**20),

time: 107 us -> 110 us (1.028); the launches traced: 106 us -> 110 us
  Pallas kernels: 28.2 us -> 17.3 us
  waiting for transfers between devices: 18.8 us -> 28.8 us
  starting transfers between devices: 22.9 us -> 32 us
  blocking collectives: 31.2 us -> 29.1 us
    all_to_all x1 -> x0, blocking collectives: 17.3 us -> none  [body(): lax.all_to_all(value.reshape(plane, -1, PATCH), PLANE, 0, 0, tiled=True)]
    all_to_all x1 -> x2, blocking collectives: 13.8 us -> 29.1 us  [everyone(): return lax.all_to_all(sent, axes, 0, 0, tiled=True)]
    ppermute x1, waiting for transfers between devices: 0.01 us -> 14.9 us  [body(): corner = lax.ppermute(corner, BOTH, diagonal_back)]
    pallas_call x1, Pallas kernels: 15.7 us -> 7.22 us  [body(): pl.pallas_call(upper_kernel, out_shape=(own_shape, right_shape, probe_sha...]
    all_to_all x1, starting transfers between devices: 3.7 us -> 9.84 us  [body(): lax.all_to_all(probe_2.reshape(plane, -1, PATCH), PLANE, 0, 0, tiled=True)]
    ppermute x1, starting transfers between devices: 1.52 us -> 7.12 us  [body(): above = lax.ppermute(g_below, ROW, down)]
    ppermute x1, waiting for transfers between devices: 13.1 us -> 10.1 us  [body(): right = lax.ppermute(right, COL, back)]
    ppermute x1, starting transfers between devices: 4.83 us -> 2.11 us  [body(): left = lax.ppermute(g_right, COL, along)]
  transfers between devices with their start and end apart: 8 -> 7, of which waited for: 4 -> 3; matrix products, arithmetic and copies ran while one was open for 2% -> 0% of each run, Pallas kernels for 15% -> 7%
where the time goes in v7:
time: 110 us
  starting transfers between devices  32 us (29%)
  blocking collectives  29.1 us (26%)
  waiting for transfers between devices  28.8 us (26%)
  Pallas kernels  17.3 us (16%)
  local copies, waits for them, and re-layouts  1.49 us (1%)
  between operations  1.41 us (1%)
    all_to_all x2, blocking collectives, everyone(): return lax.all_to_all(sent, axes, 0, 0, tiled=True)  29.1 us
    ppermute x1, waiting for transfers between devices, body(): corner = lax.ppermute(corner, BOTH, diagonal_back)  14.9 us
    ppermute x1, waiting for transfers between devices, body(): right = lax.ppermute(right, COL, back)  10.1 us
    all_to_all x1, starting transfers between devices, body(): lax.all_to_all(probe_2.reshape(plane, -1, PATCH), PLANE, 0, 0, tiled=True)  9.84 us
    pallas_call x1, Pallas kernels, body(): pl.pallas_call(upper_kernel, out_shape=(own_shape, right_shape, probe_sha...  7.22 us
    ppermute x1, starting transfers between devices, body(): above = lax.ppermute(g_below, ROW, down)  7.12 us
    pallas_call x1, Pallas kernels, body(): pl.pallas_call(functools.partial(lower_kernel, scale), out_shape=(own_sha...  5.62 us
    ppermute x1, starting transfers between devices, body(): from_corner = lax.ppermute(g_corner, BOTH, diagonal)  5.17 us
  transfers between devices with their start and end apart: 7, of which 3 were waited for; matrix products, arithmetic and copies ran while one was open for 0% of the time, Pallas kernels for 7%

profile of v7, /device:TPU:1, one launch (start us, length us, event | category | flops | bytes accessed | tf_op | source)
XLA Modules:
  0.0 110.1 jit_solution(1533676756101360711)
XLA Ops:
  0.6 2.2 %rims.1 = (f32[2,128,512]{2,1,0:T(8,128)}, f32[2,512,128]{2,1,0:T(8,128)}, f32[2,128,128]{2,1,0:T(8,128)}) custom-call(f32[2,512,512]{2,1,0:T(8,128)} %own.5), custom_call_target="tpu_custom_call" | custom-call | tf_op jit(solution)/shard_map/rims/pallas_call | solution.py:315
  2.9 5.1 %collective-permute-start = (f32[2,512,128]{2,1,0:T(8,128)}, f32[2,512,128]{2,1,0:T(8,128)S(1)}, u32[]{:S(2)}, u32[]{:S(2)}) collective-permute-start(f32[2,512,128]{2,1,0:T(8,128)} %get-tuple-element.19), channel_id=1, source_target_pairs={{1,0},{2,1},{3,2},{4,3},{5,4},{6,5},{7,6},{8,7},{9,8},{10,9},{11,1... | collective-permute-start | bytes 1572872 | tf_op jit(solution)/shard_map/ppermute | solution.py:329
  8.0 1.3 %collective-permute-start.1 = (f32[2,128,512]{2,1,0:T(8,128)}, f32[2,128,512]{2,1,0:T(8,128)}, u32[]{:S(2)}, u32[]{:S(2)}) collective-permute-start(f32[2,128,512]{2,1,0:T(8,128)} %get-tuple-element.20), channel_id=1, source_target_pairs={{64,0},{128,64},{192,128},{65,1},{129,65},{193,129},{66,2},{130,66... | collective-permute-start | bytes 1572872 | tf_op jit(solution)/shard_map/ppermute | solution.py:328
  9.3 1.3 %collective-permute-start.2 = (f32[2,128,128]{2,1,0:T(8,128)}, f32[2,128,128]{2,1,0:T(8,128)S(1)}, u32[]{:S(2)}, u32[]{:S(2)}) collective-permute-start(f32[2,128,128]{2,1,0:T(8,128)} %get-tuple-element.21), channel_id=1, source_target_pairs={{65,0},{66,1},{67,2},{68,3},{69,4},{70,5},{71,6},{72,7},{73,8},{74... | collective-permute-start | bytes 393224 | tf_op jit(solution)/shard_map/ppermute | solution.py:330
  11.3 10.1 %collective-permute-done.right = f32[2,512,128]{2,1,0:T(8,128)S(1)} collective-permute-done((f32[2,512,128]{2,1,0:T(8,128)}, f32[2,512,128]{2,1,0:T(8,128)S(1)}, u32[]{:S(2)}, u32[]{:S(2)}) %collective-permute-start) | collective-permute-done | bytes 524320 | tf_op jit(solution)/shard_map/ppermute | solution.py:329
  21.3 0.0 copy-start
  21.3 0.8 copy-done
  22.1 7.2 %upper_slots.1 = (f32[2,512,512]{2,1,0:T(8,128)}, f32[2,512,128]{2,1,0:T(8,128)}, f32[2,2,128,128]{3,2,1,0:T(8,128)}) custom-call(s32[2,64]{1,0:T(2,128)} %bitcast.12, s32[1]{0:T(128)} %bitcast.7.count, f32[2,512,512]{2,1,0:T(8,128)} %own.5, f32[2,512,128]{2,1,0:T(8,128)} %copy-done, bf16[64,128,128]{2,1,0:T(8,128)(2,1)} %bitcast.9, ...), custom_call_target="tpu_custom_call" | custom-call | flops 1000000000 | bytes 1048576 | tf_op jit(solution)/shard_map/upper_slots/pallas_call | solution.py:348
  29.4 14.9 %collective-permute-done.2.corner = f32[2,128,128]{2,1,0:T(8,128)S(1)} collective-permute-done((f32[2,128,128]{2,1,0:T(8,128)}, f32[2,128,128]{2,1,0:T(8,128)S(1)}, u32[]{:S(2)}, u32[]{:S(2)}) %collective-permute-start.2) | collective-permute-done | bytes 131104 | tf_op jit(solution)/shard_map/ppermute | solution.py:330
  44.3 0.0 copy-start.1
  44.3 0.0 collective-permute-done.1.below
  44.3 0.7 copy-done.1
  44.9 5.6 %lower_slots.1 = (f32[2,512,512]{2,1,0:T(8,128)}, f32[2,512,128]{2,1,0:T(8,128)}, f32[2,128,512]{2,1,0:T(8,128)}, f32[2,128,128]{2,1,0:T(8,128)}, f32[2,2,128,128]{3,2,1,0:T(8,128)}) custom-call(s32[2,64]{1,0:T(2,128)} %bitcast.13, s32[1]{0:T(128)} %bitcast.8.count, f32[2,512,512]{2,1,0:T(8,128)} %own.5, ...), custom_call_target="tpu_custom_call", output_to_operand_aliasing={{0}: (9, {}), {1}: (10, {})} | custom-call | flops 1000000000 | bytes 1048576 | tf_op jit(solution)/shard_map/lower_slots/pallas_call | solution.py:358
  50.5 7.1 %collective-permute-start.3 = (f32[2,128,512]{2,1,0:T(8,128)}, f32[2,128,512]{2,1,0:T(8,128)S(1)}, u32[]{:S(2)}, u32[]{:S(2)}) collective-permute-start(f32[2,128,512]{2,1,0:T(8,128)} %get-tuple-element.27), channel_id=1, source_target_pairs={{0,64},{64,128},{128,192},{1,65},{65,129},{129,193},{2,66},{66,130... | collective-permute-start | bytes 1572872 | tf_op jit(solution)/shard_map/ppermute | solution.py:371
  57.7 2.1 %collective-permute-start.4 = (f32[2,512,128]{2,1,0:T(8,128)}, f32[2,512,128]{2,1,0:T(8,128)S(1)}, u32[]{:S(2)}, u32[]{:S(2)}) collective-permute-start(f32[2,512,128]{2,1,0:T(8,128)} %get-tuple-element.28), channel_id=1, source_target_pairs={{0,1},{1,2},{2,3},{3,4},{4,5},{5,6},{6,7},{7,8},{8,9},{9,10},{10,1... | collective-permute-start | bytes 1572872 | tf_op jit(solution)/shard_map/ppermute | solution.py:372
  59.8 9.8 %all-to-all-start = ((f32[32,16,128]{2,1,0:T(8,128)}), f32[32,16,128]{2,1,0:T(8,128)S(1)}, u32[]{:S(2)}, u32[]{:S(2)}) async-start(f32[32,16,128]{2,1,0:T(8,128)} %bitcast.11), calls=%async_computation | async-start | bytes 524288 | tf_op jit(solution)/shard_map/all_to_all | solution.py:374
  69.6 5.2 %collective-permute-start.5 = (f32[2,128,128]{2,1,0:T(8,128)}, f32[2,128,128]{2,1,0:T(8,128)S(1)}, u32[]{:S(2)}, u32[]{:S(2)}) collective-permute-start(f32[2,128,128]{2,1,0:T(8,128)} %get-tuple-element.29), channel_id=1, source_target_pairs={{0,65},{1,66},{2,67},{3,68},{4,69},{5,70},{6,71},{7,72},{8,73},{9,... | collective-permute-start | bytes 393224 | tf_op jit(solution)/shard_map/ppermute | solution.py:373
  74.8 3.8 %all-to-all-done = f32[32,16,128]{2,1,0:T(8,128)S(1)} async-done(((f32[32,16,128]{2,1,0:T(8,128)}), f32[32,16,128]{2,1,0:T(8,128)S(1)}, u32[]{:S(2)}, u32[]{:S(2)}) %all-to-all-start) | async-done | bytes 262176 | tf_op jit(solution)/shard_map/all_to_all | solution.py:374
  78.7 11.5 %all_to_all.15 = f32[8,16,128]{2,1,0:T(8,128)S(1)} all-to-all(f32[8,16,128]{2,1,0:T(8,128)S(1)} %broadcast_in_dim.4), channel_id=1, replica_groups=mesh['z_hi'=4,'x'=4,'y'=4,'z_lo'=2,'core'=2] {'z_hi','z_lo'}, dimensions={0} | all-to-all | bytes 131072 | tf_op jit(solution)/shard_map/all_to_all | solution.py:290
  90.2 0.0 collective-permute-done.5.corner
  90.3 0.0 collective-permute-done.3.above
  90.3 0.0 collective-permute-done.4.left
  90.3 17.6 %all_to_all.16.parts = f32[32,16,128]{2,1,0:T(8,128)S(1)} all-to-all(f32[32,16,128]{2,1,0:T(8,128)S(1)} %broadcast_in_dim.5), channel_id=1, replica_groups=mesh['z_hi'=4,'x'=4,'y'=4,'z_lo'=2,'core'=2] {'x','y','core'}, dimensions={0} | all-to-all | bytes 524288 | tf_op jit(solution)/shard_map/all_to_all | solution.py:290
  107.9 2.2 %seams.1 = (f32[2,512,512]{2,1,0:T(8,128)}, f32[32,16,128]{2,1,0:T(8,128)}) custom-call(f32[2,512,512]{2,1,0:T(8,128)} %get-tuple-element.25.grad_in, f32[2,128,512]{2,1,0:T(8,128)S(1)} %collective-permute-done.3.above, f32[2,512,128]{2,1,0:T(8,128)S(1)} %collective-permute-done.4.left, ...), custom_call_target="tpu_custom_call", output_to_operand_aliasing={{0}: (0, {})} | custom-call | tf_op jit(solution)/shard_map/seams/pallas_call | solution.py:380
  (4 shorter events, 0.1 us)
Async XLA Ops:
  2.9 18.5 %collective-permute-start = (f32[2,512,128]{2,1,0:T(8,128)}, f32[2,512,128]{2,1,0:T(8,128)S(1)}, u32[]{:S(2)}, u32[]{:S(2)}) collective-permute-start(f32[2,512,128]{2,1,0:T(8,128)} %get-tuple-element.19), channel_id=1, source_target_pairs={{1,0},{2,1},{3,2},{4,3},{5,4},{6,5},{7,6},{8,7},{9,8},{10,9},{11,1... | collective-permute-start | bytes 1572872 | tf_op jit(solution)/shard_map/ppermute | solution.py:329
  8.0 36.2 %collective-permute-start.1 = (f32[2,128,512]{2,1,0:T(8,128)}, f32[2,128,512]{2,1,0:T(8,128)}, u32[]{:S(2)}, u32[]{:S(2)}) collective-permute-start(f32[2,128,512]{2,1,0:T(8,128)} %get-tuple-element.20), channel_id=1, source_target_pairs={{64,0},{128,64},{192,128},{65,1},{129,65},{193,129},{66,2},{130,66... | collective-permute-start | bytes 1572872 | tf_op jit(solution)/shard_map/ppermute | solution.py:328
  9.3 34.9 %collective-permute-start.2 = (f32[2,128,128]{2,1,0:T(8,128)}, f32[2,128,128]{2,1,0:T(8,128)S(1)}, u32[]{:S(2)}, u32[]{:S(2)}) collective-permute-start(f32[2,128,128]{2,1,0:T(8,128)} %get-tuple-element.21), channel_id=1, source_target_pairs={{65,0},{66,1},{67,2},{68,3},{69,4},{70,5},{71,6},{72,7},{73,8},{74... | collective-permute-start | bytes 393224 | tf_op jit(solution)/shard_map/ppermute | solution.py:330
  21.3 0.8 copy-start
  44.3 0.7 copy-start.1
  50.5 39.7 %collective-permute-start.3 = (f32[2,128,512]{2,1,0:T(8,128)}, f32[2,128,512]{2,1,0:T(8,128)S(1)}, u32[]{:S(2)}, u32[]{:S(2)}) collective-permute-start(f32[2,128,512]{2,1,0:T(8,128)} %get-tuple-element.27), channel_id=1, source_target_pairs={{0,64},{64,128},{128,192},{1,65},{65,129},{129,193},{2,66},{66,130... | collective-permute-start | bytes 1572872 | tf_op jit(solution)/shard_map/ppermute | solution.py:371
  57.7 32.6 %collective-permute-start.4 = (f32[2,512,128]{2,1,0:T(8,128)}, f32[2,512,128]{2,1,0:T(8,128)S(1)}, u32[]{:S(2)}, u32[]{:S(2)}) collective-permute-start(f32[2,512,128]{2,1,0:T(8,128)} %get-tuple-element.28), channel_id=1, source_target_pairs={{0,1},{1,2},{2,3},{3,4},{4,5},{5,6},{6,7},{7,8},{8,9},{9,10},{10,1... | collective-permute-start | bytes 1572872 | tf_op jit(solution)/shard_map/ppermute | solution.py:372
  59.8 18.8 %all-to-all-start = ((f32[32,16,128]{2,1,0:T(8,128)}), f32[32,16,128]{2,1,0:T(8,128)S(1)}, u32[]{:S(2)}, u32[]{:S(2)}) async-start(f32[32,16,128]{2,1,0:T(8,128)} %bitcast.11), calls=%async_computation | async-start | bytes 524288 | tf_op jit(solution)/shard_map/all_to_all | solution.py:374
  69.6 20.6 %collective-permute-start.5 = (f32[2,128,128]{2,1,0:T(8,128)}, f32[2,128,128]{2,1,0:T(8,128)S(1)}, u32[]{:S(2)}, u32[]{:S(2)}) collective-permute-start(f32[2,128,128]{2,1,0:T(8,128)} %get-tuple-element.29), channel_id=1, source_target_pairs={{0,65},{1,66},{2,67},{3,68},{4,69},{5,70},{6,71},{7,72},{8,73},{9,... | collective-permute-start | bytes 393224 | tf_op jit(solution)/shard_map/ppermute | solution.py:373
